TPU v7x, 32 devices: a whole 2x2x4 slice. The times are simulated.
32 devices in a mesh: dp: 16 (over z, y, x), tensor: 2 (over core).
Axes of the slice: x: 2, y: 2, z: 4, core: 2. Of those that a mesh axis runs over, the one named last changes fastest.
Arguments:
- tokens: bfloat16 [4096, 2048], P('dp'), may hold values from -6 to 6
- out_grad: bfloat16 [4096, 2048], P('dp'), may hold values from -6 to 6
- segments: int32 [1, 4096], replicated, may hold values from 0 to 7, never falling along the last dimension, each value on 1 to 3072 neighbouring positions
- routes: int32 [4096, 6], P('dp'), may hold values from 0 to 15, as said below
- attn_gain: bfloat16 [2048], P('dp'), may hold values from 0.5 to 1.5
- w_query: bfloat16 [2048, 3072], P('dp', 'tensor'), may hold values from -0.125 to 0.125
- w_latent: bfloat16 [2048, 576], P('dp'), may hold values from -0.125 to 0.125
- latent_gain: bfloat16 [512], P('dp'), may hold values from 0.5 to 1.5
- w_keyval: bfloat16 [512, 4096], P('dp', 'tensor'), may hold values from -0.25 to 0.25
- w_out: bfloat16 [2048, 2048], P('tensor', 'dp'), may hold values from -2 to 2
- moe_gain: bfloat16 [2048], P('dp'), may hold values from 0.5 to 1.5
- w_router: bfloat16 [2048, 16], P('dp'), may hold values from -0.0625 to 0.0625
- shared_gate: bfloat16 [2048, 2816], P('dp', 'tensor'), may hold values from -0.125 to 0.125
- shared_up: bfloat16 [2048, 2816], P('dp', 'tensor'), may hold values from -0.125 to 0.125
- shared_down: bfloat16 [2816, 2048], P('tensor', 'dp'), may hold values from -0.109375 to 0.109375
- expert_gate: bfloat16 [16, 2048, 1408], P('dp', None, 'tensor'), may hold values from -0.125 to 0.125
- routed_up_weight: bfloat16 [16, 2048, 1408], P('dp', None, 'tensor'), may hold values from -0.125 to 0.125
- expert_down: bfloat16 [16, 1408, 2048], P('dp', 'tensor'), may hold values from -1.5 to 1.5
Outputs:
- result: bfloat16 [4096, 2048], P('dp')
- token_input_gradient: float32 [4096, 2048], P('dp')
- grad_attn_gain: float32 [2048], P('dp')
- grad_w_query: float32 [2048, 3072], P('dp', 'tensor')
- grad_w_latent: float32 [2048, 576], P('dp')
- grad_latent_gain: float32 [512], P('dp')
- grad_w_keyval: float32 [512, 4096], P('dp', 'tensor')
- grad_w_out: float32 [2048, 2048], P('tensor', 'dp')
- grad_moe_gain: float32 [2048], P('dp')
- grad_w_router: float32 [2048, 16], P('dp')
- grad_shared_gate: float32 [2048, 2816], P('dp', 'tensor')
- grad_shared_up: float32 [2048, 2816], P('dp', 'tensor')
- grad_shared_down: float32 [2816, 2048], P('tensor', 'dp')
- grad_expert_gate: float32 [16, 2048, 1408], P('dp', None, 'tensor')
- grad_expert_up: float32 [16, 2048, 1408], P('dp', None, 'tensor')
- grad_expert_down: float32 [16, 1408, 2048], P('dp', 'tensor')
Inputs may be any that keep to these rules, and one draw needn't show every extreme that they name: `routes`: each row names 6 different experts. Among the rows of one index of dp (aligned blocks of 256 rows) no expert is named more than 128 times, and in every draw one expert is named exactly 128 times by the rows of every block. `segments`: along each sequence the numbers never fall; a document has at most 3072 tokens and some document has exactly that many.
All inputs are finite; a program needn't handle non-finite values.
Results may differ from a plain program's by a relative error of at most 0.025.
Values may be sent and summed in bfloat16 or wider, within the bound.
A program may use at most 320 MiB of HBM per device.

v0:
```python
import math

import jax
import jax.numpy as jnp
from jax import lax
from jax.sharding import PartitionSpec as P

NOPE = 128
ROPE = 64
VDIM = 128
RANK = 512
TOPK = 6
WINDOW = 1024


eps_norm = 1e-06
highest = lax.Precision.HIGHEST


def passed_along(value, axis, steps):
    count = lax.axis_size(axis)
    leading, last = (max(0, -steps), min(count, count - steps))
    return lax.ppermute(value, axis, [(source, source + steps) for source in range(leading, last)])


def rms_scale(values, gain_vec):
    inv_root = lax.rsqrt(jnp.mean(values * values, axis=-1, keepdims=True) + eps_norm)
    return values * inv_root * gain_vec


def rope_tables(positions):
    half_width = ROPE // 2
    frequency = jnp.exp(
        -jnp.arange(half_width, dtype=jnp.float32) * (2.0 * math.log(10000.0) / ROPE)
    )
    angles = positions[:, None] * frequency[None, :]
    return (jnp.cos(angles), jnp.sin(angles))


def rotate(values, cos_tab, sin_tab):
    half_width = values.shape[-1] // 2
    first_half = values[..., :half_width]
    second = values[..., half_width:]
    return jnp.concatenate(
        [first_half * cos_tab - second * sin_tab, second * cos_tab + first_half * sin_tab], axis=-1
    )


def gated_act(gate_a, up_b):
    return jax.nn.silu(gate_a) * up_b


def matmul(left_mat, right_mat):
    return jnp.dot(left_mat, right_mat, preferred_element_type=jnp.float32)


def matmul_nt(left_mat, right_mat):
    return lax.dot_general(
        left_mat, right_mat, (((1,), (1,)), ((), ())), preferred_element_type=jnp.float32
    )


def matmul_tn(left_mat, right_mat):
    return lax.dot_general(
        left_mat, right_mat, (((0,), (0,)), ((), ())), preferred_element_type=jnp.float32
    )


def shards(
    tokens,
    out_grad,
    segments,
    routes,
    attn_gain,
    w_query,
    w_latent,
    latent_gain,
    w_keyval,
    w_out,
    moe_gain,
    w_router,
    shared_gate,
    shared_up,
    shared_down,
    expert_gate,
    routed_up_weight,
    expert_down,
):
    n_rows = tokens.shape[0]
    model_width = tokens.shape[1]
    dp_count = lax.axis_size("dp")
    dp_index = lax.axis_index("dp")
    seq_len = segments.shape[1]
    seq_devs = seq_len // n_rows
    hop_count = (WINDOW - 1) // n_rows + 1
    n_keys = (hop_count + 1) * n_rows
    experts = w_router.shape[1]
    local_experts = expert_gate.shape[0]
    capacity = 4 * n_rows * TOPK // (3 * experts)
    slot_total = experts * capacity
    score_scale = (NOPE + ROPE) ** (-0.5)
    row_start = dp_index % seq_devs * n_rows
    seg_row = lax.dynamic_index_in_dim(segments, dp_index // seq_devs, 0, keepdims=False)
    gathered = (
        lax.all_gather(attn_gain, "dp", axis=0, tiled=True),
        lax.all_gather(w_query, "dp", axis=0, tiled=True),
        lax.all_gather(w_latent, "dp", axis=0, tiled=True),
        lax.all_gather(latent_gain, "dp", axis=0, tiled=True),
        lax.all_gather(w_keyval, "dp", axis=0, tiled=True),
        lax.all_gather(w_out, "dp", axis=1, tiled=True),
        lax.all_gather(moe_gain, "dp", axis=0, tiled=True),
        lax.all_gather(w_router, "dp", axis=0, tiled=True),
        lax.all_gather(shared_gate, "dp", axis=0, tiled=True),
        lax.all_gather(shared_up, "dp", axis=0, tiled=True),
        lax.all_gather(shared_down, "dp", axis=1, tiled=True),
    )
    (
        gain_attn,
        wq_full,
        wlat_full,
        gain_latent,
        wkv_full,
        wo_full,
        gain_moe,
        wr_full,
        sgate_full,
        sup_full,
        sdown_full,
    ) = gathered
    local_heads = wq_full.shape[1] // (NOPE + ROPE)
    positions = (row_start + jnp.arange(n_rows, dtype=jnp.int32)).astype(jnp.float32)
    cos_tab, sin_tab = rope_tables(positions)
    resid_in = tokens.astype(jnp.float32)
    normed, attn_norm_back = jax.vjp(rms_scale, resid_in, gain_attn.astype(jnp.float32))
    normed_low = normed.astype(jnp.bfloat16)

    def rope_queries(q_flat):
        shaped = q_flat.reshape(n_rows, local_heads, NOPE + ROPE)
        return jnp.concatenate(
            [shaped[..., :NOPE], rotate(shaped[..., NOPE:], cos_tab[:, None], sin_tab[:, None])], -1
        )

    queries, query_back = jax.vjp(rope_queries, matmul(normed_low, wq_full))
    query_low = queries.astype(jnp.bfloat16)

    def latent_piece(latent_raw, gain_vec):
        return (
            rms_scale(latent_raw[:, :RANK], gain_vec),
            rotate(latent_raw[:, RANK:], cos_tab, sin_tab),
        )

    (latent, key_rope), latent_back = jax.vjp(
        latent_piece, matmul(normed_low, wlat_full), gain_latent.astype(jnp.float32)
    )
    latent_low = latent.astype(jnp.bfloat16)
    rope_low = key_rope.astype(jnp.bfloat16)
    latent_parts = []
    rope_parts = []
    for distance in range(hop_count, 0, -1):
        moved_latent, moved_rope = passed_along((latent_low, rope_low), "dp", distance)
        latent_parts.append(moved_latent)
        rope_parts.append(moved_rope)
    keys_latent = jnp.concatenate(latent_parts + [latent_low], 0)
    keys_rope = jnp.concatenate(rope_parts + [rope_low], 0)
    keyval = (
        matmul(keys_latent, wkv_full).astype(jnp.bfloat16).reshape(n_keys, local_heads, NOPE + VDIM)
    )
    key_nope = keyval[..., :NOPE]
    values = keyval[..., NOPE:]
    key_pos = row_start - hop_count * n_rows + jnp.arange(n_keys, dtype=jnp.int32)
    query_pos = row_start + jnp.arange(n_rows, dtype=jnp.int32)
    padded_seg = jnp.concatenate([jnp.full((hop_count * n_rows,), -1, jnp.int32), seg_row])
    key_seg = lax.dynamic_slice_in_dim(padded_seg, row_start, n_keys, 0)
    query_seg = lax.dynamic_slice_in_dim(seg_row, row_start, n_rows, 0)
    allowed = (key_pos[None, :] >= 0) & (key_pos[None, :] <= query_pos[:, None])
    allowed = (
        allowed
        & (query_pos[:, None] - key_pos[None, :] < WINDOW)
        & (query_seg[:, None] == key_seg[None, :])
    )

    def masked_scores():
        nope_part = jnp.einsum(
            "qhd,khd->hqk", query_low[..., :NOPE], key_nope, preferred_element_type=jnp.float32
        )
        rope_part = jnp.einsum(
            "qhr,kr->hqk", query_low[..., NOPE:], keys_rope, preferred_element_type=jnp.float32
        )
        return jnp.where(allowed[None], score_scale * (nope_part + rope_part), -jnp.inf)

    scores = masked_scores()
    top_score = jnp.max(scores, axis=-1, keepdims=True)
    exp_scores = jnp.exp(scores - top_score)
    denom = jnp.sum(exp_scores, axis=-1, keepdims=True)
    attn_probs = exp_scores / denom
    log_total = top_score + jnp.log(denom)
    attended = jnp.einsum(
        "hqk,khv->qhv", attn_probs.astype(jnp.bfloat16), values, preferred_element_type=jnp.float32
    )
    attended_low = attended.astype(jnp.bfloat16).reshape(n_rows, local_heads * VDIM)
    attn_out = lax.psum(matmul(attended_low, wo_full).astype(jnp.bfloat16), "tensor").astype(
        jnp.float32
    )
    middle = resid_in + attn_out
    moe_normed, moe_norm_back = jax.vjp(rms_scale, middle, gain_moe.astype(jnp.float32))
    moe_low = moe_normed.astype(jnp.bfloat16)
    router, router_back = jax.vjp(
        lambda logit_vals: jax.nn.softmax(logit_vals, axis=-1), matmul(moe_low, wr_full)
    )
    expert_ids = jnp.arange(experts, dtype=jnp.int32)
    route_hot = (routes[:, :, None] == expert_ids[None, None, :]).astype(jnp.float32)
    gate_w = jnp.einsum("te,tke->tk", router, route_hot, precision=highest)
    flat_routes = routes.reshape(-1)
    assign_count = flat_routes.shape[0]
    flat_hot = (flat_routes[:, None] == expert_ids[None, :]).astype(jnp.int32)
    earlier = jnp.cumsum(flat_hot, axis=0) - flat_hot
    slot_in = jnp.sum(earlier * flat_hot, axis=1)
    target = flat_routes * capacity + slot_in
    assign_ids = jnp.arange(assign_count, dtype=jnp.int32)
    assign_of_slot = jnp.zeros((slot_total,), jnp.int32).at[target].set(assign_ids)
    slot_live = (
        jnp.zeros((slot_total,), jnp.bfloat16)
        .at[target]
        .set(jnp.ones((assign_count,), jnp.bfloat16))
    )
    send_rows = moe_low[assign_of_slot // TOPK] * slot_live[:, None]
    recv_rows = lax.all_to_all(
        send_rows.reshape(dp_count, local_experts * capacity, model_width),
        "dp",
        split_axis=0,
        concat_axis=0,
        tiled=True,
    )
    received_four_parts = recv_rows.reshape(dp_count, local_experts, capacity, model_width)
    exp_gate = jnp.einsum(
        "sjcd,jdf->sjcf", received_four_parts, expert_gate, preferred_element_type=jnp.float32
    )
    exp_up = jnp.einsum(
        "sjcd,jdf->sjcf", received_four_parts, routed_up_weight, preferred_element_type=jnp.float32
    )
    exp_act, exp_act_back = jax.vjp(gated_act, exp_gate, exp_up)
    exp_act_low = exp_act.astype(jnp.bfloat16)
    exp_result = jnp.einsum(
        "sjcf,jfd->sjcd", exp_act_low, expert_down, preferred_element_type=jnp.float32
    )
    returned = lax.all_to_all(
        exp_result.reshape(dp_count, local_experts * capacity, model_width).astype(jnp.bfloat16),
        "dp",
        split_axis=0,
        concat_axis=0,
        tiled=True,
    ).astype(jnp.float32)
    per_assign = returned.reshape(slot_total, model_width)[target].reshape(
        n_rows, TOPK, model_width
    )
    routed = jnp.einsum("tk,tkd->td", gate_w, per_assign, precision=highest)
    shared_a = matmul(moe_low, sgate_full)
    shared_b = matmul(moe_low, sup_full)
    shared_act, shared_back = jax.vjp(gated_act, shared_a, shared_b)
    shared_low = shared_act.astype(jnp.bfloat16)
    moe_out = lax.psum(
        (routed + matmul(shared_low, sdown_full)).astype(jnp.bfloat16), "tensor"
    ).astype(jnp.float32)
    result = (middle + moe_out).astype(jnp.bfloat16)
    grad_y = out_grad.astype(jnp.float32)
    grad_sdown = matmul_tn(shared_low, out_grad)
    d_shared_a, d_shared_b = shared_back(matmul_nt(out_grad, sdown_full))
    d_sa_low = d_shared_a.astype(jnp.bfloat16)
    d_sb_low = d_shared_b.astype(jnp.bfloat16)
    grad_sgate = matmul_tn(moe_low, d_sa_low)
    grad_sup = matmul_tn(moe_low, d_sb_low)
    d_moe = matmul_nt(d_sa_low, sgate_full) + matmul_nt(d_sb_low, sup_full)
    d_gate_part = jnp.einsum("td,tkd->tk", grad_y, per_assign, precision=highest)
    d_assign = (
        (gate_w[:, :, None] * grad_y[:, None, :])
        .astype(jnp.bfloat16)
        .reshape(assign_count, model_width)
    )
    send_grads = d_assign[assign_of_slot] * slot_live[:, None]
    recv_grads = lax.all_to_all(
        send_grads.reshape(dp_count, local_experts * capacity, model_width),
        "dp",
        split_axis=0,
        concat_axis=0,
        tiled=True,
    )
    recv_grads = recv_grads.reshape(dp_count, local_experts, capacity, model_width)
    expert_down_weight_gradient = jnp.einsum(
        "sjcf,sjcd->jfd", exp_act_low, recv_grads, preferred_element_type=jnp.float32
    )
    d_exp_act = jnp.einsum(
        "sjcd,jfd->sjcf", recv_grads, expert_down, preferred_element_type=jnp.float32
    )
    d_exp_gate, expert_up_act_gradient = exp_act_back(d_exp_act)
    d_egate_low = d_exp_gate.astype(jnp.bfloat16)
    expert_up_gradient_lowp = expert_up_act_gradient.astype(jnp.bfloat16)
    expert_gate_weight_gradient = jnp.einsum(
        "bmky,bmkx->myx", received_four_parts, d_egate_low, preferred_element_type=jnp.float32
    )
    expert_up_weight_gradient = jnp.einsum(
        "bmky,bmkx->myx",
        received_four_parts,
        expert_up_gradient_lowp,
        preferred_element_type=jnp.float32,
    )
    d_slots = jnp.einsum(
        "hteg,tmg->htem", d_egate_low, expert_gate, preferred_element_type=jnp.float32
    )
    d_slots = d_slots + jnp.einsum(
        "hteg,tmg->htem",
        expert_up_gradient_lowp,
        routed_up_weight,
        preferred_element_type=jnp.float32,
    )
    back_grads = lax.all_to_all(
        d_slots.reshape(dp_count, local_experts * capacity, model_width).astype(jnp.bfloat16),
        "dp",
        split_axis=0,
        concat_axis=0,
        tiled=True,
    ).astype(jnp.float32)
    d_moe = d_moe + jnp.sum(
        back_grads.reshape(slot_total, model_width)[target].reshape(n_rows, TOPK, model_width),
        axis=1,
    )
    d_moe, d_gate = (
        lax.psum(d_moe.astype(jnp.bfloat16), "tensor").astype(jnp.float32),
        lax.psum(d_gate_part.astype(jnp.bfloat16), "tensor").astype(jnp.float32),
    )
    d_router = jnp.einsum("tk,tke->te", d_gate, route_hot, precision=highest)
    (d_logits,) = router_back(d_router)
    d_logits_low = d_logits.astype(jnp.bfloat16)
    grad_router = matmul_tn(moe_low, d_logits_low)
    d_moe = d_moe + matmul_nt(d_logits_low, wr_full)
    d_mid_norm, grad_gain_moe = moe_norm_back(d_moe)
    d_middle = grad_y + d_mid_norm
    d_middle_low = d_middle.astype(jnp.bfloat16)
    grad_wout = matmul_tn(attended_low, d_middle_low)
    d_att_low = (
        matmul_nt(d_middle_low, wo_full).astype(jnp.bfloat16).reshape(n_rows, local_heads, VDIM)
    )
    again_probs = jnp.exp(masked_scores() - log_total)
    d_values = jnp.einsum(
        "hqk,qhv->khv",
        again_probs.astype(jnp.bfloat16),
        d_att_low,
        preferred_element_type=jnp.float32,
    )
    d_probs = jnp.einsum("qhv,khv->hqk", d_att_low, values, preferred_element_type=jnp.float32)
    d_scores = (
        again_probs * (d_probs - jnp.sum(d_probs * again_probs, axis=-1, keepdims=True))
    ).astype(jnp.bfloat16)
    d_query_nope = score_scale * jnp.einsum(
        "hqk,khd->qhd", d_scores, key_nope, preferred_element_type=jnp.float32
    )
    d_query_rope = score_scale * jnp.einsum(
        "hqk,kr->qhr", d_scores, keys_rope, preferred_element_type=jnp.float32
    )
    d_key_nope = score_scale * jnp.einsum(
        "hqk,qhd->khd", d_scores, query_low[..., :NOPE], preferred_element_type=jnp.float32
    )
    d_key_rope = score_scale * jnp.einsum(
        "hqk,qhr->kr", d_scores, query_low[..., NOPE:], preferred_element_type=jnp.float32
    )
    (d_q_raw,) = query_back(jnp.concatenate([d_query_nope, d_query_rope], -1))
    d_q_low = d_q_raw.astype(jnp.bfloat16)
    grad_wq = matmul_tn(normed_low, d_q_low)
    d_normed = matmul_nt(d_q_low, wq_full)
    d_kv_low = (
        jnp.concatenate([d_key_nope, d_values], -1)
        .astype(jnp.bfloat16)
        .reshape(n_keys, local_heads * (NOPE + VDIM))
    )
    grad_wkv = matmul_tn(keys_latent, d_kv_low)
    d_keys_latent = matmul_nt(d_kv_low, wkv_full)
    own_latent = d_keys_latent[hop_count * n_rows :]
    own_rope = d_key_rope[hop_count * n_rows :]
    for distance in range(hop_count, 0, -1):
        block_index = hop_count - distance
        lower = block_index * n_rows
        home_latent, home_rope = (
            passed_along(
                d_keys_latent[lower : lower + n_rows].astype(jnp.bfloat16), "dp", -distance
            ).astype(jnp.float32),
            passed_along(
                d_key_rope[lower : lower + n_rows].astype(jnp.bfloat16), "dp", -distance
            ).astype(jnp.float32),
        )
        own_latent = own_latent + home_latent
        own_rope = own_rope + home_rope
    d_normed, own_latent, own_rope = (
        lax.psum(d_normed.astype(jnp.bfloat16), "tensor").astype(jnp.float32),
        lax.psum(own_latent.astype(jnp.bfloat16), "tensor").astype(jnp.float32),
        lax.psum(own_rope.astype(jnp.bfloat16), "tensor").astype(jnp.float32),
    )
    d_latent_raw, grad_gain_latent = latent_back((own_latent, own_rope))
    d_latent_low = d_latent_raw.astype(jnp.bfloat16)
    grad_wlat = matmul_tn(normed_low, d_latent_low)
    d_normed = d_normed + matmul_nt(d_latent_low, wlat_full)
    d_tokens_norm, grad_gain_attn = attn_norm_back(d_normed)
    token_input_gradient = d_middle + d_tokens_norm
    reduced_result = tuple(
        (
            lax.psum_scatter(grad_gain_attn, "dp", scatter_dimension=0, tiled=True),
            lax.psum_scatter(grad_wq, "dp", scatter_dimension=0, tiled=True),
            lax.psum_scatter(grad_wlat, "dp", scatter_dimension=0, tiled=True),
            lax.psum_scatter(grad_gain_latent, "dp", scatter_dimension=0, tiled=True),
            lax.psum_scatter(grad_wkv, "dp", scatter_dimension=0, tiled=True),
            lax.psum_scatter(grad_wout, "dp", scatter_dimension=1, tiled=True),
            lax.psum_scatter(grad_gain_moe, "dp", scatter_dimension=0, tiled=True),
            lax.psum_scatter(grad_router, "dp", scatter_dimension=0, tiled=True),
            lax.psum_scatter(grad_sgate, "dp", scatter_dimension=0, tiled=True),
            lax.psum_scatter(grad_sup, "dp", scatter_dimension=0, tiled=True),
            lax.psum_scatter(grad_sdown, "dp", scatter_dimension=1, tiled=True),
        )
    )
    return (
        (result, token_input_gradient)
        + reduced_result
        + (expert_gate_weight_gradient, expert_up_weight_gradient, expert_down_weight_gradient)
    )


def solution(mesh):
    placed = (
        P("dp", None),
        P("dp", None),
        P(),
        P("dp", None),
        P("dp"),
        P("dp", "tensor"),
        P("dp", None),
        P("dp"),
        P("dp", "tensor"),
        P("tensor", "dp"),
        P("dp"),
        P("dp", None),
        P("dp", "tensor"),
        P("dp", "tensor"),
        P("tensor", "dp"),
        P("dp", None, "tensor"),
        P("dp", None, "tensor"),
        P("dp", "tensor", None),
    )
    return jax.shard_map(
        shards,
        mesh=mesh,
        in_specs=placed,
        out_specs=(
            P("dp", None),
            P("dp", None),
            P("dp"),
            P("dp", "tensor"),
            P("dp", None),
            P("dp"),
            P("dp", "tensor"),
            P("tensor", "dp"),
            P("dp"),
            P("dp", None),
            P("dp", "tensor"),
            P("dp", "tensor"),
            P("tensor", "dp"),
            P("dp", None, "tensor"),
            P("dp", None, "tensor"),
            P("dp", "tensor", None),
        ),
        check_vma=False,
    )
```

profile of v0, /device:TPU:0, one launch (start us, length us, event | category | flops | bytes accessed | tf_op | source)
XLA Modules:
  0.0 3099.4 jit_solution(4053046883331058101)
XLA Ops:
  14.9 42.5 %all-gather = bf16[16,1,128]{2,1,0:T(2,128)(2,1)S(1)} all-gather(bf16[1,1,128]{2,1,0:T(2,128)(2,1)} %bitcast.281), channel_id=1, replica_groups=mesh['dp'=16,'tensor'=2] {'dp'}, dimensions={0}, use_global_device_ids=true | all-gather | bytes 4352 | tf_op jit(solution)/shard_map/all_gather | solution.py:105
  60.4 37.1 %all-reduce.9 = bf16[512]{0:T(512)(128)(2,1)S(1)} all-reduce(bf16[512]{0:T(512)(128)(2,1)S(1)} %dynamic-update-slice), channel_id=1, replica_groups=mesh['dp'=16,'tensor'=2] {'dp'}, use_global_device_ids=true, to_apply=%add.9 | all-reduce | flops 512 | bytes 2048
  97.4 37.2 %all-gather.1 = bf16[16,1,128]{2,1,0:T(2,128)(2,1)S(1)} all-gather(bf16[1,1,128]{2,1,0:T(2,128)(2,1)} %bitcast.282), channel_id=1, replica_groups=mesh['dp'=16,'tensor'=2] {'dp'}, dimensions={0}, use_global_device_ids=true | all-gather | bytes 4352 | tf_op jit(solution)/shard_map/all_gather | solution.py:111
  135.3 9.2 mul.497
  144.5 15.8 mul.498
  212.6 32.3 %all-gather.14.cloned.1.call-done = bf16[2048,1536]{1,0:T(8,128)(2,1)} async-done(((bf16[128,1536]{1,0:T(8,128)(2,1)}), bf16[2048,1536]{1,0:T(8,128)(2,1)}) %all-gather.14.cloned.1.call-update) | async-done | bytes 6291472 | tf_op jit(solution)/shard_map/all_gather | solution.py:106
  245.0 6.0 fusion.137
  251.1 5.6 fusion.45
  270.6 63.7 %all-gather.16.cloned.1.call-done = bf16[1024,2048]{1,0:T(8,128)(2,1)} async-done(((bf16[1024,128]{1,0:T(8,128)(2,1)}), bf16[1024,2048]{1,0:T(8,128)(2,1)}) %all-gather.16.cloned.1.call-update) | async-done | bytes 4194320 | tf_op jit(solution)/shard_map/all_gather | solution.py:110
  340.1 6.2 scatter_custom_fusion
  346.3 11.3 scatter_custom_fusion.1
  357.5 38.1 %all_gather.40 = bf16[2048,16]{0,1:T(8,128)(2,1)S(1)} all-gather(bf16[128,16]{0,1:T(8,128)(2,1)S(1)} %copy-done.81), channel_id=1, replica_groups=mesh['dp'=16,'tensor'=2] {'dp'}, dimensions={0}, use_global_device_ids=true | all-gather | bytes 69632 | tf_op jit(solution)/shard_map/all_gather | solution.py:112
  403.6 17.7 gather_fusion
  421.3 7.9 multiply_convert_fusion
  429.2 19.9 gather_fusion.2
  449.1 9.2 broadcast_multiply_fusion
  458.3 180.4 %all_to_all.20 = bf16[16,128,2048]{2,1,0:T(8,128)(2,1)} all-to-all(bf16[16,128,2048]{2,1,0:T(8,128)(2,1)S(1)} %get-tuple-element.56), channel_id=1, replica_groups=mesh['dp'=16,'tensor'=2] {'dp'}, dimensions={0} | all-to-all | bytes 16777216 | tf_op jit(solution)/shard_map/all_to_all | solution.py:280
  644.1 11.2 fusion.28
  655.4 172.6 %all-to-all-done = bf16[16,128,2048]{2,1,0:T(8,128)(2,1)} async-done(((bf16[16,128,2048]{2,1,0:T(8,128)(2,1)}), bf16[16,128,2048]{2,1,0:T(8,128)(2,1)}, u32[]{:S(2)}, u32[]{:S(2)}) %all-to-all-start) | async-done | bytes 8388640 | tf_op jit(solution)/shard_map/all_to_all | solution.py:227
  828.0 11.2 fusion.32
  839.1 13.7 fusion.24
  852.8 10.8 fusion.26
  863.6 12.5 add_convert_fusion
  876.1 55.4 %all-to-all-start.3 = ((bf16[16,128,2048]{2,1,0:T(8,128)(2,1)}), bf16[16,128,2048]{2,1,0:T(8,128)(2,1)}, u32[]{:S(2)}, u32[]{:S(2)}) async-start(bf16[16,128,2048]{2,1,0:T(8,128)(2,1)} %add_convert_fusion), calls=%async_computation.3 | async-start | bytes 16777216 | tf_op jit(solution)/shard_map/all_to_all | solution.py:315
  932.3 10.8 convolution_convert_fusion.1
  943.2 164.8 %all-to-all-done.3 = bf16[16,128,2048]{2,1,0:T(8,128)(2,1)} async-done(((bf16[16,128,2048]{2,1,0:T(8,128)(2,1)}), bf16[16,128,2048]{2,1,0:T(8,128)(2,1)}, u32[]{:S(2)}, u32[]{:S(2)}) %all-to-all-start.3) | async-done | bytes 8388640 | tf_op jit(solution)/shard_map/all_to_all | solution.py:315
  1108.0 68.0 %all-to-all-start.1 = ((bf16[16,128,2048]{2,1,0:T(8,128)(2,1)}), bf16[16,128,2048]{2,1,0:T(8,128)(2,1)}, u32[]{:S(2)}, u32[]{:S(2)}) async-start(bf16[16,128,2048]{2,1,0:T(8,128)(2,1)} %convolution_convert_fusion.1), calls=%async_computation.1 | async-start | bytes 16777216 | tf_op jit(solution)/shard_map/all_to_all | solution.py:246
  1177.1 5.5 fusion.151
  1182.7 5.6 fusion.152
  1188.3 230.8 %all-gather.22.cloned.1.call-done = bf16[1408,2048]{1,0:T(8,128)(2,1)} async-done(((bf16[1408,128]{1,0:T(8,128)(2,1)}), bf16[1408,2048]{1,0:T(8,128)(2,1)}) %all-gather.22.cloned.1.call-update) | async-done | bytes 5767184 | tf_op jit(solution)/shard_map/all_gather | solution.py:115
  1419.1 6.8 multiply_convert_fusion.4
  1429.9 11.3 bitcast_convert_fusion
  1441.2 18.6 gather_fusion.3
  1459.8 15.0 reshape.451
  1474.8 9.8 reduce_sum.147
  1484.6 6.7 fusion.39
  1491.4 17.2 gather_fusion.1
  1508.6 10.9 reshape.446
  1519.6 9.0 fusion.53
  1533.3 9.2 fusion.86
  1542.6 5.9 fusion.38
  1555.8 6.4 multiply_reduce_fusion
  1562.2 7.6 fusion.19
  1604.4 6.0 fusion.155
  1611.5 6.4 fusion.156
  1619.1 7.3 fusion.157
  1627.4 8.6 fusion.154
  1645.7 13.1 collective-permute-done.10
  1660.4 6.5 collective-permute-done.9
  1677.1 6.1 fusion.79
  1684.4 6.5 fusion.135
  1692.3 11.2 convolution_bitcast_fusion
  1703.4 10.2 convolution_bitcast_fusion.1
  1713.7 7.9 convolution_bitcast_fusion.2
  1724.3 73.7 %all-reduce.13 = (f32[2048]{0:T(1024)S(1)}, f32[512]{0:T(512)S(1)}, f32[2048]{0:T(1024)S(1)}) all-reduce(f32[2048]{0:T(1024)S(1)} %get-tuple-element.18, f32[512]{0:T(512)S(1)} %get-tuple-element.20, f32[2048]{0:T(1024)S(1)} %get-tuple-element.16), channel_id=2, replica_groups=mesh['dp'=16,'tensor'=2] {'dp'}, use_global_device_ids=true, to_apply=%region_26.27.clone | all-reduce | flops 4608 | bytes 36864
  1799.8 6.0 fusion.50
  1805.8 76.0 %reduce-scatter.19.cloned.1.call-done = f32[128,1408]{1,0:T(8,128)} async-done(((f32[2048,1408]{1,0:T(8,128)}), f32[128,1408]{1,0:T(8,128)}) %reduce-scatter.19.cloned.1.call-update) | async-done | bytes 720912 | tf_op jit(solution)/shard_map/reduce_scatter | solution.py:412
  1881.8 248.5 %reduce-scatter.21.cloned.1.call-done = f32[128,1408]{1,0:T(8,128)} async-done(((f32[2048,1408]{1,0:T(8,128)}), f32[128,1408]{1,0:T(8,128)}) %reduce-scatter.21.cloned.1.call-update) | async-done | bytes 720912 | tf_op jit(solution)/shard_map/reduce_scatter | solution.py:413
  2130.3 248.6 %reduce-scatter.23.cloned.1.call-done = f32[1408,128]{1,0:T(8,128)} async-done(((f32[1408,2048]{1,0:T(8,128)}), f32[1408,128]{1,0:T(8,128)}) %reduce-scatter.23.cloned.1.call-update) | async-done | bytes 720912 | tf_op jit(solution)/shard_map/reduce_scatter | solution.py:414
  2378.9 83.5 %reduce-scatter.17.cloned.1.call-done = f32[128,16]{0,1:T(8,128)} async-done(((f32[2048,16]{0,1:T(8,128)}), f32[128,16]{0,1:T(8,128)}) %reduce-scatter.17.cloned.1.call-update) | async-done | bytes 8208 | tf_op jit(solution)/shard_map/reduce_scatter | solution.py:411
  2462.3 94.2 %reduce-scatter.13.cloned.1.call-done = f32[32,2048]{1,0:T(8,128)} async-done(((f32[512,2048]{1,0:T(8,128)}), f32[32,2048]{1,0:T(8,128)}) %reduce-scatter.13.cloned.1.call-update) | async-done | bytes 262160 | tf_op jit(solution)/shard_map/reduce_scatter | solution.py:408
  2556.5 142.1 %reduce-scatter.11.cloned.1.call-done = f32[128,576]{0,1:T(8,128)} async-done(((f32[2048,576]{0,1:T(8,128)}), f32[128,576]{0,1:T(8,128)}) %reduce-scatter.11.cloned.1.call-update) | async-done | bytes 294928 | tf_op jit(solution)/shard_map/reduce_scatter | solution.py:406
  2698.7 179.9 %reduce-scatter.15.cloned.1.call-done = f32[1024,128]{1,0:T(8,128)} async-done(((f32[1024,2048]{1,0:T(8,128)}), f32[1024,128]{1,0:T(8,128)}) %reduce-scatter.15.cloned.1.call-update) | async-done | bytes 524304 | tf_op jit(solution)/shard_map/reduce_scatter | solution.py:409
  2878.6 213.5 %reduce-scatter.9.cloned.1.call-done = f32[128,1536]{1,0:T(8,128)} async-done(((f32[2048,1536]{1,0:T(8,128)}), f32[128,1536]{1,0:T(8,128)}) %reduce-scatter.9.cloned.1.call-update) | async-done | bytes 786448 | tf_op jit(solution)/shard_map/reduce_scatter | solution.py:405
  (384 shorter events, 177.6 us)
Async XLA Ops:
  7.2 831.9 %copy-start = (bf16[1,2048,704]{1,2,0:T(8,128)(2,1)S(1)}, bf16[1,2048,704]{1,2,0:T(8,128)(2,1)}, u32[]{:S(2)}) copy-start(bf16[1,2048,704]{1,2,0:T(8,128)(2,1)} %param.33) | copy-start | bytes 8650756
  7.2 158.4 %all-gather.10.cloned.1.call-start = ((), (), s32[]{:S(2)}) async-start(), calls=%async_computation.12 | async-start | bytes 2506752 | tf_op jit(solution)/shard_map/all_gather | solution.py:107
  7.9 189.7 %all-gather.12.cloned.1.call-start = ((), (), s32[]{:S(2)}) async-start(), calls=%async_computation.13 | async-start | bytes 2228224 | tf_op jit(solution)/shard_map/all_gather | solution.py:109
  8.7 236.3 %all-gather.14.cloned.1.call-start = ((), (), s32[]{:S(2)}) async-start(), calls=%async_computation.14 | async-start | bytes 6684672 | tf_op jit(solution)/shard_map/all_gather | solution.py:106
  9.4 324.8 %all-gather.16.cloned.1.call-start = ((), (), s32[]{:S(2)}) async-start(), calls=%async_computation.15 | async-start | bytes 4456448 | tf_op jit(solution)/shard_map/all_gather | solution.py:110
  10.0 385.7 %all-reduce.19.cloned.1.call-start = ((), (), s32[]{:S(2)}) async-start(), calls=%async_computation.16 | async-start | bytes 2097152 | tf_op jit(solution)/shard_map/psum | solution.py:201
  12.0 390.4 %copy-start.29 = (s32[256,6]{1,0:T(8,128)}, s32[256,6]{1,0:T(8,128)S(1)}, u32[]{:S(2)}) copy-start(s32[256,6]{1,0:T(8,128)S(1)} %copy.85) | copy-start | bytes 18436
  14.9 230.0 %copy-start.51 = (f32[256]{0:T(256)}, f32[256]{0:T(256)S(1)}, u32[]{:S(2)}) copy-start(f32[256]{0:T(256)S(1)} %fusion.126) | copy-start | bytes 3076
  57.5 187.5 %copy-start.43 = (f32[16,1,128]{2,1,0:T(1,128)}, f32[16,1,128]{2,1,0:T(1,128)S(1)}, u32[]{:S(2)}) copy-start(f32[16,1,128]{2,1,0:T(1,128)S(1)} %convert_element_type.246) | copy-start | bytes 24580
  97.4 99.3 %copy-start.57 = (f32[512]{0:T(512)}, f32[512]{0:T(512)S(1)}, u32[]{:S(2)}) copy-start(f32[512]{0:T(512)S(1)} %convert_element_type.194) | copy-start | bytes 6148
  169.4 81.6 %copy-start.45 = (f32[256,32]{0,1:T(8,128)}, f32[256,32]{0,1:T(8,128)S(1)}, u32[]{:S(2)}) copy-start(f32[256,32]{0,1:T(8,128)S(1)} %get-tuple-element.58) | copy-start | bytes 98308
  169.4 81.6 %copy-start.47 = (f32[256,32]{0,1:T(8,128)}, f32[256,32]{0,1:T(8,128)S(1)}, u32[]{:S(2)}) copy-start(f32[256,32]{0,1:T(8,128)S(1)} %get-tuple-element.59) | copy-start | bytes 98308
  169.4 12.0 collective-permute-start.4
  170.7 15.8 collective-permute-start.5
  172.0 18.5 collective-permute-start.6
  173.3 19.2 collective-permute-start.7
  176.1 17.6 collective-permute-start
  181.4 13.1 collective-permute-start.1
  186.5 8.6 collective-permute-start.2
  190.5 5.4 collective-permute-start.3
  338.9 59.3 %copy-start.55 = (f32[16,1,128]{2,1,0:T(1,128)S(1)}, f32[16,1,128]{2,1,0:T(1,128)}, u32[]{:S(2)}) copy-start(f32[16,1,128]{2,1,0:T(1,128)} %convert_element_type.247) | copy-start | bytes 24580
  340.0 61.6 %copy-start.63 = (s32[1536]{0:T(1024)}, s32[1536]{0:T(1024)S(1)}, u32[]{:S(2)}) copy-start(s32[1536]{0:T(1024)S(1)} %fusion.121) | copy-start | bytes 18436
  638.8 189.2 %all-to-all-start = ((bf16[16,128,2048]{2,1,0:T(8,128)(2,1)}), bf16[16,128,2048]{2,1,0:T(8,128)(2,1)}, u32[]{:S(2)}, u32[]{:S(2)}) async-start(bf16[16,128,2048]{2,1,0:T(8,128)(2,1)} %get-tuple-element.57), calls=%async_computation | async-start | bytes 16777216 | tf_op jit(solution)/shard_map/all_to_all | solution.py:227
  643.5 533.6 %all-gather.18.cloned.1.call-start = ((), (), s32[]{:S(2)}) async-start(), calls=%async_computation.17 | async-start | bytes 6127616 | tf_op jit(solution)/shard_map/all_gather | solution.py:113
  876.1 56.2 %copy-start.85 = (bf16[1,704,2048]{2,1,0:T(8,128)(2,1)S(1)}, bf16[1,704,2048]{2,1,0:T(8,128)(2,1)}, u32[]{:S(2)}) copy-start(bf16[1,704,2048]{2,1,0:T(8,128)(2,1)} %param.35) | copy-start | bytes 8650756
  876.1 231.9 %all-to-all-start.3 = ((bf16[16,128,2048]{2,1,0:T(8,128)(2,1)}), bf16[16,128,2048]{2,1,0:T(8,128)(2,1)}, u32[]{:S(2)}, u32[]{:S(2)}) async-start(bf16[16,128,2048]{2,1,0:T(8,128)(2,1)} %add_convert_fusion), calls=%async_computation.3 | async-start | bytes 16777216 | tf_op jit(solution)/shard_map/all_to_all | solution.py:315
  931.6 251.1 %all-gather.20.cloned.1.call-start = ((), (), s32[]{:S(2)}) async-start(), calls=%async_computation.18 | async-start | bytes 6127616 | tf_op jit(solution)/shard_map/all_gather | solution.py:114
  943.2 233.9 %copy-start.64 = (s32[1536]{0:T(1024)S(1)}, s32[1536]{0:T(1024)}, u32[]{:S(2)}) copy-start(s32[1536]{0:T(1024)} %copy-done.63) | copy-start | bytes 18436
  943.2 233.9 %copy-start.54 = (f32[8,256]{1,0:T(8,128)S(1)}, f32[8,256]{1,0:T(8,128)}, u32[]{:S(2)}) copy-start(f32[8,256]{1,0:T(8,128)} %copy-done.53) | copy-start | bytes 24580
  943.2 233.9 %copy-start.60 = (f32[8,256]{1,0:T(8,128)S(1)}, f32[8,256]{1,0:T(8,128)}, u32[]{:S(2)}) copy-start(f32[8,256]{1,0:T(8,128)} %copy-done.59) | copy-start | bytes 24580
  943.2 233.9 %copy-start.71 = (f32[256]{0:T(256)S(1)}, f32[256]{0:T(256)}, u32[]{:S(2)}) copy-start(f32[256]{0:T(256)} %copy-done.70) | copy-start | bytes 3076
  943.2 234.0 %copy-start.3 = (bf16[256,2048]{1,0:T(8,128)(2,1)S(1)}, bf16[256,2048]{1,0:T(8,128)(2,1)}, u32[]{:S(2)}) copy-start(bf16[256,2048]{1,0:T(8,128)(2,1)} %copy-done.2) | copy-start | bytes 3145732
  1108.0 383.4 %all-to-all-start.1 = ((bf16[16,128,2048]{2,1,0:T(8,128)(2,1)}), bf16[16,128,2048]{2,1,0:T(8,128)(2,1)}, u32[]{:S(2)}, u32[]{:S(2)}) async-start(bf16[16,128,2048]{2,1,0:T(8,128)(2,1)} %convolution_convert_fusion.1), calls=%async_computation.1 | async-start | bytes 16777216 | tf_op jit(solution)/shard_map/all_to_all | solution.py:246
  1176.0 243.1 %all-gather.22.cloned.1.call-start = ((), (), s32[]{:S(2)}) async-start(), calls=%async_computation.19 | async-start | bytes 6127616 | tf_op jit(solution)/shard_map/all_gather | solution.py:115
  1176.8 371.7 %all-reduce.21.cloned.1.call-start = ((), (), s32[]{:S(2)}) async-start(), calls=%async_computation.20 | async-start | bytes 2097152 | tf_op jit(solution)/shard_map/psum | solution.py:327
  1182.7 236.4 %copy-start.15 = (bf16[256,2048]{1,0:T(8,128)(2,1)S(1)}, bf16[256,2048]{1,0:T(8,128)(2,1)}, u32[]{:S(2)}) copy-start(bf16[256,2048]{1,0:T(8,128)(2,1)} %param.19) | copy-start | bytes 3145732
  1425.9 58.7 %copy-start.37 = (bf16[256,1408]{1,0:T(8,128)(2,1)}, bf16[256,1408]{1,0:T(8,128)(2,1)S(1)}, u32[]{:S(2)}) copy-start(bf16[256,1408]{1,0:T(8,128)(2,1)S(1)} %get-tuple-element.33) | copy-start | bytes 2162692
  1491.4 179.2 %all-reduce.23.cloned.1.call-start = ((), (), s32[]{:S(2)}) async-start(), calls=%async_computation.29 | async-start | bytes 4718592 | tf_op jit(solution)/shard_map/psum | solution.py:261
  1583.4 11.0 collective-permute-start.12
  1584.7 12.0 collective-permute-start.13
  1586.0 15.7 collective-permute-start.14
  1587.3 16.1 collective-permute-start.15
  1604.3 277.5 %reduce-scatter.19.cloned.1.call-start = ((), (), s32[]{:S(2)}) async-start(), calls=%async_computation.26 | async-start | bytes 12255232 | tf_op jit(solution)/shard_map/reduce_scatter | solution.py:412
  1610.4 519.8 %reduce-scatter.21.cloned.1.call-start = ((), (), s32[]{:S(2)}) async-start(), calls=%async_computation.27 | async-start | bytes 12255232 | tf_op jit(solution)/shard_map/reduce_scatter | solution.py:413
  1618.0 760.9 %reduce-scatter.23.cloned.1.call-start = ((), (), s32[]{:S(2)}) async-start(), calls=%async_computation.28 | async-start | bytes 12255232 | tf_op jit(solution)/shard_map/reduce_scatter | solution.py:414
  1626.3 836.0 %reduce-scatter.17.cloned.1.call-start = ((), (), s32[]{:S(2)}) async-start(), calls=%async_computation.25 | async-start | bytes 139264 | tf_op jit(solution)/shard_map/reduce_scatter | solution.py:411
  1627.3 929.2 %reduce-scatter.13.cloned.1.call-start = ((), (), s32[]{:S(2)}) async-start(), calls=%async_computation.23 | async-start | bytes 4456448 | tf_op jit(solution)/shard_map/reduce_scatter | solution.py:408
  1636.1 34.3 %copy-start.80 = (f32[256]{0:T(256)S(1)}, f32[256]{0:T(256)}, u32[]{:S(2)}) copy-start(f32[256]{0:T(256)} %fusion.129) | copy-start | bytes 3076
  1636.1 34.3 %copy-start.82 = (f32[32]{0:T(128)S(1)}, f32[32]{0:T(128)}, u32[]{:S(2)}) copy-start(f32[32]{0:T(128)} %multiply_exponential_fusion) | copy-start | bytes 388
  1636.1 34.5 %copy-start.12 = (f32[256,576]{0,1:T(8,128)S(1)}, f32[256,576]{0,1:T(8,128)}, u32[]{:S(2)}) copy-start(f32[256,576]{0,1:T(8,128)} %copy-done.11) | copy-start | bytes 1769476
  1636.1 34.5 %copy-start.58 = (f32[512]{0:T(512)S(1)}, f32[512]{0:T(512)}, u32[]{:S(2)}) copy-start(f32[512]{0:T(512)} %copy-done.57) | copy-start | bytes 6148
  1636.1 34.5 %copy-start.66 = (f32[256]{0:T(256)S(1)}, f32[256]{0:T(256)}, u32[]{:S(2)}) copy-start(f32[256]{0:T(256)} %copy-done.65) | copy-start | bytes 3076
  1636.1 35.7 %copy-start.77 = (f32[256]{0:T(256)S(1)}, f32[256]{0:T(256)}, u32[]{:S(2)}) copy-start(f32[256]{0:T(256)} %copy-done.76) | copy-start | bytes 3076
  1636.1 1062.5 %reduce-scatter.11.cloned.1.call-start = ((), (), s32[]{:S(2)}) async-start(), calls=%async_computation.22 | async-start | bytes 5013504 | tf_op jit(solution)/shard_map/reduce_scatter | solution.py:406
  1640.5 32.5 %copy-start.44 = (f32[16,1,128]{2,1,0:T(1,128)S(1)}, f32[16,1,128]{2,1,0:T(1,128)}, u32[]{:S(2)}) copy-start(f32[16,1,128]{2,1,0:T(1,128)} %copy-done.43) | copy-start | bytes 24580
  1640.5 32.5 %copy-start.52 = (f32[256]{0:T(256)S(1)}, f32[256]{0:T(256)}, u32[]{:S(2)}) copy-start(f32[256]{0:T(256)} %copy-done.51) | copy-start | bytes 3076
  1640.5 18.3 collective-permute-start.10
  1641.8 17.0 collective-permute-start.11
  1643.1 17.2 collective-permute-start.8
  1644.4 22.4 collective-permute-start.9
  1676.1 1202.5 %reduce-scatter.15.cloned.1.call-start = ((), (), s32[]{:S(2)}) async-start(), calls=%async_computation.24 | async-start | bytes 8912896 | tf_op jit(solution)/shard_map/reduce_scatter | solution.py:409
  1683.3 1408.8 %reduce-scatter.9.cloned.1.call-start = ((), (), s32[]{:S(2)}) async-start(), calls=%async_computation.21 | async-start | bytes 13369344 | tf_op jit(solution)/shard_map/reduce_scatter | solution.py:405
  1721.6 78.2 %copy-start.75 = (f32[256]{0:T(256)S(1)}, f32[256]{0:T(256)}, u32[]{:S(2)}) copy-start(f32[256]{0:T(256)} %copy-done.74) | copy-start | bytes 3076
  1799.8 1292.3 %copy-start.1 = (bf16[1,2048,704]{1,2,0:T(8,128)(2,1)S(1)}, bf16[1,2048,704]{1,2,0:T(8,128)(2,1)}, u32[]{:S(2)}) copy-start(bf16[1,2048,704]{1,2,0:T(8,128)(2,1)} %param.33) | copy-start | bytes 8650756
  (71 other events, 539.5 us)
Sparse Core Ops, SparseCore 0:
  10.7 69.7 all-gather.9
  83.3 59.1 all-gather.11
  145.3 99.6 all-gather.13
  247.5 86.7 all-gather.15
  339.0 17.7 all-reduce.18
  647.1 210.0 all-gather.17
  935.4 220.2 all-gather.19
  1180.0 239.0 all-gather.21
  1491.5 18.5 all-reduce.20
  1604.4 28.2 all-reduce.22
  1635.7 246.1 reduce-scatter.18
  1884.7 245.5 reduce-scatter.20
  2133.3 245.5 reduce-scatter.22
  2381.6 80.6 reduce-scatter.16
  2465.0 91.4 reduce-scatter.12
  2562.1 136.4 reduce-scatter.10
  2701.5 177.0 reduce-scatter.14
  2885.6 206.4 reduce-scatter.8
where the time goes:
time: 3110 us; the launch traced here: 3100 us
  waiting for transfers between devices  1990 us (64%)
  blocking collectives  417 us (13%)
  matrix products  267 us (9%)
  local copies, waits for them, and re-layouts  180 us (6%)
  starting transfers between devices  160 us (5%)
  other arithmetic  68.9 us (2%)
    reduce_scatter x1, waiting for transfers between devices, shards(): lax.psum_scatter(grad_sdown, 'dp', scatter_dimension=1, tiled=True)  249 us
    reduce_scatter x1, waiting for transfers between devices, shards(): lax.psum_scatter(grad_sup, 'dp', scatter_dimension=0, tiled=True)  248 us
    all_gather x1, waiting for transfers between devices, shards(): lax.all_gather(shared_down, 'dp', axis=1, tiled=True)  231 us
    reduce_scatter x1, waiting for transfers between devices, shards(): lax.psum_scatter(grad_wq, 'dp', scatter_dimension=0, tiled=True)  214 us
    all_to_all x1, blocking collectives, shards(): lax.all_to_all(send_grads.reshape(dp_count, local_experts * capacity, mod...  180 us
    reduce_scatter x1, waiting for transfers between devices, shards(): lax.psum_scatter(grad_wout, 'dp', scatter_dimension=1, tiled=True)  180 us
    all_to_all x1, waiting for transfers between devices, shards(): lax.all_to_all(send_rows.reshape(dp_count, local_experts * capacity, mode...  173 us
    all_to_all x1, waiting for transfers between devices, shards(): lax.all_to_all(d_slots.reshape(dp_count, local_experts * capacity, model_...  165 us
  transfers between devices with their start and end apart: 37, of which 20 were waited for; matrix products, arithmetic and copies ran while one was open for 13% of the time, Pallas kernels for 0%

commit v1 on v0

--- a/solution.py
+++ b/solution.py
@@ -1,8 +1,11 @@
+import functools
 import math
 
 import jax
 import jax.numpy as jnp
 from jax import lax
+from jax.experimental import pallas as pl
+from jax.experimental.pallas import tpu as pltpu
 from jax.sharding import PartitionSpec as P
 
 NOPE = 128
@@ -66,7 +69,645 @@
     )
 
 
-def shards(
+def ranks_before(hot):
+    count = hot.shape[0]
+    below = jnp.arange(count)[:, None] > jnp.arange(count)[None, :]
+    return matmul(below.astype(jnp.bfloat16), hot.astype(jnp.bfloat16)).astype(jnp.int32)
+
+
+MESH = pl.DeviceIdType.MESH
+
+def z_order(z, k):
+    zz = jnp.where(z >= 2, 3 - z, z)
+    o = [zz, 1 - zz, 2, 3][k]
+    return jnp.where(z >= 2, 3 - o, o)
+
+def ag_kernel(share, x_ref, o_ref, zsem_s, zsem_r, asem_s, asem_r, bsem_s, bsem_r, csem_s, csem_r, lsem):
+    me = lax.axis_index("dp"); core = lax.axis_index("tensor")
+    z = me // 4; y = (me // 2) % 2; x = me % 2
+    xn = z*4 + y*2 + (1-x); yn = z*4 + (1-y)*2 + x
+    up = jnp.minimum(z+1, 3)*4 + y*2 + x; dn = jnp.maximum(z-1, 0)*4 + y*2 + x
+    slot = core if share else 0
+    bar = pltpu.get_barrier_semaphore()
+    def sig(d, c): pl.semaphore_signal(bar, inc=1, device_id=(d, c), device_id_type=MESH)
+    sig(xn, core); sig(yn, core)
+    pl.when(z < 3)(lambda: sig(up, core))
+    pl.when(z > 0)(lambda: sig(dn, core))
+    n = 2 + (z < 3).astype(jnp.int32) + (z > 0).astype(jnp.int32)
+    if share:
+        sig(me, 1-core); n = n + 1
+    pl.semaphore_wait(bar, n)
+    own = pltpu.make_async_copy(x_ref, o_ref.at[me, slot], lsem); own.start()
+
+    def rc(src, dst, ss, rs, dev, c=None):
+        return pltpu.make_async_remote_copy(src_ref=src, dst_ref=dst, send_sem=ss, recv_sem=rs,
+                                            device_id=(dev, core if c is None else c), device_id_type=MESH)
+    waits = []
+    def zcopy(zp, dev, ss):
+        b = zp*4 + y*2 + x
+        return rc(o_ref.at[b, slot], o_ref.at[b, slot], zsem_s.at[ss], zsem_r.at[zp], dev)
+    def xcopy(j, b, half, zp):
+        return rc(o_ref.at[b, slot, half], o_ref.at[b, slot, half], asem_s.at[zp, j], asem_r.at[zp, j], xn)
+    def ycopy(j, b, half, zp):
+        return rc(o_ref.at[b, slot, half], o_ref.at[b, slot, half], bsem_s.at[zp, j], bsem_r.at[zp, j], yn)
+    def sib(b):
+        return rc(o_ref.at[b, slot], o_ref.at[b, slot], csem_s.at[b], csem_r.at[b], me, 1-core)
+
+    own.wait()
+    for k in range(4):
+        zp = z_order(z, k)
+        b = zp*4 + y*2 + x
+        if k > 0:
+            zcopy(zp, up, 0).wait_recv()
+        @pl.when((zp <= z) & (z < 3))
+        def _(): zcopy(zp, up, zp).start()
+        @pl.when((zp >= z) & (z > 0))
+        def _(): zcopy(zp, dn, 4 + zp).start()
+        xcopy(0, b, 0, zp).start()
+        ycopy(0, b, 1, zp).start()
+        ycopy(1, b, 0, zp).start()
+        xcopy(1, b, 1, zp).start()
+        if share: sib(b).start()
+        bx = zp*4 + y*2 + (1-x); by = zp*4 + (1-y)*2 + x
+        if k > 0: hop(*prev)
+        prev = (zp, bx, by)
+        def hop(zp, bx, by):
+            xcopy(0, bx, 0, zp).wait_recv()
+            ycopy(2, bx, 0, zp).start()
+            ycopy(0, by, 1, zp).wait_recv()
+            xcopy(2, by, 1, zp).start()
+            xcopy(1, bx, 1, zp).wait_recv()
+            ycopy(1, by, 0, zp).wait_recv()
+            if share:
+                sib(bx).start(); sib(by).start()
+    hop(*prev)
+    for k in range(4):
+        zp = z_order(z, k)
+        bd = zp*4 + (1-y)*2 + (1-x)
+        ycopy(2, bd, 0, zp).wait_recv()
+        xcopy(2, bd, 1, zp).wait_recv()
+        if share: sib(bd).start()
+    for k in range(4):
+        @pl.when((k <= z) & (z < 3))
+        def _(): zcopy(k, up, k).wait_send()
+        @pl.when((k >= z) & (z > 0))
+        def _(): zcopy(k, dn, 4 + k).wait_send()
+        for j in range(3):
+            xcopy(j, 0, 0, k).wait_send(); ycopy(j, 0, 0, k).wait_send()
+    if share:
+        for b in range(16):
+            sib(b).wait_send()
+            pltpu.make_async_remote_copy(src_ref=o_ref.at[b, slot], dst_ref=o_ref.at[b, 1-slot], send_sem=csem_s.at[b], recv_sem=csem_r.at[b], device_id=(me, 1-core), device_id_type=MESH).wait_recv()
+
+def ag16(x, share, cid):
+    S = pltpu.SemaphoreType.DMA
+    cores = 2 if share else 1
+    return pl.pallas_call(functools.partial(ag_kernel, share),
+        out_shape=jax.ShapeDtypeStruct((16, cores) + x.shape, x.dtype),
+        in_specs=[pl.BlockSpec(memory_space=pl.ANY)], out_specs=pl.BlockSpec(memory_space=pl.ANY),
+        scratch_shapes=[S((8,)), S((4,)), S((4,3)), S((4,3)), S((4,3)), S((4,3)), S((16,)), S((16,)), S],
+        compiler_params=pltpu.CompilerParams(collective_id=cid, has_side_effects=True),
+        )(x)
+
+
+def add_into(dst, src, out=None):
+    out = dst if out is None else out
+    h = dst.shape[0]
+    def step(i, _):
+        r = pl.ds(pl.multiple_of(i * 16, 16), 16)
+        out[r] = (dst[r].astype(jnp.float32) + src[r].astype(jnp.float32)).astype(out.dtype)
+        return 0
+    lax.fori_loop(0, h // 16, step, 0)
+
+def rs_kernel(share, p_ref, o_ref, own, sibr, yr, xr, zr, lsem, cs, cr, xs, xrs, ys, yrs, zs, zrs, fs, fr):
+    me = lax.axis_index("dp"); core = lax.axis_index("tensor")
+    z = me // 4; y = (me // 2) % 2; x = me % 2
+    xn = z*4 + y*2 + (1-x); yn = z*4 + (1-y)*2 + x
+    up = jnp.minimum(z+1, 3)*4 + y*2 + x; dn = jnp.maximum(z-1, 0)*4 + y*2 + x
+    slot = core if share else 0
+    other = 1 - core
+    def rc(src, dst, ss, rs, dev, c=None):
+        return pltpu.make_async_remote_copy(src_ref=src, dst_ref=dst, send_sem=ss, recv_sem=rs,
+                                            device_id=(dev, core if c is None else c), device_id_type=MESH)
+    for k in range(4):
+        zp = z_order(z, 3-k)
+        pltpu.make_async_copy(p_ref.at[pl.ds(zp*4, 4), slot], own.at[pl.ds(zp*4, 4)], lsem.at[zp]).start()
+    bar = pltpu.get_barrier_semaphore()
+    def sig(d, c): pl.semaphore_signal(bar, inc=1, device_id=(d, c), device_id_type=MESH)
+    sig(xn, core); sig(yn, core)
+    pl.when(z < 3)(lambda: sig(up, core))
+    pl.when(z > 0)(lambda: sig(dn, core))
+    n = 2 + (z < 3).astype(jnp.int32) + (z > 0).astype(jnp.int32)
+    if share:
+        sig(me, other); n = n + 1
+    pl.semaphore_wait(bar, n)
+    def sib(zp):
+        return rc(p_ref.at[pl.ds(zp*4, 4), other], sibr.at[pl.ds(zp*4, 4)], cs.at[zp], cr.at[zp], me, other)
+    if share:
+        for k in range(4): sib(z_order(z, 3-k)).start()
+    def y_(j, b, half, zp): return rc(own.at[b, half], yr.at[zp, j], ys.at[zp, j], yrs.at[zp, j], yn)
+    def x_(j, b, half, zp): return rc(own.at[b, half], xr.at[zp, j], xs.at[zp, j], xrs.at[zp, j], xn)
+    def zc(zp, dev, d):
+        b = zp*4 + y*2 + x
+        return rc(own.at[b], zr.at[d, zp], zs.at[zp], zrs.at[d, zp], dev)
+    def blk(zp, yy, xx): return zp*4 + yy*2 + xx
+    def s1(k):
+        zp = z_order(z, 3-k)
+        pltpu.make_async_copy(p_ref.at[pl.ds(zp*4, 4), slot], own.at[pl.ds(zp*4, 4)], lsem.at[zp]).wait()
+        if share:
+            sib(zp).wait_recv()
+            def one(q, _):
+                b = zp*4 + q
+                add_into(own.at[b, 0], sibr.at[b, 0]); add_into(own.at[b, 1], sibr.at[b, 1])
+                return 0
+            lax.fori_loop(0, 4, one, 0)
+        y_(0, blk(zp, 1-y, 1-x), 0, zp).start()
+        x_(0, blk(zp, 1-y, 1-x), 1, zp).start()
+        y_(1, blk(zp, 1-y, x), 0, zp).start()
+        x_(1, blk(zp, y, 1-x), 1, zp).start()
+    def s2(k):
+        zp = z_order(z, 3-k)
+        y_(0, blk(zp, 1-y, 1-x), 0, zp).wait_recv()
+        add_into(own.at[blk(zp, y, 1-x), 0], yr.at[zp, 0])
+        x_(2, blk(zp, y, 1-x), 0, zp).start()
+        x_(0, blk(zp, 1-y, 1-x), 1, zp).wait_recv()
+        add_into(own.at[blk(zp, 1-y, x), 1], xr.at[zp, 0])
+        y_(2, blk(zp, 1-y, x), 1, zp).start()
+        mine = blk(zp, y, x)
+        y_(1, blk(zp, 1-y, x), 0, zp).wait_recv()
+        add_into(own.at[mine, 0], yr.at[zp, 1])
+        x_(1, blk(zp, y, 1-x), 1, zp).wait_recv()
+        add_into(own.at[mine, 1], xr.at[zp, 1])
+    def s3(k):
+        zp = z_order(z, 3-k)
+        mine = blk(zp, y, x)
+        x_(2, blk(zp, y, 1-x), 0, zp).wait_recv()
+        add_into(own.at[mine, 0], xr.at[zp, 2])
+        y_(2, blk(zp, 1-y, x), 1, zp).wait_recv()
+        add_into(own.at[mine, 1], yr.at[zp, 2])
+        def both(d):
+            add_into(own.at[mine, 0], zr.at[d, zp, 0]); add_into(own.at[mine, 1], zr.at[d, zp, 1])
+        if k < 3:
+            @pl.when((zp < z) & (z < 3))
+            def _():
+                zc(zp, up, 1).wait_recv(); both(1)
+            @pl.when((zp > z) & (z > 0))
+            def _():
+                zc(zp, dn, 0).wait_recv(); both(0)
+            @pl.when(zp < z)
+            def _(): zc(zp, dn, 1).start()
+            @pl.when(zp > z)
+            def _(): zc(zp, up, 0).start()
+        else:
+            @pl.when(z < 3)
+            def _():
+                zc(zp, up, 1).wait_recv(); both(1)
+            @pl.when(z > 0)
+            def _():
+                zc(zp, dn, 0).wait_recv(); both(0)
+    s1(0); s1(1); s2(0); s1(2); s2(1); s3(0); s1(3); s2(2); s3(1); s2(3); s3(2); s3(3)
+    if share:
+        mine = me
+        for a in range(2):
+            add = own.at[mine, a]
+            def step(i, _):
+                r = pl.ds(pl.multiple_of(i*16, 16), 16)
+                o_ref[core, a, r] = add[r]
+                return 0
+            lax.fori_loop(0, add.shape[0]//16, step, 0)
+        f = rc(o_ref.at[core], o_ref.at[core], fs, fr, me, other)
+        f.start()
+        pltpu.make_async_remote_copy(src_ref=o_ref.at[core], dst_ref=o_ref.at[other], send_sem=fs, recv_sem=fr, device_id=(me, other), device_id_type=MESH).wait_recv()
+        f.wait_send()
+        for k in range(4): sib(k).wait_send()
+    else:
+        for a in range(2):
+            add = own.at[me, a]
+            def step(i, _):
+                r = pl.ds(pl.multiple_of(i*16, 16), 16)
+                o_ref[0, a, r] = add[r].astype(o_ref.dtype)
+                return 0
+            lax.fori_loop(0, add.shape[0]//16, step, 0)
+    for k in range(4):
+        for j in range(3):
+            x_(j, 0, 0, k).wait_send(); y_(j, 0, 0, k).wait_send()
+        @pl.when(k != z)
+        def _(): zc(k, up, 0).wait_send()
+
+def rs16(p, share, cid):
+    S = pltpu.SemaphoreType.DMA
+    cores = 2 if share else 1
+    blkshape = p.shape[2:]
+    half = p.shape[3:]
+    V = lambda s: pltpu.VMEM(s, p.dtype)
+    return pl.pallas_call(functools.partial(rs_kernel, share),
+        out_shape=jax.ShapeDtypeStruct((cores,) + blkshape, p.dtype),
+        in_specs=[pl.BlockSpec(memory_space=pl.ANY)], out_specs=pl.BlockSpec(memory_space=pltpu.VMEM),
+        scratch_shapes=[V((16,) + blkshape), V((16,) + blkshape) if share else V((1, 2, 16, 128)), V((4, 3) + half), V((4, 3) + half), V((2, 4) + blkshape),
+            S((4,)), S((4,)), S((4,)), S((4,3)), S((4,3)), S((4,3)), S((4,3)), S((4,)), S((2,4)), S, S],
+        compiler_params=pltpu.CompilerParams(collective_id=cid, has_side_effects=True, vmem_limit_bytes=60 << 20),
+        )(p)
+
+
+def swapped(v):
+    return lax.ppermute(v, "tensor", [(0, 1), (1, 0)])
+
+
+def summed(v):
+    low = lax.reduce_precision(v, 8, 7)
+    return low + swapped(low.astype(jnp.bfloat16)).astype(jnp.float32)
+
+
+def my_half(v, rows):
+    return lax.dynamic_slice_in_dim(v, lax.axis_index("tensor") * rows, rows, 0)
+
+
+def gather_rows(v, cid):
+    rows, width = v.shape[0] // 2, v.shape[1]
+    moved = ag16(my_half(v, rows).reshape(2, rows // 2, width), True, cid)
+    return moved.reshape(32 * rows, width)
+
+
+def scatter_rows(v, cid):
+    rows, width = v.shape[0] // 32, v.shape[1]
+    return rs16(v.reshape(16, 2, 2, rows // 2, width), True, cid).reshape(2 * rows, width)
+
+
+def exchange(parts):
+    return lax.all_to_all(parts, "dp", split_axis=0, concat_axis=0, tiled=True)
+
+
+def shards_sixteen(
+    tokens,
+    out_grad,
+    segments,
+    routes,
+    attn_gain,
+    w_query,
+    w_latent,
+    latent_gain,
+    w_keyval,
+    w_out,
+    moe_gain,
+    w_router,
+    shared_gate,
+    shared_up,
+    shared_down,
+    expert_gate,
+    routed_up_weight,
+    expert_down,
+):
+    n_rows, width = tokens.shape
+    dp_count = lax.axis_size("dp")
+    dp_index = lax.axis_index("dp")
+    seq_len = segments.shape[1]
+    total = n_rows * dp_count
+    hop_count = (WINDOW - 1) // n_rows + 1
+    n_keys = (hop_count + 1) * n_rows
+    experts = w_router.shape[1]
+    capacity = 4 * n_rows * TOPK // (3 * experts)
+    score_scale = (NOPE + ROPE) ** (-0.5)
+    row_start = dp_index * n_rows
+    seg_row = segments[0]
+    depth = w_query.shape[0]
+    q_width, o_width, kv_width = w_query.shape[1], w_out.shape[0], w_keyval.shape[1]
+    kv_rows = w_keyval.shape[0]
+    kv_cuts = depth // kv_rows
+    kv_part = kv_width // kv_cuts
+    lat_width = w_latent.shape[1]
+    small = (lat_width + experts + 3 + 127) // 128 * 128
+
+    shared_part = shared_gate.shape[1] // dp_count
+    shared_send = jnp.stack(
+        [
+            shared_gate.reshape(depth, dp_count, shared_part).transpose(1, 2, 0),
+            shared_up.reshape(depth, dp_count, shared_part).transpose(1, 2, 0),
+            shared_down.reshape(dp_count, shared_part, depth),
+        ],
+        1,
+    )
+    shared_all = exchange(shared_send).transpose(1, 2, 0, 3).reshape(3, shared_part, width)
+    sg_t, su_t, sd = shared_all[0], shared_all[1], shared_all[2]
+    all_routes = lax.all_gather(routes, "dp", axis=0, tiled=True)
+
+    gains = jnp.stack(
+        [attn_gain, moe_gain, jnp.pad(latent_gain, (0, depth - kv_rows))], 1
+    )
+    packed = jnp.concatenate(
+        [
+            w_query,
+            w_out.T,
+            w_keyval.reshape(kv_rows, kv_cuts, kv_part).transpose(1, 0, 2).reshape(depth, kv_part),
+            w_latent,
+            w_router,
+            gains,
+            jnp.zeros((depth, small - lat_width - experts - 3), jnp.bfloat16),
+        ],
+        1,
+    )
+    pack_width = packed.shape[1]
+    weights = ag16(packed.reshape(2, depth // 2, pack_width), False, 1).reshape(width, pack_width)
+    at = 0
+    wq_full = weights[:, at : at + q_width]
+    at += q_width
+    wo_t = weights[:, at : at + o_width]
+    at += o_width
+    wkv_full = (
+        weights[:, at : at + kv_part]
+        .reshape(dp_count, kv_cuts, kv_rows, kv_part)
+        .transpose(0, 2, 1, 3)
+        .reshape(dp_count * kv_rows, kv_width)
+    )
+    at += kv_part
+    wlat_full = weights[:, at : at + lat_width]
+    at += lat_width
+    wr_full = weights[:, at : at + experts]
+    at += experts
+    gain_attn = weights[:, at].astype(jnp.float32)
+    gain_moe = weights[:, at + 1].astype(jnp.float32)
+    gain_latent = (
+        weights[:, at + 2].reshape(dp_count, depth)[:, :kv_rows].reshape(-1).astype(jnp.float32)
+    )
+
+    grad_all = gather_rows(out_grad, 2)
+
+    local_heads = q_width // (NOPE + ROPE)
+    positions = (row_start + jnp.arange(n_rows, dtype=jnp.int32)).astype(jnp.float32)
+    cos_tab, sin_tab = rope_tables(positions)
+    resid_in = tokens.astype(jnp.float32)
+    normed, attn_norm_back = jax.vjp(rms_scale, resid_in, gain_attn)
+    normed_low = normed.astype(jnp.bfloat16)
+
+    def rope_queries(q_flat):
+        shaped = q_flat.reshape(n_rows, local_heads, NOPE + ROPE)
+        return jnp.concatenate(
+            [shaped[..., :NOPE], rotate(shaped[..., NOPE:], cos_tab[:, None], sin_tab[:, None])], -1
+        )
+
+    queries, query_back = jax.vjp(rope_queries, matmul(normed_low, wq_full))
+    query_low = queries.astype(jnp.bfloat16)
+
+    def latent_piece(latent_raw, gain_vec):
+        return (
+            rms_scale(latent_raw[:, :RANK], gain_vec),
+            rotate(latent_raw[:, RANK:], cos_tab, sin_tab),
+        )
+
+    (latent, key_rope), latent_back = jax.vjp(
+        latent_piece, matmul(normed_low, wlat_full), gain_latent
+    )
+    own_keys = jnp.concatenate([latent.astype(jnp.bfloat16), key_rope.astype(jnp.bfloat16)], 1)
+    keys_all = jnp.concatenate(
+        [passed_along(own_keys, "dp", d) for d in range(hop_count, 0, -1)] + [own_keys], 0
+    )
+    keys_latent, keys_rope = keys_all[:, :RANK], keys_all[:, RANK:]
+    keyval = (
+        matmul(keys_latent, wkv_full).astype(jnp.bfloat16).reshape(n_keys, local_heads, NOPE + VDIM)
+    )
+    key_nope = keyval[..., :NOPE]
+    values = keyval[..., NOPE:]
+    key_pos = row_start - hop_count * n_rows + jnp.arange(n_keys, dtype=jnp.int32)
+    query_pos = row_start + jnp.arange(n_rows, dtype=jnp.int32)
+    padded_seg = jnp.concatenate([jnp.full((hop_count * n_rows,), -1, jnp.int32), seg_row])
+    key_seg = lax.dynamic_slice_in_dim(padded_seg, row_start, n_keys, 0)
+    query_seg = lax.dynamic_slice_in_dim(seg_row, row_start, n_rows, 0)
+    allowed = (key_pos[None, :] >= 0) & (key_pos[None, :] <= query_pos[:, None])
+    allowed = (
+        allowed
+        & (query_pos[:, None] - key_pos[None, :] < WINDOW)
+        & (query_seg[:, None] == key_seg[None, :])
+    )
+
+    def masked_scores():
+        nope_part = jnp.einsum(
+            "qhd,khd->hqk", query_low[..., :NOPE], key_nope, preferred_element_type=jnp.float32
+        )
+        rope_part = jnp.einsum(
+            "qhr,kr->hqk", query_low[..., NOPE:], keys_rope, preferred_element_type=jnp.float32
+        )
+        return jnp.where(allowed[None], score_scale * (nope_part + rope_part), -jnp.inf)
+
+    scores = masked_scores()
+    top_score = jnp.max(scores, axis=-1, keepdims=True)
+    exp_scores = jnp.exp(scores - top_score)
+    denom = jnp.sum(exp_scores, axis=-1, keepdims=True)
+    attn_probs = exp_scores / denom
+    log_total = top_score + jnp.log(denom)
+    attended = jnp.einsum(
+        "hqk,khv->qhv", attn_probs.astype(jnp.bfloat16), values, preferred_element_type=jnp.float32
+    )
+    attended_low = attended.astype(jnp.bfloat16).reshape(n_rows, local_heads * VDIM)
+    middle = resid_in + summed(matmul_nt(attended_low, wo_t))
+    moe_normed, moe_norm_back = jax.vjp(rms_scale, middle, gain_moe)
+    moe_low = moe_normed.astype(jnp.bfloat16)
+    router, router_back = jax.vjp(
+        lambda logit_vals: jax.nn.softmax(logit_vals, axis=-1), matmul(moe_low, wr_full)
+    )
+
+    moe_all = gather_rows(moe_low, 3)
+    chosen = jnp.any(all_routes == dp_index, axis=1).reshape(dp_count, n_rows)
+    earlier = jnp.arange(n_rows)[:, None] < jnp.arange(n_rows)[None, :]
+    rank = matmul(chosen.astype(jnp.bfloat16), earlier.astype(jnp.bfloat16)).astype(jnp.int32)
+    pick = (
+        (rank[:, None, :] == jnp.arange(capacity, dtype=jnp.int32)[None, :, None])
+        & chosen[:, None, :]
+    ).astype(jnp.bfloat16)
+
+    def picked(v):
+        return (
+            jnp.einsum(
+                "bst,btd->bsd",
+                pick,
+                v.reshape(dp_count, n_rows, width),
+                preferred_element_type=jnp.float32,
+            )
+            .astype(jnp.bfloat16)
+            .reshape(dp_count * capacity, width)
+        )
+
+    def put_back(v):
+        return jnp.einsum(
+            "bst,bsd->btd",
+            pick,
+            v.reshape(dp_count, capacity, v.shape[1]),
+            preferred_element_type=jnp.float32,
+        ).reshape(total, v.shape[1])
+
+    w_gate, w_up, w_down = expert_gate[0], routed_up_weight[0], expert_down[0]
+    rows_in = picked(moe_all)
+    rows_grad = picked(grad_all)
+    row_router = jax.nn.softmax(matmul(rows_in, wr_full), axis=-1)
+    row_gate = lax.dynamic_slice_in_dim(row_router, dp_index, 1, 1)
+    exp_act, exp_act_back = jax.vjp(gated_act, matmul(rows_in, w_gate), matmul(rows_in, w_up))
+    act_low = exp_act.astype(jnp.bfloat16)
+    exp_out = (row_gate * matmul(act_low, w_down)).astype(jnp.bfloat16)
+    shared_act, shared_back = jax.vjp(
+        gated_act, matmul_nt(moe_all, sg_t), matmul_nt(moe_all, su_t)
+    )
+    shared_low = shared_act.astype(jnp.bfloat16)
+    out_part = (put_back(exp_out) + matmul(shared_low, sd)).astype(jnp.bfloat16)
+    result = (middle + scatter_rows(out_part, 4).astype(jnp.float32)).astype(jnp.bfloat16)
+
+    d_pre = matmul_nt(rows_grad, w_down)
+    row_d_gate = jnp.sum(act_low.astype(jnp.float32) * d_pre, axis=1, keepdims=True)
+    d_ea, d_eb = exp_act_back(row_gate * d_pre)
+    d_ea_low, d_eb_low = d_ea.astype(jnp.bfloat16), d_eb.astype(jnp.bfloat16)
+    d_slots = matmul_nt(d_ea_low, w_gate) + matmul_nt(d_eb_low, w_up)
+    d_sa, d_sb = shared_back(matmul_nt(grad_all, sd))
+    d_sa_low, d_sb_low = d_sa.astype(jnp.bfloat16), d_sb.astype(jnp.bfloat16)
+    lane = jnp.arange(128, dtype=jnp.int32)[None, :]
+    d_gate_cols = put_back(
+        jnp.where(lane == dp_index, row_d_gate, 0.0).astype(jnp.bfloat16)
+    )
+    d_part = put_back(d_slots.astype(jnp.bfloat16)) + matmul(d_sa_low, sg_t) + matmul(d_sb_low, su_t)
+    d_home = scatter_rows(jnp.concatenate([d_part, d_gate_cols], 1).astype(jnp.bfloat16), 5).astype(
+        jnp.float32
+    )
+    scaled_act = (row_gate * act_low.astype(jnp.float32)).astype(jnp.bfloat16)
+    grad_down = matmul_tn(scaled_act, rows_grad)[None]
+    grad_gate = matmul_tn(rows_in, d_ea_low)[None]
+    grad_up = matmul_tn(rows_in, d_eb_low)[None]
+    shared_grads = jnp.stack(
+        [matmul_tn(d_sa_low, moe_all), matmul_tn(d_sb_low, moe_all), matmul_tn(shared_low, grad_all)]
+    ).astype(jnp.bfloat16)
+    home = exchange(
+        shared_grads.reshape(3, shared_part, dp_count, depth).transpose(2, 0, 1, 3)
+    ).astype(jnp.float32)
+    home = home.transpose(1, 0, 2, 3).reshape(3, dp_count * shared_part, depth)
+    grad_sgate, grad_sup, grad_sdown = home[0].T, home[1].T, home[2]
+
+    grad_y = out_grad.astype(jnp.float32)
+    d_gate_all = d_home[:, width : width + experts]
+    routed_here = jnp.any(
+        routes[:, :, None] == jnp.arange(experts, dtype=jnp.int32)[None, None, :], axis=1
+    )
+    (d_logits,) = router_back(jnp.where(routed_here, d_gate_all, 0.0))
+    d_logits_low = d_logits.astype(jnp.bfloat16)
+    grad_router = matmul_tn(moe_low, d_logits_low)
+    d_moe = d_home[:, :width] + matmul_nt(d_logits_low, wr_full)
+    d_mid_norm, grad_gain_moe = moe_norm_back(d_moe)
+    d_middle = grad_y + d_mid_norm
+    d_middle_low = d_middle.astype(jnp.bfloat16)
+    grad_wo_t = matmul_tn(d_middle_low, attended_low)
+    d_att_low = matmul(d_middle_low, wo_t).astype(jnp.bfloat16).reshape(n_rows, local_heads, VDIM)
+    again_probs = jnp.exp(masked_scores() - log_total)
+    d_values = jnp.einsum(
+        "hqk,qhv->khv",
+        again_probs.astype(jnp.bfloat16),
+        d_att_low,
+        preferred_element_type=jnp.float32,
+    )
+    d_probs = jnp.einsum("qhv,khv->hqk", d_att_low, values, preferred_element_type=jnp.float32)
+    d_scores = (
+        again_probs * (d_probs - jnp.sum(d_probs * again_probs, axis=-1, keepdims=True))
+    ).astype(jnp.bfloat16)
+    d_query_nope = score_scale * jnp.einsum(
+        "hqk,khd->qhd", d_scores, key_nope, preferred_element_type=jnp.float32
+    )
+    d_query_rope = score_scale * jnp.einsum(
+        "hqk,kr->qhr", d_scores, keys_rope, preferred_element_type=jnp.float32
+    )
+    d_key_nope = score_scale * jnp.einsum(
+        "hqk,qhd->khd", d_scores, query_low[..., :NOPE], preferred_element_type=jnp.float32
+    )
+    d_key_rope = score_scale * jnp.einsum(
+        "hqk,qhr->kr", d_scores, query_low[..., NOPE:], preferred_element_type=jnp.float32
+    )
+    (d_q_raw,) = query_back(jnp.concatenate([d_query_nope, d_query_rope], -1))
+    d_q_low = d_q_raw.astype(jnp.bfloat16)
+    grad_wq = matmul_tn(normed_low, d_q_low)
+    d_kv_low = (
+        jnp.concatenate([d_key_nope, d_values], -1)
+        .astype(jnp.bfloat16)
+        .reshape(n_keys, local_heads * (NOPE + VDIM))
+    )
+    grad_wkv = matmul_tn(keys_latent, d_kv_low)
+    d_keys = jnp.concatenate([matmul_nt(d_kv_low, wkv_full), d_key_rope], 1)
+    d_own = d_keys[hop_count * n_rows :]
+    d_keys_low = d_keys.astype(jnp.bfloat16)
+    for distance in range(hop_count, 0, -1):
+        lower = (hop_count - distance) * n_rows
+        d_own = d_own + passed_along(
+            d_keys_low[lower : lower + n_rows], "dp", -distance
+        ).astype(jnp.float32)
+    both = summed(jnp.concatenate([matmul_nt(d_q_low, wq_full), d_own], 1))
+    d_normed, own_latent, own_rope = (
+        both[:, :width],
+        both[:, width : width + RANK],
+        both[:, width + RANK :],
+    )
+    d_latent_raw, grad_gain_latent = latent_back((own_latent, own_rope))
+    d_latent_low = d_latent_raw.astype(jnp.bfloat16)
+    grad_wlat = matmul_tn(normed_low, d_latent_low)
+    d_normed = d_normed + matmul_nt(d_latent_low, wlat_full)
+    d_tokens_norm, grad_gain_attn = attn_norm_back(d_normed)
+    token_input_gradient = d_middle + d_tokens_norm
+
+    grad_gains = jnp.stack(
+        [
+            grad_gain_attn.reshape(dp_count, depth),
+            grad_gain_moe.reshape(dp_count, depth),
+            jnp.pad(grad_gain_latent.reshape(dp_count, kv_rows), ((0, 0), (0, depth - kv_rows))),
+        ],
+        2,
+    ).reshape(width, 3)
+    grads = jnp.concatenate(
+        [
+            grad_wq.astype(jnp.bfloat16),
+            grad_wo_t.astype(jnp.bfloat16),
+            grad_wkv.astype(jnp.bfloat16)
+            .reshape(dp_count, kv_rows, kv_cuts, kv_part)
+            .transpose(0, 2, 1, 3)
+            .reshape(width, kv_part),
+            grad_wlat.astype(jnp.bfloat16),
+            grad_router.astype(jnp.bfloat16),
+            grad_gains.astype(jnp.bfloat16),
+            jnp.zeros((width, small - lat_width - experts - 3), jnp.bfloat16),
+        ],
+        1,
+    )
+    mine = (
+        rs16(grads.reshape(dp_count, 1, 2, depth // 2, pack_width), False, 6)
+        .reshape(depth, pack_width)
+        .astype(jnp.float32)
+    )
+    at = 0
+    out_wq = mine[:, at : at + q_width]
+    at += q_width
+    out_wo = mine[:, at : at + o_width].T
+    at += o_width
+    out_wkv = (
+        mine[:, at : at + kv_part]
+        .reshape(kv_cuts, kv_rows, kv_part)
+        .transpose(1, 0, 2)
+        .reshape(kv_rows, kv_width)
+    )
+    at += kv_part
+    out_wlat = mine[:, at : at + lat_width]
+    at += lat_width
+    out_router = mine[:, at : at + experts]
+    at += experts
+    return (
+        result,
+        token_input_gradient,
+        mine[:, at],
+        out_wq,
+        out_wlat,
+        mine[:kv_rows, at + 2],
+        out_wkv,
+        out_wo,
+        mine[:, at + 1],
+        out_router,
+        grad_sgate,
+        grad_sup,
+        grad_sdown,
+        grad_gate,
+        grad_up,
+        grad_down,
+    )
+
+
+def shards_general(
     tokens,
     out_grad,
     segments,
@@ -213,7 +854,7 @@
     flat_routes = routes.reshape(-1)
     assign_count = flat_routes.shape[0]
     flat_hot = (flat_routes[:, None] == expert_ids[None, :]).astype(jnp.int32)
-    earlier = jnp.cumsum(flat_hot, axis=0) - flat_hot
+    earlier = ranks_before(flat_hot)
     slot_in = jnp.sum(earlier * flat_hot, axis=1)
     target = flat_routes * capacity + slot_in
     assign_ids = jnp.arange(assign_count, dtype=jnp.int32)
@@ -442,8 +1083,9 @@
         P("dp", None, "tensor"),
         P("dp", "tensor", None),
     )
+    body = shards_sixteen if mesh.shape["dp"] == 16 and mesh.shape["tensor"] == 2 else shards_general
     return jax.shard_map(
-        shards,
+        body,
         mesh=mesh,
         in_specs=placed,
         out_specs=(

time: 3110 us -> 1360 us (0.44)
  waiting for transfers between devices: 1990 us -> 8.81 us
  Pallas kernels: 0 us -> 689 us
  blocking collectives: 417 us -> 43 us
  starting transfers between devices: 160 us -> 28.8 us
  matrix products: 267 us -> 361 us
    reduce_scatter x8 -> x0, waiting for transfers between devices: 1290 us -> none  [the longest x1 249 us: shards(): lax.psum_scatter(grad_sdown, 'dp', scatter_dimension=1, tiled=True)]
    pallas_call x0 -> x6, Pallas kernels: none -> 689 us  [the longest x3 347 us: ag16(): pl.pallas_call(functools.partial(ag_kernel, share), out_shape=jax.ShapeDt...]
    all_to_all x3 -> x2, waiting for transfers between devices: 337 us -> 0.01 us  [exchange(): return lax.all_to_all(parts, 'dp', split_axis=0, concat_axis=0, tiled=True)]
    all_gather x7 -> x0, waiting for transfers between devices: 327 us -> none  [the longest x1 231 us: shards(): lax.all_gather(shared_down, 'dp', axis=1, tiled=True)]
    all_to_all x1 -> x0, blocking collectives: 180 us -> none  [shards(): lax.all_to_all(send_grads.reshape(dp_count, local_experts * capacity, mod...]
    all_to_all x3 -> x2, starting transfers between devices: 128 us -> 8.91 us  [exchange(): return lax.all_to_all(parts, 'dp', split_axis=0, concat_axis=0, tiled=True)]
    unnamed x2 -> x0, blocking collectives: 111 us -> none
    all_gather x3 -> x1, blocking collectives: 118 us -> 43 us  [shards_sixteen(): all_routes = lax.all_gather(routes, 'dp', axis=0, tiled=True)]
  transfers between devices with their start and end apart: 37 -> 12, of which waited for: 20 -> 3; matrix products, arithmetic and copies ran while one was open for 13% -> 26% of each run, Pallas kernels for 0% -> 26%
where the time goes in v1:
time: 1360 us; the launch traced here: 1350 us
  Pallas kernels  689 us (51%)
  matrix products  361 us (27%)
  local copies, waits for them, and re-layouts  163 us (12%)
  other arithmetic  52.7 us (4%)
  blocking collectives  43 us (3%)
  starting transfers between devices  28.8 us (2%)
    pallas_call x3, Pallas kernels, ag16(): pl.pallas_call(functools.partial(ag_kernel, share), out_shape=jax.ShapeDt...  347 us
    pallas_call x3, Pallas kernels, rs16(): pl.pallas_call(functools.partial(rs_kernel, share), out_shape=jax.ShapeDt...  342 us
    dot_general x13, matrix products, matmul(): return jnp.dot(left_mat, right_mat, preferred_element_type=jnp.float32)  110 us
    dot_general x11, matrix products, matmul_nt(): lax.dot_general(left_mat, right_mat, (((1,), (1,)), ((), ())), preferred_...  87.4 us
    dot_general x11, matrix products, matmul_tn(): lax.dot_general(left_mat, right_mat, (((0,), (0,)), ((), ())), preferred_...  71.1 us
    unnamed x229, local copies, waits for them, and re-layouts  43.8 us
    all_gather x1, blocking collectives, shards_sixteen(): all_routes = lax.all_gather(routes, 'dp', axis=0, tiled=True)  43 us
    dot_general x2, local copies, waits for them, and re-layouts, matmul_tn(): lax.dot_general(left_mat, right_mat, (((0,), (0,)), ((), ())), preferred_...  41.5 us
  transfers between devices with their start and end apart: 12, of which 3 were waited for; matrix products, arithmetic and copies ran while one was open for 26% of the time, Pallas kernels for 26%

profile of v1, /device:TPU:0, one launch (start us, length us, event | category | flops | bytes accessed | tf_op | source)
XLA Modules:
  0.0 1349.3 jit_solution(320682267689441979)
XLA Ops:
  11.2 159.9 %shard_map.297 = bf16[16,1,2,64,3712]{4,3,2,1,0:T(8,128)(2,1)} custom-call(bf16[2,64,3712]{2,1,0:T(8,128)(2,1)} %concatenate.89.x_ref), custom_call_target="tpu_custom_call" | custom-call | tf_op jit(solution)/shard_map/pallas_call | solution.py:165
  179.7 3.5 fusion.49
  185.6 4.1 collective-permute-start.3
  192.2 4.2 collective-permute-start.1
  196.4 3.6 collective-permute-start
  205.4 4.4 all-to-all-start
  209.9 7.2 fusion.15
  217.1 43.0 %all_gather.3 = s32[4096,6]{0,1:T(8,128)S(1)} all-gather(s32[256,6]{0,1:T(8,128)S(1)} %copy-done.66), channel_id=1, replica_groups=mesh['dp'=16,'tensor'=2] {'dp'}, dimensions={0}, use_global_device_ids=true | all-gather | bytes 104448 | tf_op jit(solution)/shard_map/all_gather | solution.py:391
  268.0 3.0 slice.200
  271.1 3.4 copy.301
  276.4 92.6 %shard_map.300 = bf16[16,2,2,64,2048]{4,3,2,1,0:T(8,128)(2,1)} custom-call(bf16[2,64,2048]{2,1,0:T(8,128)(2,1)} %bitcast.300), custom_call_target="tpu_custom_call" | custom-call | tf_op jit(solution)/shard_map/pallas_call | solution.py:165
  369.0 20.8 %copy.339 = bf16[2048,4096]{1,0:T(8,128)(2,1)} copy(bf16[2048,4096]{0,1:T(8,128)(2,1)} %bitcast.241) | data formatting | bytes 33554432 | tf_op jit(solution)/shard_map/dot_general | solution.py:67
  394.0 3.2 convolution_convert_fusion.1
  402.0 4.8 copy.356
  406.8 7.6 fusion.53
  414.4 5.5 fusion.176
  427.1 3.7 fusion.177
  431.2 9.8 convolution_convert_fusion.2
  443.8 3.2 fusion.179
  448.0 94.5 %shard_map.298 = bf16[16,2,2,64,2048]{4,3,2,1,0:T(8,128)(2,1)} custom-call(bf16[2,64,2048]{2,1,0:T(8,128)(2,1)} %bitcast.299), custom_call_target="tpu_custom_call" | custom-call | tf_op jit(solution)/shard_map/pallas_call | solution.py:165
  542.5 7.5 convolution_convert_fusion.3
  550.0 3.6 fusion.178
  553.6 8.0 fusion.34
  561.6 8.0 fusion.38
  569.6 16.3 %fusion.7 = (bf16[2048]{0:T(1024)(128)(2,1)S(1)}, bf16[2048,704]{0,1:T(8,128)(2,1)}, bf16[2048,704]{0,1:T(8,128)(2,1)}, bf16[2048,704]{0,1:T(8,128)(2,1)}) fusion(f32[2048,704]{0,1:T(8,128)} %fusion.34, f32[2048,704]{0,1:T(8,128)} %fusion.38, f32[2048]{0:T(1024)S(1)} %bitcast.326, bf16[2048,2048]{1,0:T(8,128)(2,1)} %bitcast.273, ...), kind=kOutput, calls=%fused_computation.24 | convolution fusion | flops 5934413824 | bytes 31469568 | tf_op jit(solution)/shard_map/dot_general | solution.py:61
  585.9 9.6 convolution_bitcast_fusion.1
  595.5 10.4 fusion.36
  605.9 8.4 convolution_bitcast_fusion
  614.3 9.1 multiply_convert_fusion
  623.4 12.6 add_convert_fusion
  636.0 20.7 %copy.338 = bf16[2048,4096]{1,0:T(8,128)(2,1)} copy(bf16[2048,4096]{0,1:T(8,128)(2,1)} %bitcast.236) | data formatting | bytes 33554432 | tf_op jit(solution)/shard_map/dot_general | solution.py:67
  656.7 15.7 %fusion.64 = f32[16,256,2048]{2,1,0:T(8,128)} fusion(bf16[16,128,2048]{2,1,0:T(8,128)(2,1)} %bitcast.272, s32[16,256]{1,0:T(8,128)S(1)} %convolution_convert_fusion.11, pred[16,256]{1,0:T(8,128)(4,1)S(1)} %reshape.563), kind=kOutput, calls=%fused_computation.110 | convolution fusion | flops 2148532224 | bytes 41963520 | tf_op jit(solution)/shard_map/bst,bsd->btd/dot_general | solution.py:529
  672.4 15.7 %fusion.67 = f32[16,256,2048]{2,1,0:T(8,128)} fusion(bf16[16,128,2048]{2,1,0:T(8,128)(2,1)} %bitcast.271, s32[16,256]{1,0:T(8,128)S(1)} %convolution_convert_fusion.11, pred[16,256]{1,0:T(8,128)(4,1)S(1)} %reshape.563), kind=kOutput, calls=%fused_computation.111 | convolution fusion | flops 2148532224 | bytes 41963520 | tf_op jit(solution)/shard_map/bst,bsd->btd/dot_general | solution.py:529
  688.1 3.0 fusion.71
  691.2 8.0 convolution_bitcast_fusion.2
  700.7 11.1 fusion.128
  711.9 11.1 fusion.132
  723.1 5.8 multiply_convert_fusion.5
  728.9 13.1 fusion.130
  742.1 9.5 fusion.91
  751.6 9.5 fusion.92
  761.1 28.4 %fusion.1 = bf16[4096,2048]{1,0:T(8,128)(2,1)} fusion(f32[4096,2048]{1,0:T(8,128)} %fusion.130, f32[16,256,2048]{2,1,0:T(8,128)} %fusion.64, bf16[4096,88]{0,1:T(8,128)(2,1)S(1)} %get-tuple-element.132, bf16[11,8,16,128]{3,2,1,0:T(8,128)(2,1)S(1)} %bitcast.293), kind=kOutput, calls=%fused_computation.2 | convolution fusion | flops 1501560832 | bytes 84967424 | tf_op jit(solution)/shard_map/dot_general | solution.py:57
  789.5 14.2 %pad_maximum_fusion.p_ref = bf16[16,2,2,64,2176]{4,3,2,1,0:T(8,128)(2,1)} fusion(bf16[16,2,2,64,128]{4,3,2,1,0:T(8,128)(2,1)S(1)} %bitcast.307, bf16[16,2,2,64,2048]{4,3,2,1,0:T(8,128)(2,1)} %bitcast.248), kind=kLoop, calls=%fused_computation.5 | loop fusion | flops 35651584 | bytes 35651584 | tf_op jit(solution)/shard_map/concatenate | solution.py:563
  803.8 93.0 %shard_map.301 = bf16[2,2,64,2176]{3,2,1,0:T(8,128)(2,1)} custom-call(bf16[16,2,2,64,2176]{4,3,2,1,0:T(8,128)(2,1)} %pad_maximum_fusion.p_ref), custom_call_target="tpu_custom_call" | custom-call | tf_op jit(solution)/shard_map/pallas_call | solution.py:303
  899.9 19.0 %fusion.2 = bf16[4096,2048]{1,0:T(8,128)(2,1)} fusion(f32[16,256,2048]{2,1,0:T(8,128)} %fusion.67, bf16[4096,88]{0,1:T(8,128)(2,1)S(1)} %get-tuple-element.134, bf16[11,8,16,128]{3,2,1,0:T(8,128)(2,1)S(1)} %bitcast.306), kind=kOutput, calls=%fused_computation.4 | convolution fusion | flops 1493172224 | bytes 51412992 | tf_op jit(solution)/shard_map/dot_general | solution.py:57
  918.9 86.0 %shard_map.299 = bf16[2,2,64,2048]{3,2,1,0:T(8,128)(2,1)} custom-call(bf16[16,2,2,64,2048]{4,3,2,1,0:T(8,128)(2,1)} %bitcast.249), custom_call_target="tpu_custom_call" | custom-call | tf_op jit(solution)/shard_map/pallas_call | solution.py:303
  1011.5 3.1 multiply_reduce_fusion.1
  1017.6 3.5 fusion.86
  1021.4 7.6 fusion.21
  1029.0 7.8 multiply_reduce_fusion
  1036.8 5.8 multiply_convert_fusion.1
  1046.5 3.5 fusion.90
  1052.5 9.0 fusion.93
  1062.7 4.5 all-to-all-start.1
  1081.0 6.2 fusion.13
  1094.9 6.0 collective-permute-done.6
  1104.2 6.6 convolution_convert_fusion.6
  1110.8 3.3 reshape.578
  1116.2 3.3 convolution_convert_fusion.4
  1119.6 4.5 convolution_convert_fusion
  1126.5 4.2 fusion.56
  1135.2 4.4 copy.329
  1140.5 22.8 %concatenate.105.p_ref = bf16[16,1,2,64,3712]{4,3,2,1,0:T(8,128)(2,1)} concatenate(bf16[16,1,2,64,1536]{4,3,2,1,0:T(8,128)(2,1)} %bitcast.256, bf16[16,1,2,64,1024]{4,3,2,1,0:T(8,128)(2,1)} %bitcast.257, bf16[16,1,2,64,512]{4,3,2,1,0:T(8,128)(2,1)} %bitcast.279, bf16[16,1,2,64,576]{4,3,2,1,0:T(8,128)(2,1)} %bitcast.277, bf16[16,1,2,64,16]{4,3,2,1,0:T(8,128)(2,1)S(1)} %bitcast.298, ...), dimensions={4} | concatenate | bytes 30408704 | tf_op jit(solution)/shard_map/concatenate | solution.py:654
  1163.3 163.1 %shard_map.302 = bf16[1,2,64,3712]{3,2,1,0:T(8,128)(2,1)} custom-call(bf16[16,1,2,64,3712]{4,3,2,1,0:T(8,128)(2,1)} %concatenate.105.p_ref), custom_call_target="tpu_custom_call" | custom-call | tf_op jit(solution)/shard_map/pallas_call | solution.py:303
  (362 shorter events, 138.4 us)
Async XLA Ops:
  0.6 569.0 %copy-start = (bf16[1,704,2048]{2,1,0:T(8,128)(2,1)S(1)}, bf16[1,704,2048]{2,1,0:T(8,128)(2,1)}, u32[]{:S(2)}) copy-start(bf16[1,704,2048]{2,1,0:T(8,128)(2,1)} %param.35) | copy-start | bytes 8650756
  175.2 34.7 %copy-start.47 = (f32[2048]{0:T(1024)}, f32[2048]{0:T(1024)S(1)}, u32[]{:S(2)}) copy-start(f32[2048]{0:T(1024)S(1)} %get-tuple-element.113) | copy-start | bytes 24580
  175.2 8.1 copy-start.82
  183.9 21.5 %copy-start.71 = (f32[256]{0:T(256)}, f32[256]{0:T(256)S(1)}, u32[]{:S(2)}) copy-start(f32[256]{0:T(256)S(1)} %fusion.159) | copy-start | bytes 3076
  184.7 11.7 copy-start.56
  184.7 11.7 copy-start.58
  184.7 77.4 %copy-start.49 = (f32[256,32]{0,1:T(8,128)}, f32[256,32]{0,1:T(8,128)S(1)}, u32[]{:S(2)}) copy-start(f32[256,32]{0,1:T(8,128)S(1)} %get-tuple-element.155) | copy-start | bytes 98308
  185.6 207.3 %collective-permute-start.3 = (bf16[256,576]{0,1:T(8,128)(2,1)}, bf16[256,576]{0,1:T(8,128)(2,1)}, u32[]{:S(2)}, u32[]{:S(2)}) collective-permute-start(bf16[256,576]{0,1:T(8,128)(2,1)} %pad_maximum_fusion.3), channel_id=1, source_target_pairs={{0,2},{2,4},{4,6},{6,8},{8,10},{10,12},{12,14},{14,16},{16,18},{18... | collective-permute-start | bytes 884744 | tf_op jit(solution)/shard_map/ppermute | solution.py:26
  189.7 202.2 %collective-permute-start.2 = (bf16[256,576]{0,1:T(8,128)(2,1)}, bf16[256,576]{0,1:T(8,128)(2,1)}, u32[]{:S(2)}, u32[]{:S(2)}) collective-permute-start(bf16[256,576]{0,1:T(8,128)(2,1)} %pad_maximum_fusion.3), channel_id=1, source_target_pairs={{0,4},{2,6},{4,8},{6,10},{8,12},{10,14},{12,16},{14,18},{16,20},{1... | collective-permute-start | bytes 884744 | tf_op jit(solution)/shard_map/ppermute | solution.py:26
  192.2 198.7 %collective-permute-start.1 = (bf16[256,576]{0,1:T(8,128)(2,1)}, bf16[256,576]{0,1:T(8,128)(2,1)}, u32[]{:S(2)}, u32[]{:S(2)}) collective-permute-start(bf16[256,576]{0,1:T(8,128)(2,1)} %pad_maximum_fusion.3), channel_id=1, source_target_pairs={{0,6},{2,8},{4,10},{6,12},{8,14},{10,16},{12,18},{14,20},{16,22},{... | collective-permute-start | bytes 884744 | tf_op jit(solution)/shard_map/ppermute | solution.py:26
  196.4 193.4 %collective-permute-start = (bf16[256,576]{0,1:T(8,128)(2,1)}, bf16[256,576]{0,1:T(8,128)(2,1)}, u32[]{:S(2)}, u32[]{:S(2)}) collective-permute-start(bf16[256,576]{0,1:T(8,128)(2,1)} %pad_maximum_fusion.3), channel_id=1, source_target_pairs={{0,8},{2,10},{4,12},{6,14},{8,16},{10,18},{12,20},{14,22},{16,24},... | collective-permute-start | bytes 884744 | tf_op jit(solution)/shard_map/ppermute | solution.py:26
  203.1 6.8 copy-start.68
  205.4 493.8 %all-to-all-start = ((bf16[16,3,88,128]{3,2,1,0:T(8,128)(2,1)}), bf16[16,3,88,128]{3,2,1,0:T(8,128)(2,1)}, u32[]{:S(2)}, u32[]{:S(2)}) async-start(bf16[16,3,88,128]{3,2,1,0:T(8,128)(2,1)} %copy.312), calls=%async_computation | async-start | bytes 2162688 | tf_op jit(solution)/shard_map/all_to_all | solution.py:337
  209.9 7.2 copy-start.66
  209.9 50.3 %copy-start.70 = (s32[1,4096]{1,0:T(1,128)S(1)}, s32[1,4096]{1,0:T(1,128)}, u32[]{:S(2)}) copy-start(s32[1,4096]{1,0:T(1,128)} %param.20) | copy-start | bytes 49156
  209.9 52.2 %copy-start.51 = (f32[256,32]{0,1:T(8,128)S(1)}, f32[256,32]{0,1:T(8,128)}, u32[]{:S(2)}) copy-start(f32[256,32]{0,1:T(8,128)} %get-tuple-element.156) | copy-start | bytes 98308
  369.0 24.9 %copy-start.57 = (bf16[256,32]{0,1:T(8,128)(2,1)S(1)}, bf16[256,32]{0,1:T(8,128)(2,1)}, u32[]{:S(2)}) copy-start(bf16[256,32]{0,1:T(8,128)(2,1)} %copy-done.56) | copy-start | bytes 49156
  369.0 24.9 %copy-start.59 = (bf16[256,32]{0,1:T(8,128)(2,1)S(1)}, bf16[256,32]{0,1:T(8,128)(2,1)}, u32[]{:S(2)}) copy-start(bf16[256,32]{0,1:T(8,128)(2,1)} %copy-done.58) | copy-start | bytes 49156
  406.8 7.6 copy-start.40
  406.8 7.6 copy-start.42
  430.7 10.8 collective-permute-start.4
  431.2 10.4 copy-start.3
  553.6 8.0 copy-start.86
  585.9 9.6 copy-start.90
  595.5 10.4 copy-start.91
  605.9 8.4 copy-start.93
  614.3 9.1 copy-start.88
  614.3 9.1 copy-start.92
  656.7 34.4 %slice-start.7 = ((s8[8388608]{0:T(1024)(128)(4,1)}), s8[4194304]{0:T(1024)(128)(4,1)S(1)}, s32[]{:S(2)}) async-start(s8[8388608]{0:T(1024)(128)(4,1)} %bitcast.274), calls=%async_computation.9 | async-start | bytes 8388608
  672.4 15.7 %copy-start.55 = (f32[256,16]{0,1:T(8,128)S(1)}, f32[256,16]{0,1:T(8,128)}, u32[]{:S(2)}) copy-start(f32[256,16]{0,1:T(8,128)} %get-tuple-element.166) | copy-start | bytes 49156
  672.4 15.7 %copy-start.73 = (f32[256]{0:T(256)S(1)}, f32[256]{0:T(256)}, u32[]{:S(2)}) copy-start(f32[256]{0:T(256)} %get-tuple-element.165) | copy-start | bytes 3076
  672.4 15.7 %copy-start.89 = (pred[128]{0:T(512)(128)(4,1)S(1)}, pred[128]{0:T(512)(128)(4,1)}, u32[]{:S(2)}) copy-start(pred[128]{0:T(512)(128)(4,1)} %iota_compare_fusion.4) | copy-start | bytes 388
  672.4 18.8 %slice-start.8 = ((s8[8388608]{0:T(1024)(128)(4,1)}), s8[4194304]{0:T(1024)(128)(4,1)S(1)}, s32[]{:S(2)}) async-start(s8[8388608]{0:T(1024)(128)(4,1)} %bitcast.274), calls=%async_computation.10 | async-start | bytes 8388608
  672.4 18.8 %copy-start.94 = (bf16[2048,704]{0,1:T(8,128)(2,1)S(1)}, bf16[2048,704]{0,1:T(8,128)(2,1)}, u32[]{:S(2)}) copy-start(bf16[2048,704]{0,1:T(8,128)(2,1)} %get-tuple-element.123) | copy-start | bytes 8650756
  700.7 22.3 %slice-start.3 = ((s8[16777216]{0:T(1024)(128)(4,1)}), s8[4194304]{0:T(1024)(128)(4,1)S(1)}, s32[]{:S(2)}) async-start(s8[16777216]{0:T(1024)(128)(4,1)} %bitcast.243), calls=%async_computation.5 | async-start | bytes 8388608
  700.7 22.3 %slice-start.4 = ((s8[16777216]{0:T(1024)(128)(4,1)}), s8[4194304]{0:T(1024)(128)(4,1)S(1)}, s32[]{:S(2)}) async-start(s8[16777216]{0:T(1024)(128)(4,1)} %bitcast.243), calls=%async_computation.6 | async-start | bytes 8388608
  711.9 11.2 slice-start.5
  711.9 11.2 slice-start.6
  728.9 171.0 %copy-start.29 = (bf16[4096,88]{0,1:T(8,128)(2,1)}, bf16[4096,88]{0,1:T(8,128)(2,1)S(1)}, u32[]{:S(2)}) copy-start(bf16[4096,88]{0,1:T(8,128)(2,1)S(1)} %get-tuple-element.134) | copy-start | bytes 2162692
  761.1 28.4 %copy-start.44 = (bf16[16,256,128]{2,1,0:T(8,128)(2,1)S(1)}, bf16[16,256,128]{2,1,0:T(8,128)(2,1)}, u32[]{:S(2)}) copy-start(bf16[16,256,128]{2,1,0:T(8,128)(2,1)} %fusion.71) | copy-start | bytes 3145732
  898.1 20.8 %copy-start.17 = (f32[256,2176]{1,0:T(8,128)}, f32[256,2176]{1,0:T(8,128)S(1)}, u32[]{:S(2)}) copy-start(f32[256,2176]{1,0:T(8,128)S(1)} %bitcast_convert_fusion) | copy-start | bytes 6684676
  1021.4 7.7 copy-start.14
  1021.4 15.4 %slice-start = ((s8[10485760]{0:T(1024)(128)(4,1)}), s8[4194304]{0:T(1024)(128)(4,1)S(1)}, s32[]{:S(2)}) async-start(s8[10485760]{0:T(1024)(128)(4,1)} %bitcast.239), calls=%async_computation.2 | async-start | bytes 8388608
  1021.4 15.4 %slice-start.1 = ((s8[10485760]{0:T(1024)(128)(4,1)}), s8[4194304]{0:T(1024)(128)(4,1)S(1)}, s32[]{:S(2)}) async-start(s8[10485760]{0:T(1024)(128)(4,1)} %bitcast.239), calls=%async_computation.3 | async-start | bytes 8388608
  1029.0 7.8 slice-start.2
  1036.8 5.8 copy-start.10
  1052.4 9.0 copy-start.38
  1052.4 9.0 copy-start.39
  1061.5 5.8 copy-start.50
  1061.5 5.8 copy-start.52
  1061.6 6.8 copy-start.16
  1062.7 278.8 %all-to-all-start.1 = ((bf16[16,3,88,128]{3,2,1,0:T(8,128)(2,1)}), bf16[16,3,88,128]{3,2,1,0:T(8,128)(2,1)}, u32[]{:S(2)}, u32[]{:S(2)}) async-start(bf16[16,3,88,128]{3,2,1,0:T(8,128)(2,1)} %copy.340), calls=%async_computation.1 | async-start | bytes 2162688 | tf_op jit(solution)/shard_map/all_to_all | solution.py:337
  1073.7 7.2 copy-start.28
  1075.6 18.9 %collective-permute-start.5 = (bf16[256,576]{0,1:T(8,128)(2,1)}, bf16[256,576]{0,1:T(8,128)(2,1)S(1)}, u32[]{:S(2)}, u32[]{:S(2)}) collective-permute-start(bf16[256,576]{0,1:T(8,128)(2,1)} %get-tuple-element.144), channel_id=1, source_target_pairs={{8,0},{10,2},{12,4},{14,6},{16,8},{18,10},{20,12},{22,14},{24,16},... | collective-permute-start | bytes 884744 | tf_op jit(solution)/shard_map/ppermute | solution.py:26
  1076.9 17.9 %collective-permute-start.8 = (bf16[256,576]{0,1:T(8,128)(2,1)}, bf16[256,576]{0,1:T(8,128)(2,1)}, u32[]{:S(2)}, u32[]{:S(2)}) collective-permute-start(bf16[256,576]{0,1:T(8,128)(2,1)} %get-tuple-element.145), channel_id=1, source_target_pairs={{2,0},{4,2},{6,4},{8,6},{10,8},{12,10},{14,12},{16,14},{18,16},{20... | collective-permute-start | bytes 884744 | tf_op jit(solution)/shard_map/ppermute | solution.py:26
  1078.2 16.6 %collective-permute-start.7 = (bf16[256,576]{0,1:T(8,128)(2,1)}, bf16[256,576]{0,1:T(8,128)(2,1)}, u32[]{:S(2)}, u32[]{:S(2)}) collective-permute-start(bf16[256,576]{0,1:T(8,128)(2,1)} %get-tuple-element.146), channel_id=1, source_target_pairs={{4,0},{6,2},{8,4},{10,6},{12,8},{14,10},{16,12},{18,14},{20,16},{2... | collective-permute-start | bytes 884744 | tf_op jit(solution)/shard_map/ppermute | solution.py:26
  1079.5 21.3 %collective-permute-start.6 = (bf16[256,576]{0,1:T(8,128)(2,1)}, bf16[256,576]{0,1:T(8,128)(2,1)}, u32[]{:S(2)}, u32[]{:S(2)}) collective-permute-start(bf16[256,576]{0,1:T(8,128)(2,1)} %get-tuple-element.147), channel_id=1, source_target_pairs={{6,0},{8,2},{10,4},{12,6},{14,8},{16,10},{18,12},{20,14},{22,16},{... | collective-permute-start | bytes 884744 | tf_op jit(solution)/shard_map/ppermute | solution.py:26
  1081.0 6.2 copy-start.31
  1081.0 6.2 copy-start.27
  1081.0 7.8 copy-start.12
  1089.2 13.1 copy-start.19
  1103.5 20.5 %collective-permute-start.9 = (bf16[256,2624]{0,1:T(8,128)(2,1)}, bf16[256,2624]{0,1:T(8,128)(2,1)}, u32[]{:S(2)}, u32[]{:S(2)}) collective-permute-start(bf16[256,2624]{0,1:T(8,128)(2,1)} %fusion.70), channel_id=1, source_target_pairs={{0,1},{1,0},{2,3},{3,2},{4,5},{5,4},{6,7},{7,6},{8,9},{9,8},{10,11... | collective-permute-start | bytes 4030472 | tf_op jit(solution)/shard_map/ppermute | solution.py:313
  1332.0 5.5 slice-start.12
  1341.5 7.4 copy-start.1
  (56 other events, 163.9 us)

commit v2 on v1

--- a/solution.py
+++ b/solution.py
@@ -309,6 +309,366 @@
         )(p)
 
 
+def plane_at(z, k):
+    edge = jnp.where(z >= 2, 3 - z, z)
+    near = jnp.where(k == 0, edge, jnp.where(k == 1, 1 - edge, k))
+    return jnp.where(z >= 2, 3 - near, near)
+
+
+def nt(a, b):
+    return lax.dot_general(a, b, (((1,), (1,)), ((), ())), preferred_element_type=jnp.float32)
+
+
+def tn(a, b):
+    return lax.dot_general(a, b, (((0,), (0,)), ((), ())), preferred_element_type=jnp.float32)
+
+
+def mm(a, b):
+    return jnp.dot(a, b, preferred_element_type=jnp.float32)
+
+
+def gate_parts(a, b, dc):
+    s = 1.0 / (1.0 + jnp.exp(-a))
+    act = a * s
+    return act * b, dc * b * (s * (1.0 + a * (1.0 - s))), dc * act
+
+
+def moe_kernel(
+    moe, grd, pick, pick_t, wg, wu, wd, wr, sgu, sdn,
+    o_out, r_out, rg_out, act_out, da_out, db_out, sg_out, sibr, yr, xr, zr,
+    own, sib, stage, xb, gb, pk, pt, rr, rg, ly, ld, ry, rd, acts, das, dbs,
+    in_sem, out_sem, st_sem, cs, cr, xs, xrs, ys, yrs, zs, zrs, fs, fr,
+):
+    me = lax.axis_index("dp")
+    core = lax.axis_index("tensor")
+    other = 1 - core
+    z = me // 4
+    y = (me // 2) % 2
+    x = me % 2
+    xn = z * 4 + y * 2 + (1 - x)
+    yn = z * 4 + (1 - y) * 2 + x
+    up = jnp.minimum(z + 1, 3) * 4 + y * 2 + x
+    dn = jnp.maximum(z - 1, 0) * 4 + y * 2 + x
+    width = moe.shape[2]
+    hid = 128
+    cut = 512
+
+    def rc(src, dst, ss, rs, dev, c):
+        return pltpu.make_async_remote_copy(
+            src_ref=src, dst_ref=dst, send_sem=ss, recv_sem=rs, device_id=(dev, c), device_id_type=MESH
+        )
+
+    def loads(i):
+        k, half = i // 2, i % 2
+        b = plane_at(z, 3 - k) * 4 + jnp.where(half == 0, 1 - y, y) * 2
+        at = pl.ds(b, 2)
+        return [
+            pltpu.make_async_copy(moe.at[at], xb, in_sem.at[0]),
+            pltpu.make_async_copy(grd.at[at], gb, in_sem.at[1]),
+            pltpu.make_async_copy(pick.at[at], pk, in_sem.at[2]),
+            pltpu.make_async_copy(pick_t.at[at], pt, in_sem.at[3]),
+        ]
+
+    for c in loads(0):
+        c.start()
+    bar = pltpu.get_barrier_semaphore()
+
+    def sig(d, c):
+        pl.semaphore_signal(bar, inc=1, device_id=(d, c), device_id_type=MESH)
+
+    sig(xn, core)
+    sig(yn, core)
+    sig(me, other)
+    pl.when(z < 3)(lambda: sig(up, core))
+    pl.when(z > 0)(lambda: sig(dn, core))
+    pl.semaphore_wait(bar, 3 + (z < 3).astype(jnp.int32) + (z > 0).astype(jnp.int32))
+
+    for q in range(2):
+        ry[q, hid:] = sdn[...]
+        rd[q, hid:] = sgu[...]
+    sg_out[...] = jnp.zeros_like(sg_out)
+
+    def y_(j, b, half, zp):
+        return rc(own.at[b, half], yr.at[zp, j], ys.at[zp, j], yrs.at[zp, j], yn, core)
+
+    def x_(j, b, half, zp):
+        return rc(own.at[b, half], xr.at[zp, j], xs.at[zp, j], xrs.at[zp, j], xn, core)
+
+    def zc(zp, dev, d):
+        b = zp * 4 + y * 2 + x
+        return rc(own.at[b], zr.at[d, zp], zs.at[zp], zrs.at[d, zp], dev, core)
+
+    def sib_send(i):
+        return rc(sib, sibr.at[i], cs, cr.at[i], me, other)
+
+    def outs(i):
+        at = pl.ds(pl.multiple_of(i * 256, 256), 256)
+        return [
+            pltpu.make_async_copy(rr, r_out.at[at], out_sem.at[0]),
+            pltpu.make_async_copy(rg, rg_out.at[at], out_sem.at[1]),
+            pltpu.make_async_copy(acts, act_out.at[at], out_sem.at[2]),
+            pltpu.make_async_copy(das, da_out.at[at], out_sem.at[3]),
+            pltpu.make_async_copy(dbs, db_out.at[at], out_sem.at[4]),
+        ]
+
+    def columns(step):
+        def one(n, _):
+            step(pl.ds(pl.multiple_of(n * cut, cut), cut))
+            return 0
+
+        lax.fori_loop(0, width // cut, one, 0)
+
+    def first_part(i):
+        for c in loads(i):
+            c.wait()
+
+        @pl.when(i > 0)
+        def _():
+            for c in outs(i - 1):
+                c.wait()
+
+        def pick_rows(n):
+            for q in range(2):
+                rr[q * hid : (q + 1) * hid, n] = mm(pk[q], xb[q, :, n]).astype(jnp.bfloat16)
+                rg[q * hid : (q + 1) * hid, n] = mm(pk[q], gb[q, :, n]).astype(jnp.bfloat16)
+
+        columns(pick_rows)
+        for q in range(2):
+            ab = nt(xb[q], sgu[...])
+            act, d_a, d_b = gate_parts(ab[:, :hid], ab[:, hid:], nt(gb[q], sdn[...]))
+            ly[q, :, :hid] = pt[q]
+            ly[q, :, hid:] = act.astype(jnp.bfloat16)
+            ld[q, :, :hid] = pt[q]
+            ld[q, :, hid : 2 * hid] = d_a.astype(jnp.bfloat16)
+            ld[q, :, 2 * hid :] = d_b.astype(jnp.bfloat16)
+
+        def shared_grads(n):
+            sg_out[: 2 * hid, n] += tn(ld[0, :, hid:], xb[0, :, n]) + tn(ld[1, :, hid:], xb[1, :, n])
+            sg_out[2 * hid :, n] += tn(ly[0, :, hid:], gb[0, :, n]) + tn(ly[1, :, hid:], gb[1, :, n])
+
+        columns(shared_grads)
+
+        @pl.when(i < 7)
+        def _():
+            for c in loads(i + 1):
+                c.start()
+
+    def second_part(i):
+        logits = mm(rr[...], wr[...])
+        lane = lax.broadcasted_iota(jnp.int32, logits.shape, 1)
+        logits = jnp.where(lane < 16, logits, -jnp.inf)
+        e = jnp.exp(logits - jnp.max(logits, axis=1, keepdims=True))
+        gate = jnp.sum(jnp.where(lane == me, e, 0.0), axis=1, keepdims=True) / jnp.sum(
+            e, axis=1, keepdims=True
+        )
+        pre = nt(rg[...], wd[...])
+        act, d_a, d_b = gate_parts(mm(rr[...], wg[...]), mm(rr[...], wu[...]), gate * pre)
+        low = act.astype(jnp.bfloat16)
+        back = low.astype(jnp.float32)
+        d_gate = jnp.sum(back * pre, axis=1, keepdims=True)
+        acts[...] = (gate * back).astype(jnp.bfloat16)
+        das[...] = d_a.astype(jnp.bfloat16)
+        dbs[...] = d_b.astype(jnp.bfloat16)
+
+        def spread(n):
+            o = (gate * mm(low, wd[:, n])).astype(jnp.bfloat16)
+            s = (nt(das[...], wg[n]) + nt(dbs[...], wu[n])).astype(jnp.bfloat16)
+            for q in range(2):
+                ry[q, :hid, n] = o[q * hid : (q + 1) * hid]
+                rd[q, :hid, n] = s[q * hid : (q + 1) * hid]
+
+        columns(spread)
+        for c in outs(i):
+            c.start()
+        return jnp.where(lane == me, d_gate, 0.0).astype(jnp.bfloat16)
+
+    def third_part(i, d_cols):
+        k, half = i // 2, i % 2
+        b = plane_at(z, 3 - k) * 4 + jnp.where(half == 0, 1 - y, y) * 2
+
+        @pl.when(i > 0)
+        def _():
+            sib_send(i - 1).wait_send()
+
+        def store(q, n, v):
+            v = v.astype(jnp.bfloat16)
+            mine = jnp.where(core == 0, v[:128], v[128:])
+            theirs = jnp.where(core == 0, v[128:], v[:128])
+            own[b + q, 0, :, n] = mine[:64]
+            own[b + q, 1, :, n] = mine[64:]
+            sib[q, 0, :, n] = theirs[:64]
+            sib[q, 1, :, n] = theirs[64:]
+
+        def put(m, _):
+            n = pl.ds(pl.multiple_of(m * cut, cut), cut)
+            n2 = pl.ds(pl.multiple_of(width + m * cut, cut), cut)
+            for q in range(2):
+                store(q, n, mm(ly[q], ry[q, :, n]))
+                store(q, n2, mm(ld[q], rd[q, :, n]))
+            return 0
+
+        lax.fori_loop(0, width // cut, put, 0)
+        for q in range(2):
+            store(q, pl.ds(2 * width, 128), mm(pt_of(q), d_cols[q * hid : (q + 1) * hid]))
+        sib_send(i).start()
+
+    def pt_of(q):
+        return ly[q, :, :hid]
+
+    def staged(src, dst, sem):
+        return pltpu.make_async_copy(src, dst, sem)
+
+    def blk(zp, yy, xx):
+        return zp * 4 + yy * 2 + xx
+
+    def pair_sum(i):
+        k, half = i // 2, i % 2
+        zp = plane_at(z, 3 - k)
+        b = zp * 4 + jnp.where(half == 0, 1 - y, y) * 2
+        sib_send(i).wait_recv()
+        c = staged(sibr.at[i], stage, st_sem.at[0])
+        c.start()
+        c.wait()
+
+        def one(q, _):
+            add_into(own.at[b + q, 0], stage.at[q, 0])
+            add_into(own.at[b + q, 1], stage.at[q, 1])
+            return 0
+
+        lax.fori_loop(0, 2, one, 0)
+
+        @pl.when(half == 0)
+        def _():
+            y_(0, blk(zp, 1 - y, 1 - x), 0, zp).start()
+            x_(0, blk(zp, 1 - y, 1 - x), 1, zp).start()
+            y_(1, blk(zp, 1 - y, x), 0, zp).start()
+
+        @pl.when(half == 1)
+        def _():
+            x_(1, blk(zp, y, 1 - x), 1, zp).start()
+
+    def second_hop(k):
+        zp = plane_at(z, 3 - k)
+        mine = blk(zp, y, x)
+        y_(0, blk(zp, 1 - y, 1 - x), 0, zp).wait_recv()
+        c0 = staged(yr.at[zp, 0], stage.at[0, 0], st_sem.at[0])
+        c0.start()
+        x_(0, blk(zp, 1 - y, 1 - x), 1, zp).wait_recv()
+        c1 = staged(xr.at[zp, 0], stage.at[0, 1], st_sem.at[1])
+        c1.start()
+        c0.wait()
+        add_into(own.at[blk(zp, y, 1 - x), 0], stage.at[0, 0])
+        x_(2, blk(zp, y, 1 - x), 0, zp).start()
+        c1.wait()
+        add_into(own.at[blk(zp, 1 - y, x), 1], stage.at[0, 1])
+        y_(2, blk(zp, 1 - y, x), 1, zp).start()
+        y_(1, blk(zp, 1 - y, x), 0, zp).wait_recv()
+        c2 = staged(yr.at[zp, 1], stage.at[1, 0], st_sem.at[2])
+        c2.start()
+        x_(1, blk(zp, y, 1 - x), 1, zp).wait_recv()
+        c3 = staged(xr.at[zp, 1], stage.at[1, 1], st_sem.at[3])
+        c3.start()
+        c2.wait()
+        add_into(own.at[mine, 0], stage.at[1, 0])
+        c3.wait()
+        add_into(own.at[mine, 1], stage.at[1, 1])
+
+    def last_hop(k):
+        zp = plane_at(z, 3 - k)
+        mine = blk(zp, y, x)
+        x_(2, blk(zp, y, 1 - x), 0, zp).wait_recv()
+        c0 = staged(xr.at[zp, 2], stage.at[0, 0], st_sem.at[0])
+        c0.start()
+        y_(2, blk(zp, 1 - y, x), 1, zp).wait_recv()
+        c1 = staged(yr.at[zp, 2], stage.at[0, 1], st_sem.at[1])
+        c1.start()
+        c0.wait()
+        add_into(own.at[mine, 0], stage.at[0, 0])
+        c1.wait()
+        add_into(own.at[mine, 1], stage.at[0, 1])
+
+        def arrived(d):
+            zc(zp, me, d).wait_recv()
+            c = staged(zr.at[d, zp], stage.at[1], st_sem.at[2])
+            c.start()
+            c.wait()
+            add_into(own.at[mine, 0], stage.at[1, 0])
+            add_into(own.at[mine, 1], stage.at[1, 1])
+
+        pl.when((zp <= z) & (z < 3))(lambda: arrived(1))
+        pl.when((zp >= z) & (z > 0))(lambda: arrived(0))
+        pl.when(zp < z)(lambda: zc(zp, dn, 1).start())
+        pl.when(zp > z)(lambda: zc(zp, up, 0).start())
+
+    def step(i, _):
+        pl.when(i < 8)(lambda: first_part(i))
+        pl.when((i >= 1) & (i <= 8))(lambda: pair_sum(i - 1))
+        pl.when((i % 2 == 0) & (i >= 4) & (i <= 10))(lambda: second_hop((i - 4) // 2))
+        pl.when((i % 2 == 1) & (i >= 7) & (i <= 13))(lambda: last_hop((i - 7) // 2))
+
+        @pl.when(i < 8)
+        def _():
+            third_part(i, second_part(i))
+
+        return 0
+
+    lax.fori_loop(0, 14, step, 0)
+    for a in range(2):
+
+        def row(n, _):
+            r = pl.ds(pl.multiple_of(n * 16, 16), 16)
+            o_out[core, a, r] = own[me, a, r]
+            return 0
+
+        lax.fori_loop(0, 4, row, 0)
+    f = rc(o_out.at[core], o_out.at[core], fs, fr, me, other)
+    f.start()
+    for c in outs(7):
+        c.wait()
+    sib_send(7).wait_send()
+    for k in range(4):
+        for j in range(3):
+            x_(j, 0, 0, k).wait_send()
+            y_(j, 0, 0, k).wait_send()
+
+        @pl.when(k != z)
+        def _():
+            zc(k, up, 0).wait_send()
+
+    rc(o_out.at[core], o_out.at[other], fs, fr, me, other).wait_recv()
+    f.wait_send()
+
+
+def moe_call(moe, grd, pick, pick_t, wg, wu, wd, wr, sgu, sdn, cid):
+    width, ffe = wg.shape
+    total = 2 * width + 128
+    slots = pick.shape[0] * pick.shape[1]
+    low, S, V = jnp.bfloat16, pltpu.SemaphoreType.DMA, pltpu.VMEM
+    any_, vmem = pl.BlockSpec(memory_space=pl.ANY), pl.BlockSpec(memory_space=pltpu.VMEM)
+    shape = lambda *s: jax.ShapeDtypeStruct(s, low)
+    blk = (2, 64, total)
+    return pl.pallas_call(
+        moe_kernel,
+        out_shape=[
+            shape(2, *blk), shape(slots, width), shape(slots, width), shape(slots, ffe), shape(slots, ffe),
+            shape(slots, ffe), jax.ShapeDtypeStruct((384, width), jnp.float32),
+            shape(8, 2, *blk), shape(4, 3, 64, total), shape(4, 3, 64, total), shape(2, 4, *blk),
+        ],
+        in_specs=[any_] * 4 + [vmem] * 6,
+        out_specs=[vmem] + [any_] * 5 + [vmem] + [any_] * 4,
+        scratch_shapes=[
+            V((16,) + blk, low), V((2,) + blk, low), V((2,) + blk, low),
+            V((2, 256, width), low), V((2, 256, width), low), V((2, 128, 256), low), V((2, 256, 128), low),
+            V((256, width), low), V((256, width), low), V((2, 256, 256), low), V((2, 256, 384), low),
+            V((2, 256, width), low), V((2, 384, width), low),
+            V((256, ffe), low), V((256, ffe), low), V((256, ffe), low),
+            S((4,)), S((5,)), S((4,)), S, S((8,)), S((4, 3)), S((4, 3)), S((4, 3)), S((4, 3)), S((4,)), S((2, 4)), S, S,
+        ],
+        compiler_params=pltpu.CompilerParams(collective_id=cid, has_side_effects=True, vmem_limit_bytes=60 << 20),
+        cost_estimate=pl.CostEstimate(flops=65 * 10**9, bytes_accessed=80 * 10**6, transcendentals=0),
+    )(moe, grd, pick, pick_t, wg, wu, wd, wr, sgu, sdn)
+
+
 def swapped(v):
     return lax.ppermute(v, "tensor", [(0, 1), (1, 0)])
 
@@ -331,6 +691,29 @@
 def scatter_rows(v, cid):
     rows, width = v.shape[0] // 32, v.shape[1]
     return rs16(v.reshape(16, 2, 2, rows // 2, width), True, cid).reshape(2 * rows, width)
+
+
+def gather_background(v):
+    rows, width = v.shape[0] // 2, v.shape[1]
+    moved = lax.all_gather(my_half(v, rows), "dp", axis=0)
+    theirs = swapped(moved)
+    core = lax.axis_index("tensor")
+    pair = jnp.stack([jnp.where(core == 0, moved, theirs), jnp.where(core == 0, theirs, moved)], 1)
+    return pair.reshape(-1, width)
+
+
+def scatter_background(v):
+    rows, width = v.shape[0] // 32, v.shape[1]
+    core = lax.axis_index("tensor")
+    cut = v.reshape(16, 2, rows, width)
+    keep = lax.dynamic_index_in_dim(cut, core, 1, keepdims=False)
+    give = lax.dynamic_index_in_dim(cut, 1 - core, 1, keepdims=False)
+    pair = (keep.astype(jnp.float32) + swapped(give).astype(jnp.float32)).astype(jnp.bfloat16)
+    mine = lax.psum_scatter(pair.reshape(16 * rows, width), "dp", scatter_dimension=0, tiled=True)
+    theirs = swapped(mine)
+    return jnp.where(
+        core == 0, jnp.concatenate([mine, theirs]), jnp.concatenate([theirs, mine])
+    ).astype(jnp.float32)
 
 
 def exchange(parts):
@@ -375,7 +758,8 @@
     kv_cuts = depth // kv_rows
     kv_part = kv_width // kv_cuts
     lat_width = w_latent.shape[1]
-    small = (lat_width + experts + 3 + 127) // 128 * 128
+    route_width = n_rows * TOPK // depth
+    small = (lat_width + experts + 3 + route_width + 127) // 128 * 128
 
     shared_part = shared_gate.shape[1] // dp_count
     shared_send = jnp.stack(
@@ -387,8 +771,8 @@
         1,
     )
     shared_all = exchange(shared_send).transpose(1, 2, 0, 3).reshape(3, shared_part, width)
-    sg_t, su_t, sd = shared_all[0], shared_all[1], shared_all[2]
-    all_routes = lax.all_gather(routes, "dp", axis=0, tiled=True)
+    lead = jnp.pad(shared_all, ((0, 0), (0, 128 - shared_part), (0, 0)))
+    shared_in, shared_out = lead[:2].reshape(256, width), lead[2]
 
     gains = jnp.stack(
         [attn_gain, moe_gain, jnp.pad(latent_gain, (0, depth - kv_rows))], 1
@@ -401,7 +785,8 @@
             w_latent,
             w_router,
             gains,
-            jnp.zeros((depth, small - lat_width - experts - 3), jnp.bfloat16),
+            routes.reshape(depth, route_width).astype(jnp.bfloat16),
+            jnp.zeros((depth, small - lat_width - experts - 3 - route_width), jnp.bfloat16),
         ],
         1,
     )
@@ -429,7 +814,10 @@
         weights[:, at + 2].reshape(dp_count, depth)[:, :kv_rows].reshape(-1).astype(jnp.float32)
     )
 
-    grad_all = gather_rows(out_grad, 2)
+    all_routes = (
+        weights[:, at + 3 : at + 3 + route_width].reshape(total, TOPK).astype(jnp.int32)
+    )
+    grad_all = gather_background(out_grad)
 
     local_heads = q_width // (NOPE + ROPE)
     positions = (row_start + jnp.arange(n_rows, dtype=jnp.int32)).astype(jnp.float32)
@@ -513,68 +901,34 @@
         & chosen[:, None, :]
     ).astype(jnp.bfloat16)
 
-    def picked(v):
-        return (
-            jnp.einsum(
-                "bst,btd->bsd",
-                pick,
-                v.reshape(dp_count, n_rows, width),
-                preferred_element_type=jnp.float32,
-            )
-            .astype(jnp.bfloat16)
-            .reshape(dp_count * capacity, width)
-        )
-
-    def put_back(v):
-        return jnp.einsum(
-            "bst,bsd->btd",
-            pick,
-            v.reshape(dp_count, capacity, v.shape[1]),
-            preferred_element_type=jnp.float32,
-        ).reshape(total, v.shape[1])
-
-    w_gate, w_up, w_down = expert_gate[0], routed_up_weight[0], expert_down[0]
-    rows_in = picked(moe_all)
-    rows_grad = picked(grad_all)
-    row_router = jax.nn.softmax(matmul(rows_in, wr_full), axis=-1)
-    row_gate = lax.dynamic_slice_in_dim(row_router, dp_index, 1, 1)
-    exp_act, exp_act_back = jax.vjp(gated_act, matmul(rows_in, w_gate), matmul(rows_in, w_up))
-    act_low = exp_act.astype(jnp.bfloat16)
-    exp_out = (row_gate * matmul(act_low, w_down)).astype(jnp.bfloat16)
-    shared_act, shared_back = jax.vjp(
-        gated_act, matmul_nt(moe_all, sg_t), matmul_nt(moe_all, su_t)
-    )
-    shared_low = shared_act.astype(jnp.bfloat16)
-    out_part = (put_back(exp_out) + matmul(shared_low, sd)).astype(jnp.bfloat16)
-    result = (middle + scatter_rows(out_part, 4).astype(jnp.float32)).astype(jnp.bfloat16)
-
-    d_pre = matmul_nt(rows_grad, w_down)
-    row_d_gate = jnp.sum(act_low.astype(jnp.float32) * d_pre, axis=1, keepdims=True)
-    d_ea, d_eb = exp_act_back(row_gate * d_pre)
-    d_ea_low, d_eb_low = d_ea.astype(jnp.bfloat16), d_eb.astype(jnp.bfloat16)
-    d_slots = matmul_nt(d_ea_low, w_gate) + matmul_nt(d_eb_low, w_up)
-    d_sa, d_sb = shared_back(matmul_nt(grad_all, sd))
-    d_sa_low, d_sb_low = d_sa.astype(jnp.bfloat16), d_sb.astype(jnp.bfloat16)
-    lane = jnp.arange(128, dtype=jnp.int32)[None, :]
-    d_gate_cols = put_back(
-        jnp.where(lane == dp_index, row_d_gate, 0.0).astype(jnp.bfloat16)
-    )
-    d_part = put_back(d_slots.astype(jnp.bfloat16)) + matmul(d_sa_low, sg_t) + matmul(d_sb_low, su_t)
-    d_home = scatter_rows(jnp.concatenate([d_part, d_gate_cols], 1).astype(jnp.bfloat16), 5).astype(
-        jnp.float32
-    )
-    scaled_act = (row_gate * act_low.astype(jnp.float32)).astype(jnp.bfloat16)
+    slot_rows = dp_count * capacity
+    moe_wr = jnp.pad(wr_full, ((0, 0), (0, 128 - experts)))
+    home, rows_in, rows_grad, scaled_act, d_ea_low, d_eb_low, shared_grads = moe_call(
+        moe_all.reshape(dp_count, n_rows, width),
+        grad_all.reshape(dp_count, n_rows, width),
+        pick,
+        pick.transpose(0, 2, 1),
+        expert_gate[0],
+        routed_up_weight[0],
+        expert_down[0],
+        moe_wr,
+        shared_in,
+        shared_out,
+        4,
+    )[:7]
+    home = home.reshape(n_rows, 2 * width + 128)
+    result = (middle + home[:, :width].astype(jnp.float32)).astype(jnp.bfloat16)
+    d_home = home[:, width:].astype(jnp.float32)
     grad_down = matmul_tn(scaled_act, rows_grad)[None]
     grad_gate = matmul_tn(rows_in, d_ea_low)[None]
     grad_up = matmul_tn(rows_in, d_eb_low)[None]
-    shared_grads = jnp.stack(
-        [matmul_tn(d_sa_low, moe_all), matmul_tn(d_sb_low, moe_all), matmul_tn(shared_low, grad_all)]
-    ).astype(jnp.bfloat16)
-    home = exchange(
-        shared_grads.reshape(3, shared_part, dp_count, depth).transpose(2, 0, 1, 3)
+    shared_home = exchange(
+        shared_grads.astype(jnp.bfloat16)
+        .reshape(3, 128, dp_count, depth)[:, :shared_part]
+        .transpose(2, 0, 1, 3)
     ).astype(jnp.float32)
-    home = home.transpose(1, 0, 2, 3).reshape(3, dp_count * shared_part, depth)
-    grad_sgate, grad_sup, grad_sdown = home[0].T, home[1].T, home[2]
+    shared_home = shared_home.transpose(1, 0, 2, 3).reshape(3, dp_count * shared_part, depth)
+    grad_sgate, grad_sup, grad_sdown = shared_home[0].T, shared_home[1].T, shared_home[2]
 
     grad_y = out_grad.astype(jnp.float32)
     d_gate_all = d_home[:, width : width + experts]
@@ -1083,7 +1437,12 @@
         P("dp", None, "tensor"),
         P("dp", "tensor", None),
     )
-    body = shards_sixteen if mesh.shape["dp"] == 16 and mesh.shape["tensor"] == 2 else shards_general
+    sixteen = mesh.shape["dp"] == 16 and mesh.shape["tensor"] == 2
+
+    def body(*args):
+        fits_sixteen = sixteen and args[2].shape[0] == 1 and args[15].shape[0] == 1
+        return (shards_sixteen if fits_sixteen else shards_general)(*args)
+
     return jax.shard_map(
         body,
         mesh=mesh,

time: 1360 us -> 1040 us (0.76)
  matrix products: 361 us -> 113 us
  blocking collectives: 43 us -> 0 us
  local copies, waits for them, and re-layouts: 163 us -> 139 us
    pallas_call x0 -> x1, Pallas kernels: none -> 236 us  [moe_call(): pl.pallas_call(moe_kernel, out_shape=[shape(2, *blk), shape(slots, width)...]
    pallas_call x3 -> x1, Pallas kernels: 342 us -> 139 us  [rs16(): pl.pallas_call(functools.partial(rs_kernel, share), out_shape=jax.ShapeDt...]
    dot_general x13 -> x6, matrix products: 110 us -> 18 us  [matmul(): return jnp.dot(left_mat, right_mat, preferred_element_type=jnp.float32)]
    dot_general x11 -> x5, matrix products: 87.4 us -> 22.3 us  [matmul_nt(): lax.dot_general(left_mat, right_mat, (((1,), (1,)), ((), ())), preferred_...]
    dot_general x5 -> x0, matrix products: 51.7 us -> none  [the longest x3 34.4 us: put_back(): jnp.einsum('bst,bsd->btd', pick, v.reshape(dp_count, capacity, v.shape[1]...]
    pallas_call x3 -> x2, Pallas kernels: 347 us -> 302 us  [ag16(): pl.pallas_call(functools.partial(ag_kernel, share), out_shape=jax.ShapeDt...]
    all_gather x1 -> x0, blocking collectives: 43 us -> none  [shards_sixteen(): all_routes = lax.all_gather(routes, 'dp', axis=0, tiled=True)]
    dot_general x2 -> x0, local copies, waits for them, and re-layouts: 41.5 us -> none  [matmul_tn(): lax.dot_general(left_mat, right_mat, (((0,), (0,)), ((), ())), preferred_...]
  transfers between devices with their start and end apart: 12 -> 14, of which waited for: 3 -> 0; matrix products, arithmetic and copies ran while one was open for 26% -> 19% of each run, Pallas kernels for 26% -> 43%
where the time goes in v2:
time: 1040 us; the launch traced here: 1030 us
  Pallas kernels  677 us (65%)
  local copies, waits for them, and re-layouts  139 us (13%)
  matrix products  113 us (11%)
  other arithmetic  51.1 us (5%)
  starting transfers between devices  36.5 us (4%)
  between operations  15.5 us (1%)
    pallas_call x2, Pallas kernels, ag16(): pl.pallas_call(functools.partial(ag_kernel, share), out_shape=jax.ShapeDt...  302 us
    pallas_call x1, Pallas kernels, moe_call(): pl.pallas_call(moe_kernel, out_shape=[shape(2, *blk), shape(slots, width)...  236 us
    pallas_call x1, Pallas kernels, rs16(): pl.pallas_call(functools.partial(rs_kernel, share), out_shape=jax.ShapeDt...  139 us
    unnamed x173, local copies, waits for them, and re-layouts  57 us
    dot_general x8, matrix products, matmul_tn(): lax.dot_general(left_mat, right_mat, (((0,), (0,)), ((), ())), preferred_...  43 us
    concatenate x1, local copies, waits for them, and re-layouts, shards_sixteen(): jnp.concatenate([grad_wq.astype(jnp.bfloat16), grad_wo_t.astype(jnp.bfloa...  23 us
    dot_general x5, matrix products, matmul_nt(): lax.dot_general(left_mat, right_mat, (((1,), (1,)), ((), ())), preferred_...  22.3 us
  transfers between devices with their start and end apart: 14, of which 0 were waited for; matrix products, arithmetic and copies ran while one was open for 19% of the time, Pallas kernels for 43%

profile of v2, /device:TPU:0, one launch (start us, length us, event | category | flops | bytes accessed | tf_op | source)
XLA Modules:
  0.0 1032.8 jit_solution(11634442617456203615)
XLA Ops:
  7.3 1.9 constant_dynamic-slice_fusion
  14.6 209.1 %shard_map.297 = bf16[16,1,2,64,3712]{4,3,2,1,0:T(8,128)(2,1)} custom-call(bf16[2,64,3712]{2,1,0:T(8,128)(2,1)} %concatenate.78.x_ref), custom_call_target="tpu_custom_call" | custom-call | tf_op jit(solution)/shard_map/pallas_call | solution.py:165
  226.3 2.5 convert_reduce_fusion
  229.1 3.2 fusion.28
  234.1 3.0 collective-permute-start
  237.1 3.9 collective-permute-start.1
  241.0 5.3 collective-permute-start.2
  246.3 2.7 collective-permute-start.3
  250.7 4.6 all-to-all-start
  255.4 2.1 convert_compare_fusion
  257.5 5.7 fusion.6
  267.1 2.0 slice.219
  269.2 2.3 copy.259
  273.2 2.0 copy.304
  277.8 4.6 copy.252
  282.4 4.6 copy.253
  291.9 3.6 convolution_convert_fusion.1
  295.5 4.6 copy.305
  300.1 4.2 fusion.101
  304.3 4.8 copy.293
  309.2 7.4 fusion.32
  316.6 5.5 fusion.104
  323.8 2.7 copy-done
  326.5 2.7 fusion.56
  329.3 3.7 fusion.105
  335.1 2.5 fusion.43.pick_t
  339.5 2.0 copy.250
  341.5 93.3 %shard_map.298 = bf16[16,2,2,64,2048]{4,3,2,1,0:T(8,128)(2,1)} custom-call(bf16[2,64,2048]{2,1,0:T(8,128)(2,1)} %bitcast.195), custom_call_target="tpu_custom_call" | custom-call | tf_op jit(solution)/shard_map/pallas_call | solution.py:165
  439.8 6.5 select_bitcast_fusion.1
  446.3 6.9 pad_maximum_fusion
  453.2 236.0 %shard_map.299 = (bf16[2,2,64,4224]{3,2,1,0:T(8,128)(2,1)}, bf16[2048,2048]{1,0:T(8,128)(2,1)}, bf16[2048,2048]{1,0:T(8,128)(2,1)}, bf16[2048,704]{1,0:T(8,128)(...) custom-call(bf16[16,256,2048]{2,1,0:T(8,128)(2,1)} %bitcast.168, ...), custom_call_target="tpu_custom_call" | custom-call | flops 65000001536 | bytes 80000000 | tf_op jit(solution)/shard_map/pallas_call | solution.py:650
  689.2 2.3 slice.221
  691.6 2.3 copy.296
  695.7 3.3 multiply_reduce_fusion.1
  699.1 2.4 slice.220
  701.5 2.3 copy.295
  703.8 3.5 fusion.36
  708.6 3.7 fusion.53
  713.3 6.5 multiply_reduce_fusion
  720.5 2.5 multiply_convert_fusion
  724.8 1.8 fusion.48
  729.1 2.2 fusion.12
  732.9 4.4 fusion.107
  737.3 4.5 convolution_convert_fusion.4
  742.1 6.1 fusion.4
  748.2 4.5 convolution_convert_fusion
  752.7 8.3 convolution_bitcast_fusion.1
  761.0 8.2 convolution_bitcast_fusion.2
  770.2 1.9 fusion.19
  778.3 3.5 reshape.497
  781.8 2.0 copy.268
  785.6 2.3 copy.280
  787.9 2.1 convert_bitcast_fusion.1
  791.9 11.2 %all-to-all-start.1 = ((bf16[16,3,88,128]{3,2,1,0:T(8,128)(2,1)}), bf16[16,3,88,128]{3,2,1,0:T(8,128)(2,1)}, u32[]{:S(2)}, u32[]{:S(2)}) async-start(bf16[16,3,88,128]{3,2,1,0:T(8,128)(2,1)} %bitcast.185), calls=%async_computation.1 | async-start | bytes 2162688 | tf_op jit(solution)/shard_map/all_to_all | solution.py:720
  803.2 4.5 convolution_convert_fusion.2
  811.5 10.2 convolution_bitcast_fusion
  823.3 2.3 convolution_convert_fusion.3
  825.6 4.9 fusion.35
  830.5 4.4 copy.269
  839.5 23.0 %concatenate.91.p_ref = bf16[16,1,2,64,3712]{4,3,2,1,0:T(8,128)(2,1)} concatenate(bf16[16,1,2,64,1536]{4,3,2,1,0:T(8,128)(2,1)} %bitcast.152, bf16[16,1,2,64,1024]{4,3,2,1,0:T(8,128)(2,1)} %bitcast.153, bf16[16,1,2,64,512]{4,3,2,1,0:T(8,128)(2,1)} %bitcast.173, bf16[16,1,2,64,576]{4,3,2,1,0:T(8,128)(2,1)} %bitcast.170, bf16[16,1,2,64,16]{4,3,2,1,0:T(8,128)(2,1)} %bitcast.194, ...), dimensions={4} | concatenate | bytes 30408704 | tf_op jit(solution)/shard_map/concatenate | solution.py:1008
  862.5 139.0 %shard_map.300 = bf16[1,2,64,3712]{3,2,1,0:T(8,128)(2,1)} custom-call(bf16[16,1,2,64,3712]{4,3,2,1,0:T(8,128)(2,1)} %concatenate.91.p_ref), custom_call_target="tpu_custom_call" | custom-call | tf_op jit(solution)/shard_map/pallas_call | solution.py:303
  1005.6 2.0 copy.298
  1011.7 3.5 fusion.37
  1015.2 2.9 copy.281
  (281 shorter events, 82.6 us)
Async XLA Ops:
  7.2 5.2 copy-start.46
  7.2 5.4 copy-start.64
  7.2 5.7 copy-start.59
  7.2 5.8 copy-start.62
  7.2 6.0 copy-start.63
  7.2 6.3 copy-start.29
  7.2 292.9 %all-gather.3.cloned.1.call-start = ((), (), s32[]{:S(2)}) async-start(), calls=%async_computation.2 | async-start | bytes 8912896 | tf_op jit(solution)/shard_map/all_gather | solution.py:698
  14.6 209.1 %copy-start.26 = (bf16[256,2048]{1,0:T(8,128)(2,1)S(1)}, bf16[256,2048]{1,0:T(8,128)(2,1)}, u32[]{:S(2)}) copy-start(bf16[256,2048]{1,0:T(8,128)(2,1)} %param.18) | copy-start | bytes 3145732
  224.3 113.3 %copy-start.1 = (bf16[256,2048]{0,1:T(8,128)(2,1)}, bf16[256,2048]{0,1:T(8,128)(2,1)S(1)}, u32[]{:S(2)}) copy-start(bf16[256,2048]{0,1:T(8,128)(2,1)S(1)} %copy.234) | copy-start | bytes 3145732
  226.2 6.6 copy-start.44
  226.2 6.3 copy-start.60
  226.2 6.3 copy-start.57
  228.8 28.7 %copy-start.33 = (f32[2048]{0:T(1024)}, f32[2048]{0:T(1024)S(1)}, u32[]{:S(2)}) copy-start(f32[2048]{0:T(1024)S(1)} %get-tuple-element.111) | copy-start | bytes 24580
  229.1 28.4 %copy-start.48 = (f32[256]{0:T(256)}, f32[256]{0:T(256)S(1)}, u32[]{:S(2)}) copy-start(f32[256]{0:T(256)S(1)} %fusion.86) | copy-start | bytes 3076
  229.1 19.8 %copy-start.30 = (bf16[128,1408]{1,0:T(8,128)(2,1)S(1)}, bf16[128,1408]{1,0:T(8,128)(2,1)}, u32[]{:S(2)}) copy-start(bf16[128,1408]{1,0:T(8,128)(2,1)} %param.30) | copy-start | bytes 1081348
  232.4 16.8 %copy-start.31 = (bf16[128,1408]{1,0:T(8,128)(2,1)S(1)}, bf16[128,1408]{1,0:T(8,128)(2,1)}, u32[]{:S(2)}) copy-start(bf16[128,1408]{1,0:T(8,128)(2,1)} %param.31) | copy-start | bytes 1081348
  232.4 17.0 %copy-start.32 = (bf16[1408,128]{1,0:T(8,128)(2,1)S(1)}, bf16[1408,128]{1,0:T(8,128)(2,1)}, u32[]{:S(2)}) copy-start(bf16[1408,128]{1,0:T(8,128)(2,1)} %param.32) | copy-start | bytes 1081348
  232.5 13.8 %copy-start.55 = (f32[256]{0:T(256)}, f32[256]{0:T(256)S(1)}, u32[]{:S(2)}) copy-start(f32[256]{0:T(256)S(1)} %multiply_reduce_fusion.6) | copy-start | bytes 3076
  232.5 16.9 %copy-start.51 = (f32[256]{0:T(256)}, f32[256]{0:T(256)S(1)}, u32[]{:S(2)}) copy-start(f32[256]{0:T(256)S(1)} %fusion.87) | copy-start | bytes 3076
  233.2 17.5 %copy-start.41 = (bf16[256,32]{0,1:T(8,128)(2,1)}, bf16[256,32]{0,1:T(8,128)(2,1)S(1)}, u32[]{:S(2)}) copy-start(bf16[256,32]{0,1:T(8,128)(2,1)S(1)} %get-tuple-element.146) | copy-start | bytes 49156
  233.2 31.4 %copy-start.35 = (f32[256,32]{0,1:T(8,128)}, f32[256,32]{0,1:T(8,128)S(1)}, u32[]{:S(2)}) copy-start(f32[256,32]{0,1:T(8,128)S(1)} %get-tuple-element.143) | copy-start | bytes 98308
  233.2 31.4 %copy-start.37 = (f32[256,32]{0,1:T(8,128)}, f32[256,32]{0,1:T(8,128)S(1)}, u32[]{:S(2)}) copy-start(f32[256,32]{0,1:T(8,128)S(1)} %get-tuple-element.144) | copy-start | bytes 98308
  234.1 52.9 %collective-permute-start = (bf16[256,576]{0,1:T(8,128)(2,1)}, bf16[256,576]{0,1:T(8,128)(2,1)}, u32[]{:S(2)}, u32[]{:S(2)}) collective-permute-start(bf16[256,576]{0,1:T(8,128)(2,1)} %pad_maximum_fusion.3), channel_id=1, source_target_pairs={{0,8},{2,10},{4,12},{6,14},{8,16},{10,18},{12,20},{14,22},{16,24},... | collective-permute-start | bytes 884744 | tf_op jit(solution)/shard_map/ppermute | solution.py:26
  237.1 51.0 %collective-permute-start.1 = (bf16[256,576]{0,1:T(8,128)(2,1)}, bf16[256,576]{0,1:T(8,128)(2,1)}, u32[]{:S(2)}, u32[]{:S(2)}) collective-permute-start(bf16[256,576]{0,1:T(8,128)(2,1)} %pad_maximum_fusion.3), channel_id=1, source_target_pairs={{0,6},{2,8},{4,10},{6,12},{8,14},{10,16},{12,18},{14,20},{16,22},{... | collective-permute-start | bytes 884744 | tf_op jit(solution)/shard_map/ppermute | solution.py:26
  241.0 48.1 %collective-permute-start.2 = (bf16[256,576]{0,1:T(8,128)(2,1)}, bf16[256,576]{0,1:T(8,128)(2,1)}, u32[]{:S(2)}, u32[]{:S(2)}) collective-permute-start(bf16[256,576]{0,1:T(8,128)(2,1)} %pad_maximum_fusion.3), channel_id=1, source_target_pairs={{0,4},{2,6},{4,8},{6,10},{8,12},{10,14},{12,16},{14,18},{16,20},{1... | collective-permute-start | bytes 884744 | tf_op jit(solution)/shard_map/ppermute | solution.py:26
  246.3 43.8 %collective-permute-start.3 = (bf16[256,576]{0,1:T(8,128)(2,1)}, bf16[256,576]{0,1:T(8,128)(2,1)}, u32[]{:S(2)}, u32[]{:S(2)}) collective-permute-start(bf16[256,576]{0,1:T(8,128)(2,1)} %pad_maximum_fusion.3), channel_id=1, source_target_pairs={{0,2},{2,4},{4,6},{6,8},{8,10},{10,12},{12,14},{14,16},{16,18},{18... | collective-permute-start | bytes 884744 | tf_op jit(solution)/shard_map/ppermute | solution.py:26
  249.6 5.7 copy-start.50
  250.7 185.8 %all-to-all-start = ((bf16[16,3,88,128]{3,2,1,0:T(8,128)(2,1)}), bf16[16,3,88,128]{3,2,1,0:T(8,128)(2,1)}, u32[]{:S(2)}, u32[]{:S(2)}) async-start(bf16[16,3,88,128]{3,2,1,0:T(8,128)(2,1)} %copy.256), calls=%async_computation | async-start | bytes 2162688 | tf_op jit(solution)/shard_map/all_to_all | solution.py:720
  265.3 51.2 %copy-start.22 = (bf16[256,8,32]{0,2,1:T(8,128)(2,1)}, bf16[256,8,32]{0,2,1:T(8,128)(2,1)S(1)}, u32[]{:S(2)}) copy-start(bf16[256,8,32]{0,2,1:T(8,128)(2,1)S(1)} %get-tuple-element.133) | copy-start | bytes 393220
  273.2 3.7 copy-start.20
  287.0 4.9 copy-start.18
  300.1 139.7 %collective-permute-start.5 = (bf16[16,128,2048]{2,1,0:T(8,128)(2,1)}, bf16[16,128,2048]{2,1,0:T(8,128)(2,1)}, u32[]{:S(2)}, u32[]{:S(2)}) collective-permute-start(bf16[16,128,2048]{2,1,0:T(8,128)(2,1)} %bitcast.171), channel_id=1, source_target_pairs={{0,1},{1,0},{2,3},{3,2},{4,5},{5,4},{6,7},{7,6},{8,9},{9,8},{10,11... | collective-permute-start | bytes 25165832 | tf_op jit(solution)/shard_map/ppermute | solution.py:673
  304.3 4.8 copy-start.15
  309.2 7.4 copy-start.21
  309.2 7.4 copy-start.24
  322.1 4.4 copy-start
  322.1 4.4 copy-start.6
  329.2 3.7 copy-start.28
  329.2 4.3 copy-start.47
  329.2 4.3 copy-start.43
  333.0 4.6 collective-permute-start.4
  699.1 4.7 copy-start.17
  708.6 4.7 copy-start.7
  713.3 6.5 slice-start
  713.3 6.6 slice-start.1
  713.3 7.2 slice-start.2
  737.3 4.5 copy-start.36
  737.3 4.5 copy-start.38
  742.0 10.7 %slice-start.3 = ((s8[8388608]{0:T(1024)(128)(4,1)}), s8[4194304]{0:T(1024)(128)(4,1)S(1)}, s32[]{:S(2)}) async-start(s8[8388608]{0:T(1024)(128)(4,1)} %bitcast.220), calls=%async_computation.6 | async-start | bytes 8388608
  742.1 6.1 copy-start.2
  742.1 6.1 copy-start.34
  742.1 6.1 copy-start.49
  742.1 10.6 %slice-start.4 = ((s8[8388608]{0:T(1024)(128)(4,1)}), s8[4194304]{0:T(1024)(128)(4,1)S(1)}, s32[]{:S(2)}) async-start(s8[8388608]{0:T(1024)(128)(4,1)} %bitcast.220), calls=%async_computation.7 | async-start | bytes 8388608
  748.2 4.5 copy-start.67
  752.7 8.3 copy-start.66
  773.2 34.5 %collective-permute-start.6 = (bf16[256,576]{0,1:T(8,128)(2,1)}, bf16[256,576]{0,1:T(8,128)(2,1)}, u32[]{:S(2)}, u32[]{:S(2)}) collective-permute-start(bf16[256,576]{0,1:T(8,128)(2,1)} %get-tuple-element.135), channel_id=1, source_target_pairs={{8,0},{10,2},{12,4},{14,6},{16,8},{18,10},{20,12},{22,14},{24,16},... | collective-permute-start | bytes 884744 | tf_op jit(solution)/shard_map/ppermute | solution.py:26
  774.4 33.2 %collective-permute-start.7 = (bf16[256,576]{0,1:T(8,128)(2,1)}, bf16[256,576]{0,1:T(8,128)(2,1)}, u32[]{:S(2)}, u32[]{:S(2)}) collective-permute-start(bf16[256,576]{0,1:T(8,128)(2,1)} %get-tuple-element.138), channel_id=1, source_target_pairs={{6,0},{8,2},{10,4},{12,6},{14,8},{16,10},{18,12},{20,14},{22,16},{... | collective-permute-start | bytes 884744 | tf_op jit(solution)/shard_map/ppermute | solution.py:26
  775.7 31.9 %collective-permute-start.8 = (bf16[256,576]{0,1:T(8,128)(2,1)}, bf16[256,576]{0,1:T(8,128)(2,1)}, u32[]{:S(2)}, u32[]{:S(2)}) collective-permute-start(bf16[256,576]{0,1:T(8,128)(2,1)} %get-tuple-element.137), channel_id=1, source_target_pairs={{4,0},{6,2},{8,4},{10,6},{12,8},{14,10},{16,12},{18,14},{20,16},{2... | collective-permute-start | bytes 884744 | tf_op jit(solution)/shard_map/ppermute | solution.py:26
  777.0 30.6 %collective-permute-start.9 = (bf16[256,576]{0,1:T(8,128)(2,1)}, bf16[256,576]{0,1:T(8,128)(2,1)}, u32[]{:S(2)}, u32[]{:S(2)}) collective-permute-start(bf16[256,576]{0,1:T(8,128)(2,1)} %get-tuple-element.136), channel_id=1, source_target_pairs={{2,0},{4,2},{6,4},{8,6},{10,8},{12,10},{14,12},{16,14},{18,16},{20... | collective-permute-start | bytes 884744 | tf_op jit(solution)/shard_map/ppermute | solution.py:26
  790.7 12.5 %copy-start.4 = (f32[256,2048]{0,1:T(8,128)S(1)}, f32[256,2048]{0,1:T(8,128)}, u32[]{:S(2)}) copy-start(f32[256,2048]{0,1:T(8,128)} %copy-done.3) | copy-start | bytes 6291460
  791.9 229.2 %all-to-all-start.1 = ((bf16[16,3,88,128]{3,2,1,0:T(8,128)(2,1)}), bf16[16,3,88,128]{3,2,1,0:T(8,128)(2,1)}, u32[]{:S(2)}, u32[]{:S(2)}) async-start(bf16[16,3,88,128]{3,2,1,0:T(8,128)(2,1)} %bitcast.185), calls=%async_computation.1 | async-start | bytes 2162688 | tf_op jit(solution)/shard_map/all_to_all | solution.py:720
  803.2 4.5 copy-start.8
  809.7 12.0 %collective-permute-start.10 = (bf16[256,2624]{0,1:T(8,128)(2,1)S(1)}, bf16[256,2624]{0,1:T(8,128)(2,1)S(1)}, u32[]{:S(2)}, u32[]{:S(2)}) collective-permute-start(bf16[256,2624]{0,1:T(8,128)(2,1)S(1)} %fusion.44), channel_id=1, source_target_pairs={{0,1},{1,0},{2,3},{3,2},{4,5},{5,4},{6,7},{7,6},{8,9},{9,8},{10,11... | collective-permute-start | bytes 4030472 | tf_op jit(solution)/shard_map/ppermute | solution.py:673
  1004.5 6.6 copy-start.54
  (23 other events, 37.5 us)
Sparse Core Ops, SparseCore 0:
  11.4 166.6 all-gather.2

commit v3 on v0

--- a/solution.py
+++ b/solution.py
@@ -1,8 +1,11 @@
+import functools
 import math
 
 import jax
 import jax.numpy as jnp
 from jax import lax
+from jax.experimental import pallas as pl
+from jax.experimental.pallas import tpu as pltpu
 from jax.sharding import PartitionSpec as P
 
 NOPE = 128
@@ -66,7 +69,1283 @@
     )
 
 
-def shards(
+def ranks_before(hot):
+    count = hot.shape[0]
+    below = jnp.arange(count)[:, None] > jnp.arange(count)[None, :]
+    return matmul(below.astype(jnp.bfloat16), hot.astype(jnp.bfloat16)).astype(jnp.int32)
+
+
+MESH = pl.DeviceIdType.MESH
+
+
+def plane_at(z, k):
+    edge = jnp.where(z >= 2, 3 - z, z)
+    near = jnp.where(k == 0, edge, jnp.where(k == 1, 1 - edge, k))
+    return jnp.where(z >= 2, 3 - near, near)
+
+
+def ag_kernel(kinds, cuts, *refs):
+    n = len(kinds)
+    ins, outs, lands, sems = refs[:n], refs[n : 2 * n], refs[2 * n : 3 * n], refs[3 * n :]
+    me = lax.axis_index("dp")
+    core = lax.axis_index("tensor")
+    z = me // 4
+    y = (me // 2) % 2
+    x = me % 2
+    xn = z * 4 + y * 2 + (1 - x)
+    yn = z * 4 + (1 - y) * 2 + x
+    up = jnp.minimum(z + 1, 3) * 4 + y * 2 + x
+    dn = jnp.maximum(z - 1, 0) * 4 + y * 2 + x
+    bar = pltpu.get_barrier_semaphore()
+
+    def sig(d, c):
+        pl.semaphore_signal(bar, inc=1, device_id=(d, c), device_id_type=MESH)
+
+    sig(xn, core)
+    sig(yn, core)
+    sig(me, 1 - core)
+    pl.when(z < 3)(lambda: sig(up, core))
+    pl.when(z > 0)(lambda: sig(dn, core))
+
+    def rc(src, dst, ss, rs, dev, c):
+        return pltpu.make_async_remote_copy(
+            src_ref=src, dst_ref=dst, send_sem=ss, recv_sem=rs, device_id=(dev, c), device_id_type=MESH
+        )
+
+    class Part:
+        def __init__(self, at, cut):
+            self.share = kinds[at]
+            self.x, self.o, self.hbm = ins[at], lands[at], outs[at]
+            rows = self.x.shape[1] // cuts[at]
+            self.rows = pl.ds(cut * rows, rows)
+            self.zs, self.zr, self.xs, self.xr, self.ys, self.yr, self.cs, self.cr, self.own, self.out = (
+                s.at[cut] for s in sems[10 * at : 10 * at + 10]
+            )
+            self.slot = core if self.share else 0
+            self.copy = pltpu.make_async_copy(self.x.at[:, self.rows], self.whole(me), self.own)
+
+        def whole(self, b):
+            return self.o.at[b, self.slot, :, self.rows]
+
+        def z_(self, zp, dev, s):
+            b = zp * 4 + y * 2 + x
+            return rc(self.whole(b), self.whole(b), self.zs.at[s], self.zr.at[zp], dev, core)
+
+        def x_(self, j, b, half, zp):
+            r = self.o.at[b, self.slot, half, self.rows]
+            return rc(r, r, self.xs.at[zp, j], self.xr.at[zp, j], xn, core)
+
+        def y_(self, j, b, half, zp):
+            r = self.o.at[b, self.slot, half, self.rows]
+            return rc(r, r, self.ys.at[zp, j], self.yr.at[zp, j], yn, core)
+
+        def twin(self, b):
+            return rc(self.whole(b), self.whole(b), self.cs.at[b], self.cr.at[b], me, 1 - core)
+
+        def first(self, k):
+            zp = plane_at(z, k)
+            b = zp * 4 + y * 2 + x
+            if k > 0:
+                self.z_(zp, up, 0).wait_recv()
+            pl.when((zp <= z) & (z < 3))(lambda: self.z_(zp, up, zp).start())
+            pl.when((zp >= z) & (z > 0))(lambda: self.z_(zp, dn, 4 + zp).start())
+            self.x_(0, b, 0, zp).start()
+            self.y_(0, b, 1, zp).start()
+            self.y_(1, b, 0, zp).start()
+            self.x_(1, b, 1, zp).start()
+            if self.share:
+                self.twin(b).start()
+
+        def second(self, k):
+            zp = plane_at(z, k)
+            bx = zp * 4 + y * 2 + (1 - x)
+            by = zp * 4 + (1 - y) * 2 + x
+            self.x_(0, bx, 0, zp).wait_recv()
+            self.y_(2, bx, 0, zp).start()
+            self.y_(0, by, 1, zp).wait_recv()
+            self.x_(2, by, 1, zp).start()
+            self.x_(1, bx, 1, zp).wait_recv()
+            self.y_(1, by, 0, zp).wait_recv()
+            if self.share:
+                self.twin(bx).start()
+                self.twin(by).start()
+
+        def third(self, k):
+            zp = plane_at(z, k)
+            bd = zp * 4 + (1 - y) * 2 + (1 - x)
+            self.y_(2, bd, 0, zp).wait_recv()
+            self.x_(2, bd, 1, zp).wait_recv()
+            if self.share:
+                self.twin(bd).start()
+
+        def save(self, k):
+            at = pl.ds(plane_at(z, k) * 4, 4)
+            return pltpu.make_async_copy(
+                self.o.at[at, :, :, self.rows], self.hbm.at[at, :, :, self.rows], self.out.at[k]
+            )
+
+        def fourth(self, k):
+            if self.share:
+                for q in range(4):
+                    b = plane_at(z, k) * 4 + q
+                    src, dst = self.o.at[b, core, :, self.rows], self.o.at[b, 1 - core, :, self.rows]
+                    rc(src, dst, self.cs.at[b], self.cr.at[b], me, 1 - core).wait_recv()
+            self.save(k).start()
+
+        def end(self):
+            for k in range(4):
+                self.save(k).wait()
+                pl.when((k <= z) & (z < 3))(lambda k=k: self.z_(k, up, k).wait_send())
+                pl.when((k >= z) & (z > 0))(lambda k=k: self.z_(k, dn, 4 + k).wait_send())
+                for j in range(3):
+                    self.x_(j, 0, 0, k).wait_send()
+                    self.y_(j, 0, 0, k).wait_send()
+            if self.share:
+                for b in range(16):
+                    self.twin(b).wait_send()
+
+    groups = [[Part(at, cut) for cut in range(cuts[at])] for at in range(n)]
+    parts = [p for g in groups for p in g]
+    for p in parts:
+        p.copy.start()
+    pl.semaphore_wait(bar, 3 + (z < 3).astype(jnp.int32) + (z > 0).astype(jnp.int32))
+    for p in parts:
+        p.copy.wait()
+    turns = [(p, k) for g in groups for k in range(4) for p in g]
+    lag = max(cuts)
+    for t in range(len(turns) + lag):
+        if t < len(turns):
+            turns[t][0].first(turns[t][1])
+        if t >= lag:
+            turns[t - lag][0].second(turns[t - lag][1])
+    for p, k in turns:
+        p.third(k)
+        if not p.share:
+            p.fourth(k)
+    for p, k in turns:
+        if p.share:
+            p.fourth(k)
+    for p in parts:
+        p.end()
+
+
+def ag16(arrays, kinds, cid, cuts=None):
+    S = pltpu.SemaphoreType.DMA
+    any_ = pl.BlockSpec(memory_space=pl.ANY)
+    cuts = cuts or (1,) * len(arrays)
+    counts = ((8,), (4,), (4, 3), (4, 3), (4, 3), (4, 3), (16,), (16,), (), (4,))
+    shapes = [(16, 2 if share else 1) + v.shape for v, share in zip(arrays, kinds)]
+    return pl.pallas_call(
+        functools.partial(ag_kernel, kinds, cuts),
+        out_shape=[jax.ShapeDtypeStruct(s, v.dtype) for s, v in zip(shapes, arrays)],
+        in_specs=[any_] * len(arrays),
+        out_specs=[any_] * len(arrays),
+        scratch_shapes=[pltpu.VMEM(s, v.dtype) for s, v in zip(shapes, arrays)]
+        + [S((c,) + s) for c in cuts for s in counts],
+        compiler_params=pltpu.CompilerParams(collective_id=cid, has_side_effects=True, vmem_limit_bytes=60 << 20),
+    )(*arrays)
+
+
+def add_into(dst, src):
+    def step(i, _):
+        r = pl.ds(pl.multiple_of(i * 16, 16), 16)
+        dst[r] = dst[r] + src[r]
+        return 0
+
+    lax.fori_loop(0, dst.shape[0] // 16, step, 0)
+
+
+def rs_kernel(a_ref, b_ref, o_ref, own, yr, xr, zr, lsem, xs, xrs, ys, yrs, zs, zrs):
+    me = lax.axis_index("dp")
+    core = lax.axis_index("tensor")
+    z = me // 4
+    y = (me // 2) % 2
+    x = me % 2
+    xn = z * 4 + y * 2 + (1 - x)
+    yn = z * 4 + (1 - y) * 2 + x
+    up = jnp.minimum(z + 1, 3) * 4 + y * 2 + x
+    dn = jnp.maximum(z - 1, 0) * 4 + y * 2 + x
+    wide = a_ref.shape[3]
+
+    def rc(src, dst, ss, rs, dev):
+        return pltpu.make_async_remote_copy(
+            src_ref=src, dst_ref=dst, send_sem=ss, recv_sem=rs, device_id=(dev, core), device_id_type=MESH
+        )
+
+    def loads(zp):
+        at = pl.ds(zp * 4, 4)
+        return [
+            pltpu.make_async_copy(a_ref.at[at], own.at[at, :, :, 0:wide], lsem.at[zp, 0]),
+            pltpu.make_async_copy(b_ref.at[at], own.at[at, :, :, wide:], lsem.at[zp, 1]),
+        ]
+
+    for k in range(4):
+        for c in loads(plane_at(z, 3 - k)):
+            c.start()
+    bar = pltpu.get_barrier_semaphore()
+
+    def sig(d):
+        pl.semaphore_signal(bar, inc=1, device_id=(d, core), device_id_type=MESH)
+
+    sig(xn)
+    sig(yn)
+    pl.when(z < 3)(lambda: sig(up))
+    pl.when(z > 0)(lambda: sig(dn))
+    pl.semaphore_wait(bar, 2 + (z < 3).astype(jnp.int32) + (z > 0).astype(jnp.int32))
+
+    def y_(j, b, half, zp):
+        return rc(own.at[b, half], yr.at[zp, j], ys.at[zp, j], yrs.at[zp, j], yn)
+
+    def x_(j, b, half, zp):
+        return rc(own.at[b, half], xr.at[zp, j], xs.at[zp, j], xrs.at[zp, j], xn)
+
+    def zc(zp, dev, d):
+        return rc(own.at[zp * 4 + y * 2 + x], zr.at[d, zp], zs.at[zp], zrs.at[d, zp], dev)
+
+    def blk(zp, yy, xx):
+        return zp * 4 + yy * 2 + xx
+
+    def s1(k):
+        zp = plane_at(z, 3 - k)
+        for c in loads(zp):
+            c.wait()
+        y_(0, blk(zp, 1 - y, 1 - x), 0, zp).start()
+        x_(0, blk(zp, 1 - y, 1 - x), 1, zp).start()
+        y_(1, blk(zp, 1 - y, x), 0, zp).start()
+        x_(1, blk(zp, y, 1 - x), 1, zp).start()
+
+    def s2(k):
+        zp = plane_at(z, 3 - k)
+        mine = blk(zp, y, x)
+        y_(0, blk(zp, 1 - y, 1 - x), 0, zp).wait_recv()
+        add_into(own.at[blk(zp, y, 1 - x), 0], yr.at[zp, 0])
+        x_(2, blk(zp, y, 1 - x), 0, zp).start()
+        x_(0, blk(zp, 1 - y, 1 - x), 1, zp).wait_recv()
+        add_into(own.at[blk(zp, 1 - y, x), 1], xr.at[zp, 0])
+        y_(2, blk(zp, 1 - y, x), 1, zp).start()
+        y_(1, blk(zp, 1 - y, x), 0, zp).wait_recv()
+        add_into(own.at[mine, 0], yr.at[zp, 1])
+        x_(1, blk(zp, y, 1 - x), 1, zp).wait_recv()
+        add_into(own.at[mine, 1], xr.at[zp, 1])
+
+    def s3(k):
+        zp = plane_at(z, 3 - k)
+        mine = blk(zp, y, x)
+        x_(2, blk(zp, y, 1 - x), 0, zp).wait_recv()
+        add_into(own.at[mine, 0], xr.at[zp, 2])
+        y_(2, blk(zp, 1 - y, x), 1, zp).wait_recv()
+        add_into(own.at[mine, 1], yr.at[zp, 2])
+
+        def arrived(d):
+            zc(zp, me, d).wait_recv()
+            add_into(own.at[mine, 0], zr.at[d, zp, 0])
+            add_into(own.at[mine, 1], zr.at[d, zp, 1])
+
+        pl.when((zp <= z) & (z < 3))(lambda: arrived(1))
+        pl.when((zp >= z) & (z > 0))(lambda: arrived(0))
+        pl.when(zp < z)(lambda: zc(zp, dn, 1).start())
+        pl.when(zp > z)(lambda: zc(zp, up, 0).start())
+
+    s1(0)
+    s1(1)
+    s2(0)
+    s1(2)
+    s2(1)
+    s3(0)
+    s1(3)
+    s2(2)
+    s3(1)
+    s2(3)
+    s3(2)
+    s3(3)
+    for a in range(2):
+
+        def row(i, _):
+            r = pl.ds(pl.multiple_of(i * 16, 16), 16)
+            o_ref[a, r] = own[me, a, r].astype(jnp.float32)
+            return 0
+
+        lax.fori_loop(0, o_ref.shape[1] // 16, row, 0)
+    for k in range(4):
+        for j in range(3):
+            x_(j, 0, 0, k).wait_send()
+            y_(j, 0, 0, k).wait_send()
+
+        @pl.when(k != z)
+        def _():
+            zc(k, up, 0).wait_send()
+
+
+def rs16(a, b, cid):
+    S = pltpu.SemaphoreType.DMA
+    half = (a.shape[2], a.shape[3] + b.shape[3])
+    blkshape = (2,) + half
+    V = lambda s: pltpu.VMEM(s, a.dtype)
+    return pl.pallas_call(
+        rs_kernel,
+        out_shape=jax.ShapeDtypeStruct(blkshape, jnp.float32),
+        in_specs=[pl.BlockSpec(memory_space=pl.ANY)] * 2,
+        out_specs=pl.BlockSpec(memory_space=pltpu.VMEM),
+        scratch_shapes=[
+            V((16,) + blkshape), V((4, 3) + half), V((4, 3) + half), V((2, 4) + blkshape),
+            S((4, 2)), S((4, 3)), S((4, 3)), S((4, 3)), S((4, 3)), S((4,)), S((2, 4)),
+        ],
+        compiler_params=pltpu.CompilerParams(collective_id=cid, has_side_effects=True, vmem_limit_bytes=60 << 20),
+    )(a, b)
+
+
+def nt(a, b):
+    return lax.dot_general(a, b, (((1,), (1,)), ((), ())), preferred_element_type=jnp.float32)
+
+
+def tn(a, b):
+    return lax.dot_general(a, b, (((0,), (0,)), ((), ())), preferred_element_type=jnp.float32)
+
+
+def mm(a, b):
+    return jnp.dot(a, b, preferred_element_type=jnp.float32)
+
+
+def gate_parts(a, b, dc):
+    s = 1.0 / (1.0 + jnp.exp(-a))
+    act = a * s
+    return act * b, dc * b * (s * (1.0 + a * (1.0 - s))), dc * act
+
+
+def moe_kernel(
+    moe, grd, pick, pick_t, wg, wu, wd, wr, sgu, sdn,
+    o_out, r_out, rg_out, act_out, da_out, db_out, sg_out, yr, xr, zr,
+    own, sib, sibr, stage, xb, gb, pk, pt, rr, rg, ly, ld, ry, rd, acts, das, dbs, dgs,
+    in_sem, out_sem, st_sem, free, cs, cr, xs, xrs, ys, yrs, zs, zrs, fs, fr,
+):
+    me = lax.axis_index("dp")
+    core = lax.axis_index("tensor")
+    other = 1 - core
+    z = me // 4
+    y = (me // 2) % 2
+    x = me % 2
+    xn = z * 4 + y * 2 + (1 - x)
+    yn = z * 4 + (1 - y) * 2 + x
+    up = jnp.minimum(z + 1, 3) * 4 + y * 2 + x
+    dn = jnp.maximum(z - 1, 0) * 4 + y * 2 + x
+    width = moe.shape[2]
+    hid = 128
+    cut = 512
+
+    def rc(src, dst, ss, rs, dev, c):
+        return pltpu.make_async_remote_copy(
+            src_ref=src, dst_ref=dst, send_sem=ss, recv_sem=rs, device_id=(dev, c), device_id_type=MESH
+        )
+
+    def loads(i):
+        k, half = i // 2, i % 2
+        b = plane_at(z, 3 - k) * 4 + jnp.where(half == 0, 1 - y, y) * 2
+        at = pl.ds(b, 2)
+        return [
+            pltpu.make_async_copy(moe.at[at], xb, in_sem.at[0]),
+            pltpu.make_async_copy(grd.at[at], gb, in_sem.at[1]),
+            pltpu.make_async_copy(pick.at[at], pk, in_sem.at[2]),
+            pltpu.make_async_copy(pick_t.at[at], pt, in_sem.at[3]),
+        ]
+
+    for c in loads(0):
+        c.start()
+    bar = pltpu.get_barrier_semaphore()
+
+    def sig(d, c):
+        pl.semaphore_signal(bar, inc=1, device_id=(d, c), device_id_type=MESH)
+
+    sig(xn, core)
+    sig(yn, core)
+    sig(me, other)
+    pl.when(z < 3)(lambda: sig(up, core))
+    pl.when(z > 0)(lambda: sig(dn, core))
+    pl.semaphore_wait(bar, 3 + (z < 3).astype(jnp.int32) + (z > 0).astype(jnp.int32))
+
+    for q in range(2):
+        ry[q, hid:] = sdn[...]
+        rd[q, hid:] = sgu[...]
+    sg_out[...] = jnp.zeros_like(sg_out)
+
+    def y_(j, b, half, zp):
+        return rc(own.at[b, half], yr.at[zp, j], ys.at[zp, j], yrs.at[zp, j], yn, core)
+
+    def x_(j, b, half, zp):
+        return rc(own.at[b, half], xr.at[zp, j], xs.at[zp, j], xrs.at[zp, j], xn, core)
+
+    def zc(zp, dev, d):
+        b = zp * 4 + y * 2 + x
+        return rc(own.at[b], zr.at[d, zp], zs.at[zp], zrs.at[d, zp], dev, core)
+
+    def sib_send(i):
+        return rc(sib, sibr, cs, cr, me, other)
+
+    def outs(i):
+        at = pl.ds(pl.multiple_of(i * 256, 256), 256)
+        return [
+            pltpu.make_async_copy(rr, r_out.at[at], out_sem.at[0]),
+            pltpu.make_async_copy(rg, rg_out.at[at], out_sem.at[1]),
+            pltpu.make_async_copy(acts, act_out.at[at], out_sem.at[2]),
+            pltpu.make_async_copy(das, da_out.at[at], out_sem.at[3]),
+            pltpu.make_async_copy(dbs, db_out.at[at], out_sem.at[4]),
+        ]
+
+    def columns(step):
+        def one(n, _):
+            step(pl.ds(pl.multiple_of(n * cut, cut), cut))
+            return 0
+
+        lax.fori_loop(0, width // cut, one, 0)
+
+    def first_part(i):
+        for c in loads(i):
+            c.wait()
+
+        @pl.when(i > 0)
+        def _():
+            for c in outs(i - 1):
+                c.wait()
+
+        def pick_rows(n):
+            for q in range(2):
+                rr[q * hid : (q + 1) * hid, n] = mm(pk[q], xb[q, :, n]).astype(jnp.bfloat16)
+                rg[q * hid : (q + 1) * hid, n] = mm(pk[q], gb[q, :, n]).astype(jnp.bfloat16)
+
+        columns(pick_rows)
+        for q in range(2):
+            ab = nt(xb[q], sgu[...])
+            act, d_a, d_b = gate_parts(ab[:, :hid], ab[:, hid:], nt(gb[q], sdn[...]))
+            ly[q, :, :hid] = pt[q]
+            ly[q, :, hid:] = act.astype(jnp.bfloat16)
+            ld[q, :, :hid] = pt[q]
+            ld[q, :, hid : 2 * hid] = d_a.astype(jnp.bfloat16)
+            ld[q, :, 2 * hid :] = d_b.astype(jnp.bfloat16)
+
+        def shared_grads(n):
+            sg_out[: 2 * hid, n] += tn(ld[0, :, hid:], xb[0, :, n]) + tn(ld[1, :, hid:], xb[1, :, n])
+            sg_out[2 * hid :, n] += tn(ly[0, :, hid:], gb[0, :, n]) + tn(ly[1, :, hid:], gb[1, :, n])
+
+        columns(shared_grads)
+
+        @pl.when(i < 7)
+        def _():
+            for c in loads(i + 1):
+                c.start()
+
+    def second_part(i):
+        logits = mm(rr[...], wr[...])
+        lane = lax.broadcasted_iota(jnp.int32, logits.shape, 1)
+        logits = jnp.where(lane < 16, logits, -jnp.inf)
+        e = jnp.exp(logits - jnp.max(logits, axis=1, keepdims=True))
+        gate = jnp.sum(jnp.where(lane == me, e, 0.0), axis=1, keepdims=True) / jnp.sum(
+            e, axis=1, keepdims=True
+        )
+        pre = nt(rg[...], wd[...])
+        act, d_a, d_b = gate_parts(mm(rr[...], wg[...]), mm(rr[...], wu[...]), gate * pre)
+        low = act.astype(jnp.bfloat16)
+        back = low.astype(jnp.float32)
+        d_gate = jnp.sum(back * pre, axis=1, keepdims=True)
+        acts[...] = (gate * back).astype(jnp.bfloat16)
+        das[...] = d_a.astype(jnp.bfloat16)
+        dbs[...] = d_b.astype(jnp.bfloat16)
+
+        def spread(n):
+            o = (gate * mm(low, wd[:, n])).astype(jnp.bfloat16)
+            s = (nt(das[...], wg[n]) + nt(dbs[...], wu[n])).astype(jnp.bfloat16)
+            for q in range(2):
+                ry[q, :hid, n] = o[q * hid : (q + 1) * hid]
+                rd[q, :hid, n] = s[q * hid : (q + 1) * hid]
+
+        columns(spread)
+        for c in outs(i):
+            c.start()
+        dgs[...] = jnp.where(lane == me, d_gate, 0.0).astype(jnp.bfloat16)
+
+    def third_part(i):
+        k, half = i // 2, i % 2
+        b = plane_at(z, 3 - k) * 4 + jnp.where(half == 0, 1 - y, y) * 2
+
+        @pl.when(i > 0)
+        def _():
+            sib_send(i - 1).wait_send()
+
+        def store(q, n, v):
+            v = v.astype(jnp.bfloat16)
+            mine = jnp.where(core == 0, v[:128], v[128:])
+            theirs = jnp.where(core == 0, v[128:], v[:128])
+            own[b + q, 0, :, n] = mine[:64]
+            own[b + q, 1, :, n] = mine[64:]
+            sib[q, 0, :, n] = theirs[:64]
+            sib[q, 1, :, n] = theirs[64:]
+
+        def put(m, _):
+            n = pl.ds(pl.multiple_of(m * cut, cut), cut)
+            n2 = pl.ds(pl.multiple_of(width + m * cut, cut), cut)
+            for q in range(2):
+                store(q, n, mm(ly[q], ry[q, :, n]))
+                store(q, n2, mm(ld[q], rd[q, :, n]))
+            return 0
+
+        lax.fori_loop(0, width // cut, put, 0)
+        for q in range(2):
+            store(q, pl.ds(2 * width, 128), mm(pt_of(q), dgs[q * hid : (q + 1) * hid]))
+
+        @pl.when(i > 0)
+        def _():
+            pl.semaphore_wait(free, 1)
+
+        sib_send(i).start()
+
+    def pt_of(q):
+        return ly[q, :, :hid]
+
+    def staged(src, dst, sem):
+        return pltpu.make_async_copy(src, dst, sem)
+
+    def blk(zp, yy, xx):
+        return zp * 4 + yy * 2 + xx
+
+    def pair_sum(i):
+        k, half = i // 2, i % 2
+        zp = plane_at(z, 3 - k)
+        b = zp * 4 + jnp.where(half == 0, 1 - y, y) * 2
+        sib_send(i).wait_recv()
+
+        def one(q, _):
+            add_into(own.at[b + q, 0], sibr.at[q, 0])
+            add_into(own.at[b + q, 1], sibr.at[q, 1])
+            return 0
+
+        lax.fori_loop(0, 2, one, 0)
+
+        @pl.when(i < 7)
+        def _():
+            pl.semaphore_signal(free, inc=1, device_id=(me, other), device_id_type=MESH)
+
+        @pl.when(half == 0)
+        def _():
+            y_(0, blk(zp, 1 - y, 1 - x), 0, zp).start()
+            x_(0, blk(zp, 1 - y, 1 - x), 1, zp).start()
+            y_(1, blk(zp, 1 - y, x), 0, zp).start()
+
+        @pl.when(half == 1)
+        def _():
+            x_(1, blk(zp, y, 1 - x), 1, zp).start()
+
+    def second_staging(k):
+        zp = plane_at(z, 3 - k)
+        return [
+            staged(yr.at[zp, 0], stage.at[0, 0], st_sem.at[0]),
+            staged(xr.at[zp, 0], stage.at[0, 1], st_sem.at[1]),
+            staged(yr.at[zp, 1], stage.at[1, 0], st_sem.at[2]),
+            staged(xr.at[zp, 1], stage.at[1, 1], st_sem.at[3]),
+        ]
+
+    def second_fetch(k):
+        zp = plane_at(z, 3 - k)
+        c = second_staging(k)
+        y_(0, blk(zp, 1 - y, 1 - x), 0, zp).wait_recv()
+        c[0].start()
+        x_(0, blk(zp, 1 - y, 1 - x), 1, zp).wait_recv()
+        c[1].start()
+        y_(1, blk(zp, 1 - y, x), 0, zp).wait_recv()
+        c[2].start()
+        x_(1, blk(zp, y, 1 - x), 1, zp).wait_recv()
+        c[3].start()
+
+    def second_hop(k):
+        zp = plane_at(z, 3 - k)
+        mine = blk(zp, y, x)
+        c = second_staging(k)
+        c[0].wait()
+        add_into(own.at[blk(zp, y, 1 - x), 0], stage.at[0, 0])
+        x_(2, blk(zp, y, 1 - x), 0, zp).start()
+        c[1].wait()
+        add_into(own.at[blk(zp, 1 - y, x), 1], stage.at[0, 1])
+        y_(2, blk(zp, 1 - y, x), 1, zp).start()
+        c[2].wait()
+        add_into(own.at[mine, 0], stage.at[1, 0])
+        c[3].wait()
+        add_into(own.at[mine, 1], stage.at[1, 1])
+
+    def last_staging(k):
+        zp = plane_at(z, 3 - k)
+        return [
+            staged(xr.at[zp, 2], stage.at[0, 0], st_sem.at[0]),
+            staged(yr.at[zp, 2], stage.at[0, 1], st_sem.at[1]),
+            staged(zr.at[1, zp], stage.at[1], st_sem.at[2]),
+            staged(zr.at[0, zp], stage.at[2], st_sem.at[3]),
+        ]
+
+    def last_fetch(k):
+        zp = plane_at(z, 3 - k)
+        c = last_staging(k)
+        x_(2, blk(zp, y, 1 - x), 0, zp).wait_recv()
+        c[0].start()
+        y_(2, blk(zp, 1 - y, x), 1, zp).wait_recv()
+        c[1].start()
+
+        @pl.when((zp <= z) & (z < 3))
+        def _():
+            zc(zp, me, 1).wait_recv()
+            c[2].start()
+
+        @pl.when((zp >= z) & (z > 0))
+        def _():
+            zc(zp, me, 0).wait_recv()
+            c[3].start()
+
+    def last_hop(k):
+        zp = plane_at(z, 3 - k)
+        mine = blk(zp, y, x)
+        c = last_staging(k)
+        c[0].wait()
+        add_into(own.at[mine, 0], stage.at[0, 0])
+        c[1].wait()
+        add_into(own.at[mine, 1], stage.at[0, 1])
+
+        def arrived(d):
+            c[3 - d].wait()
+            add_into(own.at[mine, 0], stage.at[2 - d, 0])
+            add_into(own.at[mine, 1], stage.at[2 - d, 1])
+
+        pl.when((zp <= z) & (z < 3))(lambda: arrived(1))
+        pl.when((zp >= z) & (z > 0))(lambda: arrived(0))
+        pl.when(zp < z)(lambda: zc(zp, dn, 1).start())
+        pl.when(zp > z)(lambda: zc(zp, up, 0).start())
+
+    def step(i, _):
+        pl.when(i < 8)(lambda: first_part(i))
+        pl.when((i >= 1) & (i <= 8))(lambda: pair_sum(i - 1))
+        seconds = (i % 2 == 0) & (i >= 4) & (i <= 10)
+        lasts = (i % 2 == 1) & (i >= 7) & (i <= 13)
+        pl.when(seconds)(lambda: second_fetch((i - 4) // 2))
+        pl.when(lasts)(lambda: last_fetch((i - 7) // 2))
+        pl.when(i < 8)(lambda: second_part(i))
+        pl.when(seconds)(lambda: second_hop((i - 4) // 2))
+        pl.when(lasts)(lambda: last_hop((i - 7) // 2))
+        pl.when(i < 8)(lambda: third_part(i))
+        return 0
+
+    lax.fori_loop(0, 14, step, 0)
+    for a in range(2):
+
+        def row(n, _):
+            r = pl.ds(pl.multiple_of(n * 16, 16), 16)
+            o_out[core, a, r] = own[me, a, r]
+            return 0
+
+        lax.fori_loop(0, 4, row, 0)
+    f = rc(o_out.at[core], o_out.at[core], fs, fr, me, other)
+    f.start()
+    for c in outs(7):
+        c.wait()
+    sib_send(7).wait_send()
+    for k in range(4):
+        for j in range(3):
+            x_(j, 0, 0, k).wait_send()
+            y_(j, 0, 0, k).wait_send()
+
+        @pl.when(k != z)
+        def _():
+            zc(k, up, 0).wait_send()
+
+    rc(o_out.at[core], o_out.at[other], fs, fr, me, other).wait_recv()
+    f.wait_send()
+
+
+def moe_call(moe, grd, pick, pick_t, wg, wu, wd, wr, sgu, sdn, cid):
+    width, ffe = wg.shape
+    total = 2 * width + 128
+    slots = pick.shape[0] * pick.shape[1]
+    low, S, V = jnp.bfloat16, pltpu.SemaphoreType.DMA, pltpu.VMEM
+    any_, vmem = pl.BlockSpec(memory_space=pl.ANY), pl.BlockSpec(memory_space=pltpu.VMEM)
+    shape = lambda *s: jax.ShapeDtypeStruct(s, low)
+    blk = (2, 64, total)
+    return pl.pallas_call(
+        moe_kernel,
+        out_shape=[
+            shape(2, *blk), shape(slots, width), shape(slots, width), shape(slots, ffe), shape(slots, ffe),
+            shape(slots, ffe), jax.ShapeDtypeStruct((384, width), jnp.float32),
+            shape(4, 3, 64, total), shape(4, 3, 64, total), shape(2, 4, *blk),
+        ],
+        in_specs=[any_] * 4 + [vmem] * 6,
+        out_specs=[vmem] + [any_] * 5 + [vmem] + [any_] * 3,
+        scratch_shapes=[
+            V((16,) + blk, low), V((2,) + blk, low), V((2,) + blk, low), V((3,) + blk, low),
+            V((2, 256, width), low), V((2, 256, width), low), V((2, 128, 256), low), V((2, 256, 128), low),
+            V((256, width), low), V((256, width), low), V((2, 256, 256), low), V((2, 256, 384), low),
+            V((2, 256, width), low), V((2, 384, width), low),
+            V((256, ffe), low), V((256, ffe), low), V((256, ffe), low), V((256, 128), low),
+            S((4,)), S((5,)), S((4,)), pltpu.SemaphoreType.REGULAR, S, S, S((4, 3)), S((4, 3)), S((4, 3)), S((4, 3)), S((4,)), S((2, 4)), S, S,
+        ],
+        compiler_params=pltpu.CompilerParams(collective_id=cid, has_side_effects=True, vmem_limit_bytes=60 << 20),
+        cost_estimate=pl.CostEstimate(flops=65 * 10**9, bytes_accessed=80 * 10**6, transcendentals=0),
+    )(moe, grd, pick, pick_t, wg, wu, wd, wr, sgu, sdn)
+
+
+SLOTS = 5
+KEYS = SLOTS * 256
+
+
+def turned(v, cos, sin):
+    n = v.shape[1]
+    lane = lax.broadcasted_iota(jnp.int32, v.shape, 1) % 64
+    swap = jnp.where(lane < 32, -pltpu.roll(v, n - 32, 1), pltpu.roll(v, 32, 1))
+    return v * cos + swap * sin
+
+
+def root(v):
+    return lax.rsqrt(jnp.mean(v * v, axis=1, keepdims=True) + eps_norm)
+
+
+def neighbours(me, core, bar):
+    count = jnp.int32(1)
+    pl.semaphore_signal(bar, inc=1, device_id=(me, 1 - core), device_id_type=MESH)
+    for d in range(1, SLOTS):
+
+        @pl.when(me + d < 16)
+        def _():
+            pl.semaphore_signal(bar, inc=1, device_id=(jnp.minimum(me + d, 15), core), device_id_type=MESH)
+
+        @pl.when(me >= d)
+        def _():
+            pl.semaphore_signal(bar, inc=1, device_id=(jnp.maximum(me - d, 0), core), device_id_type=MESH)
+
+        count = count + (me + d < 16).astype(jnp.int32) + (me >= d).astype(jnp.int32)
+    return count
+
+
+def slab_copies(w4, w2, wq, wo, wkv, wlat, sem):
+    pairs = [
+        (w2.at[:, 2560:3200], wlat, sem.at[0]),
+        (w2.at[:, 0:1536], wq, sem.at[1]),
+        (w2.at[:, 1536:2560], wo, sem.at[2]),
+    ]
+    for c in range(4):
+        pairs.append((w4.at[:, c, :, w4.shape[3] - 512 :], wkv.at[:, :, c * 512 : (c + 1) * 512], sem.at[3 + c]))
+    return pairs
+
+
+def att_fwd_kernel(
+    tok, w4, w2, g_att, g_moe, g_lat, cos, sin, bias,
+    middle, moe_low, normed, lat_raw, qcat, keys, kv_out, lse, att,
+    kv, wq, wo, wkv, wlat, part, arrived, w_sem, kv_sem, ks, kr, cs, cr,
+):
+    me = lax.axis_index("dp")
+    core = lax.axis_index("tensor")
+    loads = [pltpu.make_async_copy(h, v, s) for h, v, s in slab_copies(w4, w2, wq, wo, wkv, wlat, w_sem)]
+    for c in loads:
+        c.start()
+    bar = pltpu.get_barrier_semaphore()
+    pl.semaphore_wait(bar, neighbours(me, core, bar))
+    t = tok[...].astype(jnp.float32)
+    normed[...] = (t * root(t) * g_att[...]).astype(jnp.bfloat16)
+    loads[0].wait()
+    lat = mm(normed[...], wlat[...])
+    lat_raw[...] = lat
+    first = lat[:, :RANK]
+    rot = turned(lat[:, RANK:], cos[:, :128], sin[:, :128])
+    rot = jnp.where(lax.broadcasted_iota(jnp.int32, rot.shape, 1) < 64, rot, 0.0)
+    keys[SLOTS - 1, :, :RANK] = (first * root(first) * g_lat[...]).astype(jnp.bfloat16)
+    keys[SLOTS - 1, :, RANK:] = (rot + pltpu.roll(rot, 64, 1)).astype(jnp.bfloat16)
+
+    def send(d):
+        return pltpu.make_async_remote_copy(
+            src_ref=keys.at[SLOTS - 1], dst_ref=keys.at[SLOTS - 1 - d], send_sem=ks.at[d - 1], recv_sem=kr.at[d - 1],
+            device_id=(jnp.minimum(me + d, 15), core), device_id_type=MESH,
+        )
+
+    for d in range(1, SLOTS):
+        pl.when(me + d < 16)(lambda d=d: send(d).start())
+
+        @pl.when(me < d)
+        def _():
+            keys[SLOTS - 1 - d] = jnp.zeros((256, 640), jnp.bfloat16)
+
+    loads[1].wait()
+    half = lax.broadcasted_iota(jnp.int32, (256, 128), 1) < 64
+    q_nope = mm(normed[...], wq[:, :1024])
+    q_rope = turned(mm(normed[...], wq[:, 1024:]), cos[...], sin[...])
+    for h in range(8):
+        qcat[h, :, :128] = q_nope[:, h * 128 : (h + 1) * 128].astype(jnp.bfloat16)
+        pair = q_rope[:, h // 2 * 128 : (h // 2 + 1) * 128]
+        qcat[h, :, 128:] = jnp.where(half == (h % 2 == 0), pair, 0.0).astype(jnp.bfloat16)
+    for c in loads[3:]:
+        c.wait()
+    for s in range(SLOTS - 1, -1, -1):
+        if s < SLOTS - 1:
+            pl.when(me >= SLOTS - 1 - s)(lambda s=s: send(SLOTS - 1 - s).wait_recv())
+        kv[s * 256 : (s + 1) * 256] = mm(keys[s, :, :RANK], wkv[...].reshape(RANK, 2048)).astype(jnp.bfloat16)
+    save = pltpu.make_async_copy(kv, kv_out, kv_sem)
+    save.start()
+
+    def head(h, _):
+        kn = kv[:, pl.ds(pl.multiple_of(h * 256, 256), 128)]
+        v = kv[:, pl.ds(pl.multiple_of(h * 256 + 128, 128), 128)]
+        rope = keys[:, :, RANK:].reshape(KEYS, 128)
+        s = nt(qcat[h], jnp.concatenate([kn, rope], 1)) * ((NOPE + ROPE) ** -0.5) + bias[...]
+        top = jnp.max(s, axis=1, keepdims=True)
+        e = jnp.exp(s - top)
+        den = jnp.sum(e, axis=1, keepdims=True)
+        lse[h] = top + jnp.log(den)
+        p = (e * (1.0 / den)).astype(jnp.bfloat16)
+        att[:, pl.ds(pl.multiple_of(h * 128, 128), 128)] = mm(p, v).astype(jnp.bfloat16)
+        return 0
+
+    lax.fori_loop(0, 8, head, 0)
+    loads[2].wait()
+
+    def out(n, _):
+        r = pl.ds(pl.multiple_of(n * 512, 512), 512)
+        part[:, r] = nt(att[...], wo[r]).astype(jnp.bfloat16)
+        return 0
+
+    lax.fori_loop(0, 4, out, 0)
+    swap = pltpu.make_async_remote_copy(
+        src_ref=part, dst_ref=arrived, send_sem=cs, recv_sem=cr, device_id=(me, 1 - core), device_id_type=MESH
+    )
+    swap.start()
+    swap.wait()
+    m = tok[...].astype(jnp.float32) + (part[...].astype(jnp.float32) + arrived[...].astype(jnp.float32))
+    middle[...] = m
+    moe_low[...] = (m * root(m) * g_moe[...]).astype(jnp.bfloat16)
+    save.wait()
+    for d in range(1, SLOTS):
+        pl.when(me + d < 16)(lambda d=d: send(d).wait_send())
+
+
+def att_fwd(tok, weights, g_att, g_moe, g_lat, cos, sin, bias, cid):
+    low, f32, S, V = jnp.bfloat16, jnp.float32, pltpu.SemaphoreType.DMA, pltpu.VMEM
+    any_, vmem = pl.BlockSpec(memory_space=pl.ANY), pl.BlockSpec(memory_space=pltpu.VMEM)
+    shape = lambda kind, *s: jax.ShapeDtypeStruct(s, kind)
+    rows, width = tok.shape
+    pack = weights.shape[1]
+    return pl.pallas_call(
+        att_fwd_kernel,
+        out_shape=[
+            shape(f32, rows, width), shape(low, rows, width), shape(low, rows, width), shape(f32, rows, 640),
+            shape(low, 8, rows, 256), shape(low, SLOTS, rows, 640), shape(low, KEYS, 2048), shape(f32, 8, rows, 1),
+            shape(low, rows, 1024),
+        ],
+        in_specs=[vmem, any_, any_] + [vmem] * 6,
+        out_specs=[vmem] * 6 + [any_] + [vmem] * 2,
+        scratch_shapes=[
+            V((KEYS, 2048), low), V((width, 1536), low), V((width, 1024), low), V((16, 32, 2048), low), V((width, 640), low),
+            V((rows, width), low), V((rows, width), low), S((7,)), S, S((4,)), S((4,)), S, S,
+        ],
+        compiler_params=pltpu.CompilerParams(collective_id=cid, has_side_effects=True, vmem_limit_bytes=60 << 20),
+        cost_estimate=pl.CostEstimate(flops=10**10, bytes_accessed=40 * 10**6, transcendentals=0),
+    )(tok, weights.reshape(16, 4, 32, pack), weights, g_att, g_moe, g_lat, cos, sin, bias)
+
+
+def att_bwd_kernel(
+    w4, w2, home, grad, middle, moe_low, tok, normed, lat_raw, qcat, keys, kv_in, lse, att, wr,
+    g_att, g_moe, g_lat, cos, sin, bias,
+    tok_grad, packed, p4,
+    kv, wq, wo, wkv, wlat, dmid, dnorm, dmid_low, d_att, dq, dqr, dkr, dk_out, dk_in, own_dk, part, arrived,
+    w_sem, kv_sem, ks, kr, cs, cr, o_sem,
+):
+    me = lax.axis_index("dp")
+    core = lax.axis_index("tensor")
+    width = tok.shape[1]
+    scale = (NOPE + ROPE) ** -0.5
+    loads = [pltpu.make_async_copy(h, v, s) for h, v, s in slab_copies(w4, w2, wq, wo, wkv, wlat, w_sem)]
+    stores = [pltpu.make_async_copy(v, h, s) for h, v, s in slab_copies(p4, packed, wq, wo, wkv, wlat, o_sem)]
+    kv_load = pltpu.make_async_copy(kv_in, kv, kv_sem)
+    loads[2].start()
+    kv_load.start()
+    for n in (1, 3, 4, 5, 6, 0):
+        loads[n].start()
+    bar = pltpu.get_barrier_semaphore()
+    pl.semaphore_wait(bar, neighbours(me, core, bar))
+    lane = lax.broadcasted_iota(jnp.int32, (256, 128), 1)
+
+    logits = jnp.where(lane < 16, mm(moe_low[...], wr[...]), -jnp.inf)
+    e = jnp.exp(logits - jnp.max(logits, axis=1, keepdims=True))
+    router = e / jnp.sum(e, axis=1, keepdims=True)
+    d_router = jnp.where(lane < 16, home[:, width:].astype(jnp.float32), 0.0)
+    d_logits = (router * (d_router - jnp.sum(router * d_router, axis=1, keepdims=True))).astype(jnp.bfloat16)
+
+    def norm_back(v, gain, dy):
+        r = root(v)
+        hat = v * r
+        up = dy * gain
+        return r * (up - hat * jnp.mean(up * hat, axis=1, keepdims=True)), dy * hat
+
+    def one_lane(n):
+        return (lane == n).astype(jnp.bfloat16)
+
+    d_moe = home[:, :width].astype(jnp.float32) + nt(d_logits, wr[...])
+    d_norm2, gain_rows = norm_back(middle[...], g_moe[...], d_moe)
+    d_middle = grad[...].astype(jnp.float32) + d_norm2
+    dmid[...] = d_middle
+    dmid_low[...] = d_middle.astype(jnp.bfloat16)
+    gains = gain_rows.astype(jnp.bfloat16)
+    moved = pltpu.roll(d_logits.astype(jnp.float32), 64, 1).astype(jnp.bfloat16)
+    small = tn(moe_low[...], moved) + tn(gains, one_lane(81))
+
+    loads[2].wait()
+    d_att[...] = mm(dmid_low[...], wo[...]).astype(jnp.bfloat16)
+
+    def wo_rows(n, _):
+        r = pl.ds(pl.multiple_of(n * 256, 256), 256)
+        wo[r] = tn(dmid_low[:, r], att[...]).astype(jnp.bfloat16)
+        return 0
+
+    lax.fori_loop(0, width // 256, wo_rows, 0)
+    stores[2].start()
+    kv_load.wait()
+    dkr[...] = jnp.zeros_like(dkr)
+    dqr[...] = jnp.zeros_like(dqr)
+
+    def head(h, _):
+        cols = pl.ds(pl.multiple_of(h * 128, 128), 128)
+        nope_at = pl.ds(pl.multiple_of(h * 256, 256), 128)
+        value_at = pl.ds(pl.multiple_of(h * 256 + 128, 128), 128)
+        pair = pl.ds(pl.multiple_of(h // 2 * 128, 128), 128)
+        kc = jnp.concatenate([kv[:, nope_at], keys[:, :, RANK:].reshape(KEYS, 128)], 1)
+        p = jnp.exp(nt(qcat[h], kc) * scale + bias[...] - lse[h])
+        dv = tn(p.astype(jnp.bfloat16), d_att[:, cols])
+        dp = nt(d_att[:, cols], kv[:, value_at])
+        ds = (p * (dp - jnp.sum(p * dp, axis=1, keepdims=True))).astype(jnp.bfloat16)
+        dqc = mm(ds, kc) * scale
+        dkc = tn(ds, qcat[h]) * scale
+        dq[:, cols] = dqc[:, :128].astype(jnp.bfloat16)
+        dqr[:, pair] += jnp.where((lane < 64) == (h % 2 == 0), dqc[:, 128:], 0.0)
+        kv[:, nope_at] = dkc[:, :128].astype(jnp.bfloat16)
+        kv[:, value_at] = dv.astype(jnp.bfloat16)
+        dkr[...] += dkc[:, 128:]
+        return 0
+
+    lax.fori_loop(0, 8, head, 0)
+    for n in (3, 4, 5, 6):
+        loads[n].wait()
+
+    def send(d):
+        return pltpu.make_async_remote_copy(
+            src_ref=dk_out.at[d - 1], dst_ref=dk_in.at[d - 1], send_sem=ks.at[d - 1], recv_sem=kr.at[d - 1],
+            device_id=(jnp.maximum(me - d, 0), core), device_id_type=MESH,
+        )
+
+    for s in range(SLOTS):
+        r = slice(s * 256, (s + 1) * 256)
+        d_lat = nt(kv[r], wkv[...].reshape(RANK, 2048))
+        d_rope = dkr[r] + pltpu.roll(dkr[r], 64, 1)
+        if s == SLOTS - 1:
+            own_dk[:, :RANK] = d_lat
+            own_dk[:, RANK:] = d_rope
+        else:
+            d = SLOTS - 1 - s
+            dk_out[d - 1, :, :RANK] = d_lat.astype(jnp.bfloat16)
+            dk_out[d - 1, :, RANK:] = d_rope.astype(jnp.bfloat16)
+            pl.when(me >= d)(lambda d=d: send(d).start())
+    dq[:, 1024:] = turned(dqr[...], cos[...], -sin[...]).astype(jnp.bfloat16)
+    loads[1].wait()
+
+    def normed_cols(n, _):
+        r = pl.ds(pl.multiple_of(n * 512, 512), 512)
+        v = nt(dq[...], wq[r])
+        part[:, r] = v.astype(jnp.bfloat16)
+        wq[r] = tn(normed[:, r], dq[...]).astype(jnp.bfloat16)
+        return 0
+
+    lax.fori_loop(0, 4, normed_cols, 0)
+    stores[1].start()
+    latent_all = keys[:, :, :RANK].reshape(KEYS, RANK)
+    for c in range(4):
+        g = tn(latent_all, kv[:, c * 512 : (c + 1) * 512]).astype(jnp.bfloat16)
+        wkv[:, :, c * 512 : (c + 1) * 512] = g.reshape(16, 32, 512)
+        stores[3 + c].start()
+    for d in range(1, SLOTS):
+
+        @pl.when(me + d < 16)
+        def _():
+            pltpu.make_async_remote_copy(
+                src_ref=dk_out.at[d - 1], dst_ref=dk_in.at[d - 1], send_sem=ks.at[d - 1], recv_sem=kr.at[d - 1],
+                device_id=(jnp.minimum(me + d, 15), core), device_id_type=MESH,
+            ).wait_recv()
+            own_dk[...] += dk_in[d - 1].astype(jnp.float32)
+
+    part[:, width:] = own_dk[...].astype(jnp.bfloat16)
+    swap = pltpu.make_async_remote_copy(
+        src_ref=part, dst_ref=arrived, send_sem=cs, recv_sem=cr, device_id=(me, 1 - core), device_id_type=MESH
+    )
+    swap.start()
+    swap.wait()
+    dnorm[...] = part[:, :width].astype(jnp.float32) + arrived[:, :width].astype(jnp.float32)
+    d_keys = part[:, width:].astype(jnp.float32) + arrived[:, width:].astype(jnp.float32)
+
+    d_first, lat_gain_rows = norm_back(lat_raw[:, :RANK], g_lat[...], d_keys[:, :RANK])
+    d_second = turned(d_keys[:, RANK:], cos[:, :128], -sin[:, :128])
+    d_second = jnp.where(lane < 64, d_second, 0.0)
+    d_lat_low = jnp.concatenate([d_first, d_second], 1).astype(jnp.bfloat16)
+    loads[0].wait()
+    d_normed = dnorm[...] + nt(d_lat_low, wlat[...])
+    d_norm1, att_gain_rows = norm_back(tok[...].astype(jnp.float32), g_att[...], d_normed)
+    tok_grad[...] = dmid[...] + d_norm1
+    small = small + tn(normed[...], d_lat_low[:, RANK:]) + tn(att_gain_rows.astype(jnp.bfloat16), one_lane(80))
+    wlat[:, :RANK] = tn(normed[...], d_lat_low[:, :RANK]).astype(jnp.bfloat16)
+    wlat[:, RANK:] = small.astype(jnp.bfloat16)
+    lat_col = tn(lat_gain_rows.astype(jnp.bfloat16), one_lane(82))
+    for b in range(16):
+        r = slice(b * 128, b * 128 + 32)
+        wlat[r, RANK:] = (small[r] + lat_col[b * 32 : (b + 1) * 32]).astype(jnp.bfloat16)
+    stores[0].start()
+    for c in stores:
+        c.wait()
+    for d in range(1, SLOTS):
+        pl.when(me >= d)(lambda d=d: send(d).wait_send())
+
+
+def att_bwd(weights, home, grad, middle, moe_low, tok, normed, lat_raw, qcat, keys, kv, lse, att, wr, g_att, g_moe, g_lat, cos, sin, bias, cid):
+    low, f32, S, V = jnp.bfloat16, jnp.float32, pltpu.SemaphoreType.DMA, pltpu.VMEM
+    any_, vmem = pl.BlockSpec(memory_space=pl.ANY), pl.BlockSpec(memory_space=pltpu.VMEM)
+    shape = lambda kind, *s: jax.ShapeDtypeStruct(s, kind)
+    rows, width = tok.shape
+    pack = weights.shape[1]
+    return pl.pallas_call(
+        att_bwd_kernel,
+        out_shape=[shape(f32, rows, width), shape(low, width, pack - 512), shape(low, 16, 4, 32, 512)],
+        in_specs=[any_, any_] + [vmem] * 9 + [any_] + [vmem] * 9,
+        out_specs=[vmem, any_, any_],
+        scratch_shapes=[
+            V((KEYS, 2048), low), V((width, 1536), low), V((width, 1024), low), V((16, 32, 2048), low),
+            V((width, 640), low), V((rows, width), f32), V((rows, width), f32), V((rows, width), low), V((rows, 1024), low),
+            V((rows, 1536), low), V((rows, 512), f32), V((KEYS, 128), f32), V((4, rows, 640), low), V((4, rows, 640), low),
+            V((rows, 640), f32), V((rows, width + 640), low), V((rows, width + 640), low),
+            S((7,)), S, S((4,)), S((4,)), S, S, S((7,)),
+        ],
+        compiler_params=pltpu.CompilerParams(collective_id=cid, has_side_effects=True, vmem_limit_bytes=60 << 20),
+        cost_estimate=pl.CostEstimate(flops=25 * 10**9, bytes_accessed=70 * 10**6, transcendentals=0),
+    )(
+        weights.reshape(16, 4, 32, pack), weights, home, grad, middle, moe_low, tok, normed, lat_raw, qcat, keys, kv, lse, att, wr,
+        g_att, g_moe, g_lat, cos, sin, bias,
+    )
+
+
+def swapped(v):
+    return lax.ppermute(v, "tensor", [(0, 1), (1, 0)])
+
+
+def my_half(v, rows):
+    return lax.dynamic_slice_in_dim(v, lax.axis_index("tensor") * rows, rows, 0)
+
+
+def row_halves(v):
+    rows = v.shape[0] // 2
+    return my_half(v, rows).reshape(2, rows // 2, v.shape[1])
+
+
+def exchange(parts):
+    return lax.all_to_all(parts, "dp", split_axis=0, concat_axis=0, tiled=True)
+
+
+def nope_first(w):
+    heads = w.reshape(w.shape[0], -1, NOPE + ROPE)
+    return jnp.concatenate(
+        [heads[:, :, :NOPE].reshape(w.shape[0], -1), heads[:, :, NOPE:].reshape(w.shape[0], -1)], 1
+    )
+
+
+def heads_first(w):
+    heads = w.shape[1] // (NOPE + ROPE)
+    nope = w[:, : heads * NOPE].reshape(w.shape[0], heads, NOPE)
+    rope = w[:, heads * NOPE :].reshape(w.shape[0], heads, ROPE)
+    return jnp.concatenate([nope, rope], 2).reshape(w.shape[0], -1)
+
+
+def shards_sixteen(
+    tokens,
+    out_grad,
+    segments,
+    routes,
+    attn_gain,
+    w_query,
+    w_latent,
+    latent_gain,
+    w_keyval,
+    w_out,
+    moe_gain,
+    w_router,
+    shared_gate,
+    shared_up,
+    shared_down,
+    expert_gate,
+    routed_up_weight,
+    expert_down,
+):
+    n_rows, width = tokens.shape
+    dp_count = lax.axis_size("dp")
+    dp_index = lax.axis_index("dp")
+    seq_len = segments.shape[1]
+    total = n_rows * dp_count
+    hop_count = (WINDOW - 1) // n_rows + 1
+    n_keys = (hop_count + 1) * n_rows
+    experts = w_router.shape[1]
+    capacity = 4 * n_rows * TOPK // (3 * experts)
+    row_start = dp_index * n_rows
+    seg_row = segments[0]
+    depth = w_query.shape[0]
+    q_width, o_width, kv_width = w_query.shape[1], w_out.shape[0], w_keyval.shape[1]
+    kv_rows = w_keyval.shape[0]
+    kv_cuts = depth // kv_rows
+    kv_part = kv_width // kv_cuts
+    lat_width = w_latent.shape[1]
+    route_width = n_rows * TOPK // depth
+    small = (lat_width + experts + 3 + route_width + 127) // 128 * 128
+
+    gains = jnp.stack(
+        [attn_gain, moe_gain, jnp.pad(latent_gain, (0, depth - kv_rows))], 1
+    )
+    packed = jnp.concatenate(
+        [
+            nope_first(w_query),
+            w_out.T,
+            w_latent,
+            w_router,
+            gains,
+            routes.reshape(depth, route_width).astype(jnp.bfloat16),
+            jnp.zeros((depth, small - lat_width - experts - 3 - route_width), jnp.bfloat16),
+            w_keyval.reshape(kv_rows, kv_cuts, kv_part).transpose(1, 0, 2).reshape(depth, kv_part),
+        ],
+        1,
+    )
+    pack_width = packed.shape[1]
+    weights, grad_all = ag16(
+        [packed.reshape(2, depth // 2, pack_width), row_halves(out_grad)], (False, True), 1
+    )
+    weights = weights.reshape(width, pack_width)
+    shared_part = shared_gate.shape[1] // dp_count
+    shared_send = jnp.stack(
+        [
+            shared_gate.reshape(depth, dp_count, shared_part).transpose(1, 2, 0),
+            shared_up.reshape(depth, dp_count, shared_part).transpose(1, 2, 0),
+            shared_down.reshape(dp_count, shared_part, depth),
+        ],
+        1,
+    )
+    shared_send, weights = lax.optimization_barrier((shared_send, weights))
+    shared_all = exchange(shared_send).transpose(1, 2, 0, 3).reshape(3, shared_part, width)
+    lead = jnp.pad(shared_all, ((0, 0), (0, 128 - shared_part), (0, 0)))
+    shared_in, shared_out = lead[:2].reshape(256, width), lead[2]
+
+    at = q_width + o_width + lat_width
+    wr_full = weights[:, at : at + experts]
+    at += experts
+    gain_attn = weights[:, at].astype(jnp.float32)
+    gain_moe = weights[:, at + 1].astype(jnp.float32)
+    gain_latent = (
+        weights[:, at + 2].reshape(dp_count, depth)[:, :kv_rows].reshape(-1).astype(jnp.float32)
+    )
+
+    all_routes = (
+        weights[:, at + 3 : at + 3 + route_width].reshape(total, TOPK).astype(jnp.int32)
+    )
+
+    local_heads = q_width // (NOPE + ROPE)
+    positions = (row_start + jnp.arange(n_rows, dtype=jnp.int32)).astype(jnp.float32)
+    cos_tab, sin_tab = rope_tables(positions)
+    cos_lanes, sin_lanes = jnp.tile(cos_tab, (1, 2 * local_heads)), jnp.tile(sin_tab, (1, 2 * local_heads))
+    key_pos = row_start - hop_count * n_rows + jnp.arange(n_keys, dtype=jnp.int32)
+    query_pos = row_start + jnp.arange(n_rows, dtype=jnp.int32)
+    padded_seg = jnp.concatenate([jnp.full((hop_count * n_rows,), -1, jnp.int32), seg_row])
+    key_seg = lax.dynamic_slice_in_dim(padded_seg, row_start, n_keys, 0)
+    query_seg = lax.dynamic_slice_in_dim(seg_row, row_start, n_rows, 0)
+    allowed = (key_pos[None, :] >= 0) & (key_pos[None, :] <= query_pos[:, None])
+    allowed = (
+        allowed
+        & (query_pos[:, None] - key_pos[None, :] < WINDOW)
+        & (query_seg[:, None] == key_seg[None, :])
+    )
+
+    bias = jnp.where(allowed, 0.0, -jnp.inf)
+    middle, moe_low, normed_low, lat_raw, qcat, keys, kv, lse, attended_low = att_fwd(
+        tokens, weights, gain_attn[None], gain_moe[None], gain_latent[None], cos_lanes, sin_lanes, bias, 7
+    )
+    moe_low, shared_in, shared_out = lax.optimization_barrier((moe_low, shared_in, shared_out))
+    (moe_all,) = ag16([row_halves(moe_low)], (True,), 3)
+    chosen = jnp.any(all_routes == dp_index, axis=1).reshape(dp_count, n_rows)
+    earlier = jnp.arange(n_rows)[:, None] < jnp.arange(n_rows)[None, :]
+    rank = matmul(chosen.astype(jnp.bfloat16), earlier.astype(jnp.bfloat16)).astype(jnp.int32)
+    pick = (
+        (rank[:, None, :] == jnp.arange(capacity, dtype=jnp.int32)[None, :, None])
+        & chosen[:, None, :]
+    ).astype(jnp.bfloat16)
+
+    slot_rows = dp_count * capacity
+    moe_wr = jnp.pad(wr_full, ((0, 0), (0, 128 - experts)))
+    home, rows_in, rows_grad, scaled_act, d_ea_low, d_eb_low, shared_grads = moe_call(
+        moe_all.reshape(dp_count, n_rows, width),
+        grad_all.reshape(dp_count, n_rows, width),
+        pick,
+        pick.transpose(0, 2, 1),
+        expert_gate[0],
+        routed_up_weight[0],
+        expert_down[0],
+        moe_wr,
+        shared_in,
+        shared_out,
+        4,
+    )[:7]
+    home = home.reshape(n_rows, 2 * width + 128)
+    result = (middle + home[:, :width].astype(jnp.float32)).astype(jnp.bfloat16)
+    grad_down = matmul_tn(scaled_act, rows_grad)[None]
+    grad_gate = matmul_tn(rows_in, d_ea_low)[None]
+    grad_up = matmul_tn(rows_in, d_eb_low)[None]
+    shared_home = exchange(
+        shared_grads.astype(jnp.bfloat16)
+        .reshape(3, 128, dp_count, depth)[:, :shared_part]
+        .transpose(2, 0, 1, 3)
+    ).astype(jnp.float32)
+    shared_home = shared_home.transpose(1, 0, 2, 3).reshape(3, dp_count * shared_part, depth)
+
+    token_input_gradient, packed_grads, kv_grads = att_bwd(
+        weights, home[:, width:], out_grad, middle, moe_low, tokens, normed_low, lat_raw, qcat, keys, kv, lse,
+        attended_low, moe_wr, gain_attn[None], gain_moe[None], gain_latent[None], cos_lanes, sin_lanes, bias, 8
+    )
+    packed_grads, shared_home = lax.optimization_barrier((packed_grads, shared_home))
+    mine = rs16(
+        packed_grads.reshape(dp_count, 2, depth // 2, pack_width - kv_part),
+        kv_grads.reshape(dp_count, 2, depth // 2, kv_part),
+        6,
+    ).reshape(depth, pack_width)
+    grad_sgate, grad_sup, grad_sdown = shared_home[0].T, shared_home[1].T, shared_home[2]
+    out_wq = heads_first(mine[:, :q_width])
+    at = q_width
+    out_wo = mine[:, at : at + o_width].T
+    at += o_width
+    out_wlat = mine[:, at : at + lat_width]
+    at += lat_width
+    out_router = mine[:, at : at + experts]
+    at += experts
+    out_wkv = (
+        mine[:, pack_width - kv_part :]
+        .reshape(kv_cuts, kv_rows, kv_part)
+        .transpose(1, 0, 2)
+        .reshape(kv_rows, kv_width)
+    )
+    return (
+        result,
+        token_input_gradient,
+        mine[:, at],
+        out_wq,
+        out_wlat,
+        mine[:kv_rows, at + 2],
+        out_wkv,
+        out_wo,
+        mine[:, at + 1],
+        out_router,
+        grad_sgate,
+        grad_sup,
+        grad_sdown,
+        grad_gate,
+        grad_up,
+        grad_down,
+    )
+
+
+def shards_general(
     tokens,
     out_grad,
     segments,
@@ -213,7 +1492,7 @@
     flat_routes = routes.reshape(-1)
     assign_count = flat_routes.shape[0]
     flat_hot = (flat_routes[:, None] == expert_ids[None, :]).astype(jnp.int32)
-    earlier = jnp.cumsum(flat_hot, axis=0) - flat_hot
+    earlier = ranks_before(flat_hot)
     slot_in = jnp.sum(earlier * flat_hot, axis=1)
     target = flat_routes * capacity + slot_in
     assign_ids = jnp.arange(assign_count, dtype=jnp.int32)
@@ -442,8 +1721,14 @@
         P("dp", None, "tensor"),
         P("dp", "tensor", None),
     )
+    sixteen = mesh.shape["dp"] == 16 and mesh.shape["tensor"] == 2
+
+    def body(*args):
+        fits_sixteen = sixteen and args[2].shape[0] == 1 and args[15].shape[0] == 1 and args[0].shape[0] == 256
+        return (shards_sixteen if fits_sixteen else shards_general)(*args)
+
     return jax.shard_map(
-        shards,
+        body,
         mesh=mesh,
         in_specs=placed,
         out_specs=(

time: 3110 us -> 887 us (0.29)
  waiting for transfers between devices: 1990 us -> 0.01 us
  Pallas kernels: 0 us -> 759 us
  blocking collectives: 417 us -> 0 us
  matrix products: 267 us -> 32.2 us
  starting transfers between devices: 160 us -> 9.94 us
  local copies, waits for them, and re-layouts: 180 us -> 58.6 us
  other arithmetic: 68.9 us -> 17.1 us
    reduce_scatter x8 -> x0, waiting for transfers between devices: 1290 us -> none  [the longest x1 249 us: shards(): lax.psum_scatter(grad_sdown, 'dp', scatter_dimension=1, tiled=True)]
    pallas_call x0 -> x6, Pallas kernels: none -> 759 us  [the longest x2 311 us: ag16(): pl.pallas_call(functools.partial(ag_kernel, kinds, cuts), out_shape=[jax....]
    all_to_all x3 -> x2, waiting for transfers between devices: 337 us -> 0.01 us  [exchange(): return lax.all_to_all(parts, 'dp', split_axis=0, concat_axis=0, tiled=True)]
    all_gather x7 -> x0, waiting for transfers between devices: 327 us -> none  [the longest x1 231 us: shards(): lax.all_gather(shared_down, 'dp', axis=1, tiled=True)]
    dot_general x30 -> x0, matrix products: 186 us -> none  [the longest x8 29 us: matmul_nt(): lax.dot_general(left_mat, right_mat, (((1,), (1,)), ((), ())), preferred_...]
    all_to_all x1 -> x0, blocking collectives: 180 us -> none  [shards(): lax.all_to_all(send_grads.reshape(dp_count, local_experts * capacity, mod...]
    all_to_all x3 -> x2, starting transfers between devices: 128 us -> 9.94 us  [exchange(): return lax.all_to_all(parts, 'dp', split_axis=0, concat_axis=0, tiled=True)]
    all_gather x3 -> x0, blocking collectives: 118 us -> none  [the longest x1 42.5 us: shards(): lax.all_gather(attn_gain, 'dp', axis=0, tiled=True)]
  transfers between devices with their start and end apart: 37 -> 2, of which waited for: 20 -> 0; matrix products, arithmetic and copies ran while one was open for 13% -> 7% of each run, Pallas kernels for 0% -> 10%
where the time goes in v3:
time: 887 us; the launch traced here: 879 us
  Pallas kernels  759 us (86%)
  local copies, waits for them, and re-layouts  58.6 us (7%)
  matrix products  32.2 us (4%)
  other arithmetic  17.1 us (2%)
  starting transfers between devices  9.94 us (1%)
    pallas_call x2, Pallas kernels, ag16(): pl.pallas_call(functools.partial(ag_kernel, kinds, cuts), out_shape=[jax....  311 us
    pallas_call x1, Pallas kernels, moe_call(): pl.pallas_call(moe_kernel, out_shape=[shape(2, *blk), shape(slots, width)...  209 us
    pallas_call x1, Pallas kernels, rs16(): pl.pallas_call(rs_kernel, out_shape=jax.ShapeDtypeStruct(blkshape, jnp.fl...  154 us
    pallas_call x1, Pallas kernels, att_bwd(): pl.pallas_call(att_bwd_kernel, out_shape=[shape(f32, rows, width), shape(...  55.6 us
    dot_general x3, matrix products, matmul_tn(): lax.dot_general(left_mat, right_mat, (((0,), (0,)), ((), ())), preferred_...  32 us
    pallas_call x1, Pallas kernels, att_fwd(): pl.pallas_call(att_fwd_kernel, out_shape=[shape(f32, rows, width), shape(...  29.6 us
    unnamed x47, local copies, waits for them, and re-layouts  28 us
  transfers between devices with their start and end apart: 2, of which 0 were waited for; matrix products, arithmetic and copies ran while one was open for 7% of the time, Pallas kernels for 10%

profile of v3, /device:TPU:0, one launch (start us, length us, event | category | flops | bytes accessed | tf_op | source)
XLA Modules:
  0.0 878.5 jit_solution(8685782656274874516)
XLA Ops:
  0.7 1.3 copy.126
  2.1 0.7 convert_element_type.83
  2.8 0.7 pad.13
  3.6 0.9 concatenate.40
  4.5 0.9 concatenate.41
  5.4 0.8 copy.131
  6.5 0.9 copy.177
  8.8 1.9 constant_dynamic-slice_fusion.2
  10.8 1.1 concatenate.37.refs_0_
  11.9 203.5 %shard_map.297 = (bf16[16,1,2,64,3712]{4,3,2,1,0:T(8,128)(2,1)}, bf16[16,2,2,64,2048]{4,3,2,1,0:T(8,128)(2,1)}) custom-call(bf16[2,64,3712]{2,1,0:T(8,128)(2,1)} %concatenate.37.refs_0_, bf16[2,64,2048]{2,1,0:T(8,128)(2,1)} %bitcast.114), custom_call_target="tpu_custom_call" | custom-call | tf_op jit(solution)/shard_map/pallas_call | solution.py:238
  215.6 1.1 copy.139
  216.6 5.2 all-to-all-start
  221.8 1.4 slice_reduce_fusion
  223.3 2.6 convert_reduce_fusion
  225.8 1.4 convert_compare_fusion
  227.3 1.2 slice.87
  228.8 1.0 copy.138.sin
  229.8 1.0 copy.137.cos
  230.8 4.6 copy.141
  235.4 4.6 copy.142
  240.0 0.7 reshape.286.g_lat
  240.6 0.5 eq.50
  241.2 0.6 reduce_or.9
  241.9 0.9 pad.15.wr
  242.9 2.4 fusion.3.pick_t
  245.4 1.4 fusion.1.pick
  246.7 1.6 fusion.6.bias
  248.4 29.6 %shard_map.298 = (f32[256,2048]{1,0:T(8,128)}, bf16[256,2048]{1,0:T(8,128)(2,1)}, bf16[256,2048]{1,0:T(8,128)(2,1)}, f32[256,640]{1,0:T(8,128)}, bf16[8,256,256]...) custom-call(bf16[256,2048]{1,0:T(8,128)(2,1)} %tok.3, ...), custom_call_target="tpu_custom_call" | custom-call | flops 10000000000 | bytes 40000000 | tf_op jit(solution)/shard_map/pallas_call | solution.py:924
  278.1 0.8 fusion.7.sdn
  279.0 1.1 pad_slice_fusion.1
  280.0 0.8 constant_dynamic-slice_fusion
  280.9 107.4 %shard_map.299 = bf16[16,2,2,64,2048]{4,3,2,1,0:T(8,128)(2,1)} custom-call(bf16[2,64,2048]{2,1,0:T(8,128)(2,1)} %bitcast.115), custom_call_target="tpu_custom_call" | custom-call | tf_op jit(solution)/shard_map/pallas_call | solution.py:238
  388.3 209.4 %shard_map.300 = (bf16[2,2,64,4224]{3,2,1,0:T(8,128)(2,1)}, bf16[2048,2048]{1,0:T(8,128)(2,1)}, bf16[2048,2048]{1,0:T(8,128)(2,1)}, bf16[2048,704]{1,0:T(8,128)(...) custom-call(bf16[16,256,2048]{2,1,0:T(8,128)(2,1)} %bitcast.98, ...), custom_call_target="tpu_custom_call" | custom-call | flops 65000001536 | bytes 80000000 | tf_op jit(solution)/shard_map/pallas_call | solution.py:765
  597.8 2.3 slice.107.home
  600.1 2.1 convert_bitcast_fusion
  602.2 0.4 copy.170
  602.8 1.3 copy.176
  604.1 4.8 all-to-all-start.1
  608.9 11.3 %convolution_bitcast_fusion.2 = f32[1,2048,704]{1,2,0:T(8,128)} fusion(bf16[2048,2048]{1,0:T(8,128)(2,1)} %get-tuple-element.67, bf16[2048,704]{1,0:T(8,128)(2,1)} %get-tuple-element.68), kind=kOutput, calls=%fused_computation.2 | convolution fusion | flops 5905580032 | bytes 17039360 | tf_op jit(solution)/shard_map/dot_general | solution.py:67
  620.2 10.3 %convolution_bitcast_fusion = f32[1,704,2048]{2,1,0:T(8,128)} fusion(bf16[2048,704]{1,0:T(8,128)(2,1)S(1)} %copy-done.11, bf16[2048,2048]{1,0:T(8,128)(2,1)} %get-tuple-element.71), kind=kOutput, calls=%fused_computation | convolution fusion | flops 5905580032 | bytes 17039360 | tf_op jit(solution)/shard_map/dot_general | solution.py:67
  630.5 55.6 %shard_map.301 = (f32[256,2048]{1,0:T(8,128)}, bf16[2048,3200]{1,0:T(8,128)(2,1)}, bf16[16,4,32,512]{3,2,1,0:T(8,128)(2,1)}) custom-call(bf16[16,4,32,3712]{3,2,1,0:T(8,128)(2,1)} %bitcast.138, bf16[2048,3712]{1,0:T(8,128)(2,1)} %bitcast.137, bf16[256,2176]{1,0:T(8,128)(2,1)} %slice.107.home, bf16[256,2048]{1,0:T(8,128)(2,1)} %grad.1, ...), custom_call_target="tpu_custom_call" | custom-call | flops 24999999488 | bytes 70000000 | tf_op jit(solution)/shard_map/pallas_call | solution.py:1107
  686.2 2.6 add_convert_fusion
  688.8 10.4 %convolution_bitcast_fusion.1 = f32[1,2048,704]{1,2,0:T(8,128)} fusion(bf16[2048,2048]{1,0:T(8,128)(2,1)} %get-tuple-element.67, bf16[2048,704]{1,0:T(8,128)(2,1)S(1)} %copy-done.12), kind=kOutput, calls=%fused_computation.1 | convolution fusion | flops 5905580032 | bytes 17039360 | tf_op jit(solution)/shard_map/dot_general | solution.py:67
  699.4 153.6 %shard_map.302 = f32[2,64,3712]{2,1,0:T(8,128)} custom-call(bf16[16,2,64,3200]{3,2,1,0:T(8,128)(2,1)} %bitcast.99, bf16[16,2,64,512]{3,2,1,0:T(8,128)(2,1)} %bitcast.118), custom_call_target="tpu_custom_call" | custom-call | tf_op jit(solution)/shard_map/pallas_call | solution.py:384
  853.0 0.9 slice.113
  853.9 1.6 slice.117
  855.5 1.7 fusion.9
  857.1 1.0 slice.112
  858.1 1.9 fusion.11
  860.1 0.6 copy.164
  860.7 1.5 copy.167
  862.2 1.4 copy.166
  863.6 1.4 copy.161
  865.0 0.9 copy.163
  865.9 1.0 copy.165
  866.9 1.1 copy.152
  868.0 0.8 copy.171
  868.8 0.8 copy.162
  869.8 1.0 pad_maximum_fusion.1
  870.9 1.1 copy.156
  872.0 1.2 slice_bitcast_fusion
  873.3 2.4 copy.158
  875.6 1.1 copy.157
  876.8 1.3 copy.179
  (59 shorter events, 3.3 us)
Async XLA Ops:
  0.6 6.8 copy-start.9
  0.7 6.9 copy-start.7
  0.7 7.1 copy-start.4
  0.7 7.3 copy-start.5
  8.8 206.6 %copy-start.6 = (bf16[1408,128]{1,0:T(8,128)(2,1)S(1)}, bf16[1408,128]{1,0:T(8,128)(2,1)}, u32[]{:S(2)}) copy-start(bf16[1408,128]{1,0:T(8,128)(2,1)} %param.32) | copy-start | bytes 1081348
  216.6 61.3 %all-to-all-start = ((bf16[16,3,88,128]{3,2,1,0:T(8,128)(2,1)}), bf16[16,3,88,128]{3,2,1,0:T(8,128)(2,1)S(1)}, u32[]{:S(2)}, u32[]{:S(2)}) async-start(bf16[16,3,88,128]{3,2,1,0:T(8,128)(2,1)} %copy.139), calls=%async_computation | async-start | bytes 2162688 | tf_op jit(solution)/shard_map/all_to_all | solution.py:1141
  240.0 2.9 copy-start.10
  278.1 1.9 copy-start.8
  604.1 95.1 %all-to-all-start.1 = ((bf16[16,3,88,128]{3,2,1,0:T(8,128)(2,1)}), bf16[16,3,88,128]{3,2,1,0:T(8,128)(2,1)S(1)}, u32[]{:S(2)}, u32[]{:S(2)}) async-start(bf16[16,3,88,128]{3,2,1,0:T(8,128)(2,1)} %bitcast.96), calls=%async_computation.1 | async-start | bytes 2162688 | tf_op jit(solution)/shard_map/all_to_all | solution.py:1141
  608.9 11.3 %copy-start.11 = (bf16[2048,704]{1,0:T(8,128)(2,1)S(1)}, bf16[2048,704]{1,0:T(8,128)(2,1)}, u32[]{:S(2)}) copy-start(bf16[2048,704]{1,0:T(8,128)(2,1)} %get-tuple-element.70) | copy-start | bytes 8650756
  630.5 55.6 %copy-start.2 = (f32[256,2048]{1,0:T(8,128)S(1)}, f32[256,2048]{1,0:T(8,128)}, u32[]{:S(2)}) copy-start(f32[256,2048]{1,0:T(8,128)} %get-tuple-element.46.middle) | copy-start | bytes 6291460
  686.2 2.6 copy-start.12
  853.0 7.0 copy-start
  865.9 2.9 copy-start.3
  873.2 3.5 copy-start.1

commit v4 on v3

--- a/solution.py
+++ b/solution.py
@@ -113,14 +113,11 @@
         )
 
     class Part:
-        def __init__(self, at, cut):
+        def __init__(self, at, rows):
             self.share = kinds[at]
             self.x, self.o, self.hbm = ins[at], lands[at], outs[at]
-            rows = self.x.shape[1] // cuts[at]
-            self.rows = pl.ds(cut * rows, rows)
-            self.zs, self.zr, self.xs, self.xr, self.ys, self.yr, self.cs, self.cr, self.own, self.out = (
-                s.at[cut] for s in sems[10 * at : 10 * at + 10]
-            )
+            self.rows = rows
+            self.zs, self.zr, self.xs, self.xr, self.ys, self.yr, self.cs, self.cr, self.own, self.out = sems[20 * at + 10 : 20 * at + 20]
             self.slot = core if self.share else 0
             self.copy = pltpu.make_async_copy(self.x.at[:, self.rows], self.whole(me), self.own)
 
@@ -204,15 +201,121 @@
                 for b in range(16):
                     self.twin(b).wait_send()
 
-    groups = [[Part(at, cut) for cut in range(cuts[at])] for at in range(n)]
+    class Cross:
+        def __init__(self, at, rows):
+            self.share = kinds[at]
+            self.x, self.o, self.hbm = ins[at], lands[at], outs[at]
+            self.rows = rows
+            self.fs, self.fr, self.zs, self.zr, self.ls, self.lr, self.cs, self.cr, self.own, self.out = sems[20 * at : 20 * at + 10]
+            self.slot = core if self.share else 0
+            self.copy = pltpu.make_async_copy(self.x.at[:, rows], self.o.at[me, self.slot, :, rows], self.own)
+
+        def ref(self, b, half):
+            return self.o.at[b, self.slot, half, self.rows]
+
+        def block(self, zp, half, p):
+            if half == 0:
+                return zp * 4 + y * 2 + (x if p == 0 else 1 - x)
+            return zp * 4 + (y if p == 0 else 1 - y) * 2 + x
+
+        def hop(self, half):
+            r = self.ref(me, half)
+            return rc(r, r, self.fs.at[half], self.fr.at[half], xn if half == 0 else yn, core)
+
+        def line(self, zp, half, p, d):
+            r = self.ref(self.block(zp, half, p), half)
+            return rc(r, r, self.zs.at[d, zp, half, p], self.zr.at[zp, half, p], up if d == 0 else dn, core)
+
+        def last(self, zp, half, p):
+            r = self.ref(self.block(zp, half, p), half)
+            return rc(r, r, self.ls.at[zp, half, p], self.lr.at[zp, half, p], yn if half == 0 else xn, core)
+
+        def twin(self, b, half):
+            r = self.ref(b, half)
+            return rc(r, r, self.cs.at[b, half], self.cr.at[b, half], me, 1 - core)
+
+        def pass_on(self, zp, half, p):
+            pl.when((zp <= z) & (z < 3))(lambda: self.line(zp, half, p, 0).start())
+            pl.when((zp >= z) & (z > 0))(lambda: self.line(zp, half, p, 1).start())
+            self.last(zp, half, p).start()
+            if self.share:
+                self.twin(self.block(zp, half, p), half).start()
+
+        def first(self, k):
+            zp = plane_at(z, k)
+            if k == 0:
+                for half in range(2):
+                    self.hop(half).start()
+                for half in range(2):
+                    self.pass_on(zp, half, 0)
+                for half in range(2):
+                    self.hop(half).wait_recv()
+                    self.pass_on(zp, half, 1)
+            else:
+                for p in range(2):
+                    for half in range(2):
+                        self.line(zp, half, p, 0).wait_recv()
+                        self.pass_on(zp, half, p)
+
+        def second(self, k):
+            pass
+
+        def third(self, k):
+            zp = plane_at(z, k)
+            for p in range(2):
+                for half in range(2):
+                    self.last(zp, half, p).wait_recv()
+                    if self.share:
+                        far = zp * 4 + (1 - y) * 2 + (x if p == 0 else 1 - x)
+                        if half == 1:
+                            far = zp * 4 + (y if p == 0 else 1 - y) * 2 + (1 - x)
+                        self.twin(far, half).start()
+
+        def save(self, k):
+            at = pl.ds(plane_at(z, k) * 4, 4)
+            return pltpu.make_async_copy(
+                self.o.at[at, :, :, self.rows], self.hbm.at[at, :, :, self.rows], self.out.at[k]
+            )
+
+        def fourth(self, k):
+            if self.share:
+                for q in range(4):
+                    b = plane_at(z, k) * 4 + q
+                    for half in range(2):
+                        src, dst = self.o.at[b, core, half, self.rows], self.o.at[b, 1 - core, half, self.rows]
+                        rc(src, dst, self.cs.at[b, half], self.cr.at[b, half], me, 1 - core).wait_recv()
+            self.save(k).start()
+
+        def end(self):
+            for half in range(2):
+                self.hop(half).wait_send()
+            for k in range(4):
+                self.save(k).wait()
+                for half in range(2):
+                    for p in range(2):
+                        pl.when((k <= z) & (z < 3))(lambda k=k, h=half, p=p: self.line(k, h, p, 0).wait_send())
+                        pl.when((k >= z) & (z > 0))(lambda k=k, h=half, p=p: self.line(k, h, p, 1).wait_send())
+                        self.last(k, half, p).wait_send()
+            if self.share:
+                for b in range(16):
+                    for half in range(2):
+                        self.twin(b, half).wait_send()
+
+    groups = []
+    for at in range(n):
+        height = ins[at].shape[1]
+        group = [Cross(at, pl.ds(0, cuts[at]))] if cuts[at] > 0 else []
+        if cuts[at] < height:
+            group.append(Part(at, pl.ds(cuts[at], height - cuts[at])))
+        groups.append(group)
     parts = [p for g in groups for p in g]
     for p in parts:
         p.copy.start()
     pl.semaphore_wait(bar, 3 + (z < 3).astype(jnp.int32) + (z > 0).astype(jnp.int32))
     for p in parts:
         p.copy.wait()
-    turns = [(p, k) for g in groups for k in range(4) for p in g]
-    lag = max(cuts)
+    turns = [(p, k) for k in range(4) for p in parts]
+    lag = len(parts)
     for t in range(len(turns) + lag):
         if t < len(turns):
             turns[t][0].first(turns[t][1])
@@ -232,8 +335,11 @@
 def ag16(arrays, kinds, cid, cuts=None):
     S = pltpu.SemaphoreType.DMA
     any_ = pl.BlockSpec(memory_space=pl.ANY)
-    cuts = cuts or (1,) * len(arrays)
-    counts = ((8,), (4,), (4, 3), (4, 3), (4, 3), (4, 3), (16,), (16,), (), (4,))
+    cuts = cuts or tuple(v.shape[1] // 2 for v in arrays)
+    counts = (
+        ((2,), (2,), (2, 4, 2, 2), (4, 2, 2), (4, 2, 2), (4, 2, 2), (16, 2), (16, 2), (), (4,))
+        + ((8,), (4,), (4, 3), (4, 3), (4, 3), (4, 3), (16,), (16,), (), (4,))
+    )
     shapes = [(16, 2 if share else 1) + v.shape for v, share in zip(arrays, kinds)]
     return pl.pallas_call(
         functools.partial(ag_kernel, kinds, cuts),
@@ -241,7 +347,7 @@
         in_specs=[any_] * len(arrays),
         out_specs=[any_] * len(arrays),
         scratch_shapes=[pltpu.VMEM(s, v.dtype) for s, v in zip(shapes, arrays)]
-        + [S((c,) + s) for c in cuts for s in counts],
+        + [S(s) for _ in arrays for s in counts],
         compiler_params=pltpu.CompilerParams(collective_id=cid, has_side_effects=True, vmem_limit_bytes=60 << 20),
     )(*arrays)
 
@@ -255,7 +361,7 @@
     lax.fori_loop(0, dst.shape[0] // 16, step, 0)
 
 
-def rs_kernel(a_ref, b_ref, o_ref, own, yr, xr, zr, lsem, xs, xrs, ys, yrs, zs, zrs):
+def rs_kernel(a_ref, b_ref, o_ref, own, fr, zr, lr, yr, xr, z2r, lsem, fs, frs, zs, zrs, ls, lrs, xs, xrs, ys, yrs, z2s, z2rs):
     me = lax.axis_index("dp")
     core = lax.axis_index("tensor")
     z = me // 4
@@ -266,6 +372,8 @@
     up = jnp.minimum(z + 1, 3) * 4 + y * 2 + x
     dn = jnp.maximum(z - 1, 0) * 4 + y * 2 + x
     wide = a_ref.shape[3]
+    cut = fr.shape[3]
+    crossing, rest = pl.ds(0, cut), pl.ds(cut, own.shape[2] - cut)
 
     def rc(src, dst, ss, rs, dev):
         return pltpu.make_async_remote_copy(
@@ -293,53 +401,89 @@
     pl.when(z > 0)(lambda: sig(dn))
     pl.semaphore_wait(bar, 2 + (z < 3).astype(jnp.int32) + (z > 0).astype(jnp.int32))
 
-    def y_(j, b, half, zp):
-        return rc(own.at[b, half], yr.at[zp, j], ys.at[zp, j], yrs.at[zp, j], yn)
-
-    def x_(j, b, half, zp):
-        return rc(own.at[b, half], xr.at[zp, j], xs.at[zp, j], xrs.at[zp, j], xn)
-
-    def zc(zp, dev, d):
-        return rc(own.at[zp * 4 + y * 2 + x], zr.at[d, zp], zs.at[zp], zrs.at[d, zp], dev)
-
     def blk(zp, yy, xx):
         return zp * 4 + yy * 2 + xx
+
+    def place(zp, half, p):
+        if half == 0:
+            return blk(zp, y, x if p == 0 else 1 - x)
+        return blk(zp, y if p == 0 else 1 - y, x)
+
+    def hop(zp, half, p):
+        b = blk(zp, 1 - y, x if p == 0 else 1 - x) if half == 0 else blk(zp, y if p == 0 else 1 - y, 1 - x)
+        return rc(
+            own.at[b, half, crossing], fr.at[zp, half, p], fs.at[zp, half, p], frs.at[zp, half, p], yn if half == 0 else xn
+        )
+
+    def line(zp, half, p, dev, slot):
+        b = place(zp, half, p)
+        return rc(own.at[b, half, crossing], zr.at[slot, half, p], zs.at[zp, half, p], zrs.at[slot, half, p], dev)
+
+    def last(half):
+        b = place(z, half, 1)
+        return rc(own.at[b, half, crossing], lr.at[half], ls.at[half], lrs.at[half], xn if half == 0 else yn)
+
+    def y_(j, b, half, zp):
+        return rc(own.at[b, half, rest], yr.at[zp, j], ys.at[zp, j], yrs.at[zp, j], yn)
+
+    def x_(j, b, half, zp):
+        return rc(own.at[b, half, rest], xr.at[zp, j], xs.at[zp, j], xrs.at[zp, j], xn)
+
+    def zc(zp, dev, d):
+        return rc(own.at[zp * 4 + y * 2 + x, :, rest], z2r.at[d, zp], z2s.at[zp], z2rs.at[d, zp], dev)
 
     def s1(k):
         zp = plane_at(z, 3 - k)
         for c in loads(zp):
             c.wait()
+        for p in range(2):
+            for half in range(2):
+                hop(zp, half, 1 - p).start()
         y_(0, blk(zp, 1 - y, 1 - x), 0, zp).start()
         x_(0, blk(zp, 1 - y, 1 - x), 1, zp).start()
         y_(1, blk(zp, 1 - y, x), 0, zp).start()
         x_(1, blk(zp, y, 1 - x), 1, zp).start()
 
+    def arrive(zp, half, p, slot):
+        line(zp, half, p, me, slot).wait_recv()
+        add_into(own.at[place(zp, half, p), half, crossing], zr.at[slot, half, p])
+
     def s2(k):
         zp = plane_at(z, 3 - k)
+        for p in (1, 0):
+            for half in range(2):
+                hop(zp, half, p).wait_recv()
+                add_into(own.at[place(zp, half, p), half, crossing], fr.at[zp, half, p])
+                pl.when((zp <= z) & (z < 3))(lambda h=half, p=p: arrive(zp, h, p, jnp.where(zp == z, 4, zp)))
+                pl.when((zp >= z) & (z > 0))(lambda h=half, p=p: arrive(zp, h, p, zp))
+                pl.when(zp < z)(lambda h=half, p=p: line(zp, h, p, dn, jnp.where(zp == z - 1, 4, zp)).start())
+                pl.when(zp > z)(lambda h=half, p=p: line(zp, h, p, up, zp).start())
+                if k == 3 and p == 1:
+                    last(half).start()
         mine = blk(zp, y, x)
         y_(0, blk(zp, 1 - y, 1 - x), 0, zp).wait_recv()
-        add_into(own.at[blk(zp, y, 1 - x), 0], yr.at[zp, 0])
+        add_into(own.at[blk(zp, y, 1 - x), 0, rest], yr.at[zp, 0])
         x_(2, blk(zp, y, 1 - x), 0, zp).start()
         x_(0, blk(zp, 1 - y, 1 - x), 1, zp).wait_recv()
-        add_into(own.at[blk(zp, 1 - y, x), 1], xr.at[zp, 0])
+        add_into(own.at[blk(zp, 1 - y, x), 1, rest], xr.at[zp, 0])
         y_(2, blk(zp, 1 - y, x), 1, zp).start()
         y_(1, blk(zp, 1 - y, x), 0, zp).wait_recv()
-        add_into(own.at[mine, 0], yr.at[zp, 1])
+        add_into(own.at[mine, 0, rest], yr.at[zp, 1])
         x_(1, blk(zp, y, 1 - x), 1, zp).wait_recv()
-        add_into(own.at[mine, 1], xr.at[zp, 1])
+        add_into(own.at[mine, 1, rest], xr.at[zp, 1])
 
     def s3(k):
         zp = plane_at(z, 3 - k)
         mine = blk(zp, y, x)
         x_(2, blk(zp, y, 1 - x), 0, zp).wait_recv()
-        add_into(own.at[mine, 0], xr.at[zp, 2])
+        add_into(own.at[mine, 0, rest], xr.at[zp, 2])
         y_(2, blk(zp, 1 - y, x), 1, zp).wait_recv()
-        add_into(own.at[mine, 1], yr.at[zp, 2])
+        add_into(own.at[mine, 1, rest], yr.at[zp, 2])
 
         def arrived(d):
             zc(zp, me, d).wait_recv()
-            add_into(own.at[mine, 0], zr.at[d, zp, 0])
-            add_into(own.at[mine, 1], zr.at[d, zp, 1])
+            add_into(own.at[mine, 0, rest], z2r.at[d, zp, 0])
+            add_into(own.at[mine, 1, rest], z2r.at[d, zp, 1])
 
         pl.when((zp <= z) & (z < 3))(lambda: arrived(1))
         pl.when((zp >= z) & (z > 0))(lambda: arrived(0))
@@ -358,6 +502,9 @@
     s2(3)
     s3(2)
     s3(3)
+    for half in range(2):
+        last(half).wait_recv()
+        add_into(own.at[me, half, crossing], lr.at[half])
     for a in range(2):
 
         def row(i, _):
@@ -366,20 +513,24 @@
             return 0
 
         lax.fori_loop(0, o_ref.shape[1] // 16, row, 0)
+    for half in range(2):
+        last(half).wait_send()
     for k in range(4):
+        for half in range(2):
+            for p in range(2):
+                hop(k, half, p).wait_send()
+                pl.when(k != z)(lambda k=k, h=half, p=p: line(k, h, p, me, 0).wait_send())
         for j in range(3):
             x_(j, 0, 0, k).wait_send()
             y_(j, 0, 0, k).wait_send()
-
-        @pl.when(k != z)
-        def _():
-            zc(k, up, 0).wait_send()
+        pl.when(k != z)(lambda k=k: zc(k, up, 0).wait_send())
 
 
 def rs16(a, b, cid):
     S = pltpu.SemaphoreType.DMA
-    half = (a.shape[2], a.shape[3] + b.shape[3])
-    blkshape = (2,) + half
+    high, total = a.shape[2], a.shape[3] + b.shape[3]
+    blkshape = (2, high, total)
+    cross, half = (high // 2, total), (high - high // 2, total)
     V = lambda s: pltpu.VMEM(s, a.dtype)
     return pl.pallas_call(
         rs_kernel,
@@ -387,8 +538,10 @@
         in_specs=[pl.BlockSpec(memory_space=pl.ANY)] * 2,
         out_specs=pl.BlockSpec(memory_space=pltpu.VMEM),
         scratch_shapes=[
-            V((16,) + blkshape), V((4, 3) + half), V((4, 3) + half), V((2, 4) + blkshape),
-            S((4, 2)), S((4, 3)), S((4, 3)), S((4, 3)), S((4, 3)), S((4,)), S((2, 4)),
+            V((16,) + blkshape), V((4, 2, 2) + cross), V((5, 2, 2) + cross), V((2,) + cross),
+            V((4, 3) + half), V((4, 3) + half), V((2, 4, 2) + half),
+            S((4, 2)), S((4, 2, 2)), S((4, 2, 2)), S((4, 2, 2)), S((5, 2, 2)), S((2,)), S((2,)),
+            S((4, 3)), S((4, 3)), S((4, 3)), S((4, 3)), S((4,)), S((2, 4)),
         ],
         compiler_params=pltpu.CompilerParams(collective_id=cid, has_side_effects=True, vmem_limit_bytes=60 << 20),
     )(a, b)
@@ -541,7 +694,7 @@
             e, axis=1, keepdims=True
         )
         pre = nt(rg[...], wd[...])
-        act, d_a, d_b = gate_parts(mm(rr[...], wg[...]), mm(rr[...], wu[...]), gate * pre)
+        act, d_a, d_b = gate_parts(nt(rr[...], wg[...]), nt(rr[...], wu[...]), gate * pre)
         low = act.astype(jnp.bfloat16)
         back = low.astype(jnp.float32)
         d_gate = jnp.sum(back * pre, axis=1, keepdims=True)
@@ -551,7 +704,7 @@
 
         def spread(n):
             o = (gate * mm(low, wd[:, n])).astype(jnp.bfloat16)
-            s = (nt(das[...], wg[n]) + nt(dbs[...], wu[n])).astype(jnp.bfloat16)
+            s = (mm(das[...], wg[:, n]) + mm(dbs[...], wu[:, n])).astype(jnp.bfloat16)
             for q in range(2):
                 ry[q, :hid, n] = o[q * hid : (q + 1) * hid]
                 rd[q, :hid, n] = s[q * hid : (q + 1) * hid]
@@ -755,7 +908,7 @@
 
 
 def moe_call(moe, grd, pick, pick_t, wg, wu, wd, wr, sgu, sdn, cid):
-    width, ffe = wg.shape
+    ffe, width = wg.shape
     total = 2 * width + 128
     slots = pick.shape[0] * pick.shape[1]
     low, S, V = jnp.bfloat16, pltpu.SemaphoreType.DMA, pltpu.VMEM
@@ -830,7 +983,7 @@
 def att_fwd_kernel(
     tok, w4, w2, g_att, g_moe, g_lat, cos, sin, bias,
     middle, moe_low, normed, lat_raw, qcat, keys, kv_out, lse, att,
-    kv, wq, wo, wkv, wlat, part, arrived, w_sem, kv_sem, ks, kr, cs, cr,
+    kv, wq, wo, wkv, wlat, part, arrived, w_sem, kv_sem, ks, kr, ts, tr, cs, cr,
 ):
     me = lax.axis_index("dp")
     core = lax.axis_index("tensor")
@@ -850,10 +1003,25 @@
     keys[SLOTS - 1, :, :RANK] = (first * root(first) * g_lat[...]).astype(jnp.bfloat16)
     keys[SLOTS - 1, :, RANK:] = (rot + pltpu.roll(rot, 64, 1)).astype(jnp.bfloat16)
 
+    mine = pl.ds(pl.multiple_of(core * 128, 128), 128)
+
     def send(d):
         return pltpu.make_async_remote_copy(
-            src_ref=keys.at[SLOTS - 1], dst_ref=keys.at[SLOTS - 1 - d], send_sem=ks.at[d - 1], recv_sem=kr.at[d - 1],
-            device_id=(jnp.minimum(me + d, 15), core), device_id_type=MESH,
+            src_ref=keys.at[SLOTS - 1, mine], dst_ref=keys.at[SLOTS - 1 - d, mine], send_sem=ks.at[d - 1],
+            recv_sem=kr.at[d - 1], device_id=(jnp.minimum(me + d, 15), core), device_id_type=MESH,
+        )
+
+    def hand(d):
+        return pltpu.make_async_remote_copy(
+            src_ref=keys.at[SLOTS - 1 - d, mine], dst_ref=keys.at[SLOTS - 1 - d, mine], send_sem=ts.at[d - 1],
+            recv_sem=tr.at[d - 1], device_id=(me, 1 - core), device_id_type=MESH,
+        )
+
+    def handed(d):
+        other = keys.at[SLOTS - 1 - d, pl.ds(pl.multiple_of((1 - core) * 128, 128), 128)]
+        return pltpu.make_async_remote_copy(
+            src_ref=other, dst_ref=other, send_sem=ts.at[d - 1], recv_sem=tr.at[d - 1],
+            device_id=(me, 1 - core), device_id_type=MESH,
         )
 
     for d in range(1, SLOTS):
@@ -873,10 +1041,21 @@
         qcat[h, :, 128:] = jnp.where(half == (h % 2 == 0), pair, 0.0).astype(jnp.bfloat16)
     for c in loads[3:]:
         c.wait()
-    for s in range(SLOTS - 1, -1, -1):
-        if s < SLOTS - 1:
-            pl.when(me >= SLOTS - 1 - s)(lambda s=s: send(SLOTS - 1 - s).wait_recv())
+    def project(s):
         kv[s * 256 : (s + 1) * 256] = mm(keys[s, :, :RANK], wkv[...].reshape(RANK, 2048)).astype(jnp.bfloat16)
+
+    project(SLOTS - 1)
+    for d in range(1, SLOTS + 1):
+        if d < SLOTS:
+
+            @pl.when(me >= d)
+            def _(d=d):
+                send(d).wait_recv()
+                hand(d).start()
+
+        if d > 1:
+            pl.when(me >= d - 1)(lambda d=d: handed(d - 1).wait_recv())
+            project(SLOTS - d)
     save = pltpu.make_async_copy(kv, kv_out, kv_sem)
     save.start()
 
@@ -913,6 +1092,7 @@
     save.wait()
     for d in range(1, SLOTS):
         pl.when(me + d < 16)(lambda d=d: send(d).wait_send())
+        pl.when(me >= d)(lambda d=d: hand(d).wait_send())
 
 
 def att_fwd(tok, weights, g_att, g_moe, g_lat, cos, sin, bias, cid):
@@ -932,7 +1112,7 @@
         out_specs=[vmem] * 6 + [any_] + [vmem] * 2,
         scratch_shapes=[
             V((KEYS, 2048), low), V((width, 1536), low), V((width, 1024), low), V((16, 32, 2048), low), V((width, 640), low),
-            V((rows, width), low), V((rows, width), low), S((7,)), S, S((4,)), S((4,)), S, S,
+            V((rows, width), low), V((rows, width), low), S((7,)), S, S((4,)), S((4,)), S((4,)), S((4,)), S, S,
         ],
         compiler_params=pltpu.CompilerParams(collective_id=cid, has_side_effects=True, vmem_limit_bytes=60 << 20),
         cost_estimate=pl.CostEstimate(flops=10**10, bytes_accessed=40 * 10**6, transcendentals=0),
@@ -943,8 +1123,8 @@
     w4, w2, home, grad, middle, moe_low, tok, normed, lat_raw, qcat, keys, kv_in, lse, att, wr,
     g_att, g_moe, g_lat, cos, sin, bias,
     tok_grad, packed, p4,
-    kv, wq, wo, wkv, wlat, dmid, dnorm, dmid_low, d_att, dq, dqr, dkr, dk_out, dk_in, own_dk, part, arrived,
-    w_sem, kv_sem, ks, kr, cs, cr, o_sem,
+    kv, wq, wo, wkv, wlat, dmid, dnorm, dmid_low, d_att, dq, dqr, dkr, dk_out, dk_pair, dk_in, own_dk, part, arrived, d_keys,
+    w_sem, kv_sem, ks, kr, cs, cr, ps, pr, hs, hr, o_sem,
 ):
     me = lax.axis_index("dp")
     core = lax.axis_index("tensor")
@@ -1022,24 +1202,24 @@
     for n in (3, 4, 5, 6):
         loads[n].wait()
 
-    def send(d):
+    mine = pl.ds(pl.multiple_of(core * 128, 128), 128)
+    others = pl.ds(pl.multiple_of((1 - core) * 128, 128), 128)
+
+    def send(d, to):
         return pltpu.make_async_remote_copy(
-            src_ref=dk_out.at[d - 1], dst_ref=dk_in.at[d - 1], send_sem=ks.at[d - 1], recv_sem=kr.at[d - 1],
-            device_id=(jnp.maximum(me - d, 0), core), device_id_type=MESH,
+            src_ref=dk_out.at[d - 1, mine], dst_ref=dk_in.at[d - 1], send_sem=ks.at[d - 1], recv_sem=kr.at[d - 1],
+            device_id=(jnp.clip(to, 0, 15), core), device_id_type=MESH,
         )
 
+    pair = pltpu.make_async_remote_copy(
+        src_ref=dk_out.at[:, others], dst_ref=dk_pair, send_sem=ps, recv_sem=pr, device_id=(me, 1 - core), device_id_type=MESH
+    )
     for s in range(SLOTS):
         r = slice(s * 256, (s + 1) * 256)
-        d_lat = nt(kv[r], wkv[...].reshape(RANK, 2048))
-        d_rope = dkr[r] + pltpu.roll(dkr[r], 64, 1)
-        if s == SLOTS - 1:
-            own_dk[:, :RANK] = d_lat
-            own_dk[:, RANK:] = d_rope
-        else:
-            d = SLOTS - 1 - s
-            dk_out[d - 1, :, :RANK] = d_lat.astype(jnp.bfloat16)
-            dk_out[d - 1, :, RANK:] = d_rope.astype(jnp.bfloat16)
-            pl.when(me >= d)(lambda d=d: send(d).start())
+        d = SLOTS - 1 - s if s < SLOTS - 1 else SLOTS
+        dk_out[d - 1, :, :RANK] = nt(kv[r], wkv[...].reshape(RANK, 2048)).astype(jnp.bfloat16)
+        dk_out[d - 1, :, RANK:] = (dkr[r] + pltpu.roll(dkr[r], 64, 1)).astype(jnp.bfloat16)
+    pair.start()
     dq[:, 1024:] = turned(dqr[...], cos[...], -sin[...]).astype(jnp.bfloat16)
     loads[1].wait()
 
@@ -1050,7 +1230,17 @@
         wq[r] = tn(normed[:, r], dq[...]).astype(jnp.bfloat16)
         return 0
 
-    lax.fori_loop(0, 4, normed_cols, 0)
+    normed_cols(0, 0)
+    pair.wait_recv()
+    for d in range(1, SLOTS):
+        dk_out[d - 1, mine] = dk_out[d - 1, mine] + dk_pair[d - 1]
+        pl.when(me >= d)(lambda d=d: send(d, me - d).start())
+    own_dk[...] = dk_out[SLOTS - 1, mine].astype(jnp.float32) + dk_pair[SLOTS - 1].astype(jnp.float32)
+    lax.fori_loop(1, 4, normed_cols, 0)
+    swap = pltpu.make_async_remote_copy(
+        src_ref=part, dst_ref=arrived, send_sem=cs, recv_sem=cr, device_id=(me, 1 - core), device_id_type=MESH
+    )
+    swap.start()
     stores[1].start()
     latent_all = keys[:, :, :RANK].reshape(KEYS, RANK)
     for c in range(4):
@@ -1061,23 +1251,24 @@
 
         @pl.when(me + d < 16)
         def _():
-            pltpu.make_async_remote_copy(
-                src_ref=dk_out.at[d - 1], dst_ref=dk_in.at[d - 1], send_sem=ks.at[d - 1], recv_sem=kr.at[d - 1],
-                device_id=(jnp.minimum(me + d, 15), core), device_id_type=MESH,
-            ).wait_recv()
+            send(d, me + d).wait_recv()
             own_dk[...] += dk_in[d - 1].astype(jnp.float32)
 
-    part[:, width:] = own_dk[...].astype(jnp.bfloat16)
-    swap = pltpu.make_async_remote_copy(
-        src_ref=part, dst_ref=arrived, send_sem=cs, recv_sem=cr, device_id=(me, 1 - core), device_id_type=MESH
-    )
-    swap.start()
-    swap.wait()
-    dnorm[...] = part[:, :width].astype(jnp.float32) + arrived[:, :width].astype(jnp.float32)
-    d_keys = part[:, width:].astype(jnp.float32) + arrived[:, width:].astype(jnp.float32)
-
-    d_first, lat_gain_rows = norm_back(lat_raw[:, :RANK], g_lat[...], d_keys[:, :RANK])
-    d_second = turned(d_keys[:, RANK:], cos[:, :128], -sin[:, :128])
+    d_keys[mine] = own_dk[...].astype(jnp.bfloat16)
+
+    def half(rows):
+        return pltpu.make_async_remote_copy(
+            src_ref=d_keys.at[rows], dst_ref=d_keys.at[rows], send_sem=hs, recv_sem=hr,
+            device_id=(me, 1 - core), device_id_type=MESH,
+        )
+
+    half(mine).start()
+    swap.wait_recv()
+    dnorm[...] = part[...].astype(jnp.float32) + arrived[...].astype(jnp.float32)
+    half(others).wait_recv()
+
+    d_first, lat_gain_rows = norm_back(lat_raw[:, :RANK], g_lat[...], d_keys[:, :RANK].astype(jnp.float32))
+    d_second = turned(d_keys[:, RANK:].astype(jnp.float32), cos[:, :128], -sin[:, :128])
     d_second = jnp.where(lane < 64, d_second, 0.0)
     d_lat_low = jnp.concatenate([d_first, d_second], 1).astype(jnp.bfloat16)
     loads[0].wait()
@@ -1095,7 +1286,10 @@
     for c in stores:
         c.wait()
     for d in range(1, SLOTS):
-        pl.when(me >= d)(lambda d=d: send(d).wait_send())
+        pl.when(me >= d)(lambda d=d: send(d, me - d).wait_send())
+    pair.wait_send()
+    swap.wait_send()
+    half(mine).wait_send()
 
 
 def att_bwd(weights, home, grad, middle, moe_low, tok, normed, lat_raw, qcat, keys, kv, lse, att, wr, g_att, g_moe, g_lat, cos, sin, bias, cid):
@@ -1112,9 +1306,9 @@
         scratch_shapes=[
             V((KEYS, 2048), low), V((width, 1536), low), V((width, 1024), low), V((16, 32, 2048), low),
             V((width, 640), low), V((rows, width), f32), V((rows, width), f32), V((rows, width), low), V((rows, 1024), low),
-            V((rows, 1536), low), V((rows, 512), f32), V((KEYS, 128), f32), V((4, rows, 640), low), V((4, rows, 640), low),
-            V((rows, 640), f32), V((rows, width + 640), low), V((rows, width + 640), low),
-            S((7,)), S, S((4,)), S((4,)), S, S, S((7,)),
+            V((rows, 1536), low), V((rows, 512), f32), V((KEYS, 128), f32), V((SLOTS, rows, 640), low), V((SLOTS, rows // 2, 640), low),
+            V((4, rows // 2, 640), low), V((rows // 2, 640), f32), V((rows, width), low), V((rows, width), low), V((rows, 640), low),
+            S((7,)), S, S((4,)), S((4,)), S, S, S, S, S, S, S((7,)),
         ],
         compiler_params=pltpu.CompilerParams(collective_id=cid, has_side_effects=True, vmem_limit_bytes=60 << 20),
         cost_estimate=pl.CostEstimate(flops=25 * 10**9, bytes_accessed=70 * 10**6, transcendentals=0),
@@ -1280,8 +1474,8 @@
         grad_all.reshape(dp_count, n_rows, width),
         pick,
         pick.transpose(0, 2, 1),
-        expert_gate[0],
-        routed_up_weight[0],
+        expert_gate[0].T,
+        routed_up_weight[0].T,
         expert_down[0],
         moe_wr,
         shared_in,

time: 887 us -> 803 us (0.905)
  Pallas kernels: 759 us -> 682 us
  local copies, waits for them, and re-layouts: 58.6 us -> 49.4 us
    pallas_call x2, Pallas kernels: 311 us -> 267 us  [ag16(): pl.pallas_call(functools.partial(ag_kernel, kinds, cuts), out_shape=[jax....]
    pallas_call x1, Pallas kernels: 154 us -> 115 us  [rs16(): pl.pallas_call(rs_kernel, out_shape=jax.ShapeDtypeStruct(blkshape, jnp.fl...]
    unnamed x47 -> x45, local copies, waits for them, and re-layouts: 28 us -> 18.8 us
  transfers between devices with their start and end apart: 2 -> 2, of which waited for: 0 -> 0; matrix products, arithmetic and copies ran while one was open for 7% -> 7% of each run, Pallas kernels for 10% -> 11%
where the time goes in v4:
time: 803 us; the launch traced here: 794 us
  Pallas kernels  682 us (85%)
  local copies, waits for them, and re-layouts  49.4 us (6%)
  matrix products  32.2 us (4%)
  other arithmetic  17.1 us (2%)
  starting transfers between devices  11.4 us (1%)
    pallas_call x2, Pallas kernels, ag16(): pl.pallas_call(functools.partial(ag_kernel, kinds, cuts), out_shape=[jax....  267 us
    pallas_call x1, Pallas kernels, moe_call(): pl.pallas_call(moe_kernel, out_shape=[shape(2, *blk), shape(slots, width)...  211 us
    pallas_call x1, Pallas kernels, rs16(): pl.pallas_call(rs_kernel, out_shape=jax.ShapeDtypeStruct(blkshape, jnp.fl...  115 us
    pallas_call x1, Pallas kernels, att_bwd(): pl.pallas_call(att_bwd_kernel, out_shape=[shape(f32, rows, width), shape(...  60.6 us
    dot_general x3, matrix products, matmul_tn(): lax.dot_general(left_mat, right_mat, (((0,), (0,)), ((), ())), preferred_...  32 us
    pallas_call x1, Pallas kernels, att_fwd(): pl.pallas_call(att_fwd_kernel, out_shape=[shape(f32, rows, width), shape(...  29.5 us
    unnamed x45, local copies, waits for them, and re-layouts  18.8 us
  transfers between devices with their start and end apart: 2, of which 0 were waited for; matrix products, arithmetic and copies ran while one was open for 7% of the time, Pallas kernels for 11%

profile of v4, /device:TPU:0, one launch (start us, length us, event | category | flops | bytes accessed | tf_op | source)
XLA Modules:
  0.0 793.9 jit_solution(3952342413721161560)
XLA Ops:
  0.7 1.3 copy.120
  2.1 0.7 convert_element_type.83
  2.8 0.7 pad.13
  3.4 0.2 concatenate.42
  3.6 0.9 concatenate.40
  4.5 0.9 concatenate.41
  5.4 0.8 copy.125
  6.5 0.9 copy.169
  7.8 0.2 copy.118
  8.8 1.9 constant_dynamic-slice_fusion.2
  10.8 1.1 concatenate.37.refs_0_
  11.9 181.1 %shard_map.297 = (bf16[16,1,2,64,3712]{4,3,2,1,0:T(8,128)(2,1)}, bf16[16,2,2,64,2048]{4,3,2,1,0:T(8,128)(2,1)}) custom-call(bf16[2,64,3712]{2,1,0:T(8,128)(2,1)} %concatenate.37.refs_0_, bf16[2,64,2048]{2,1,0:T(8,128)(2,1)} %bitcast.116), custom_call_target="tpu_custom_call" | custom-call | tf_op jit(solution)/shard_map/pallas_call | solution.py:344
  193.2 1.1 copy.133
  194.2 5.9 all-to-all-start
  200.2 1.4 slice_reduce_fusion
  201.6 2.6 convert_reduce_fusion
  204.2 1.4 convert_compare_fusion
  205.6 1.2 slice.87
  207.1 1.0 copy.132.sin
  208.2 1.0 copy.131.cos
  209.2 0.7 reshape.286.g_lat
  209.8 0.5 eq.50
  210.3 0.6 reduce_or.9
  211.1 0.9 pad.15.wr
  212.1 2.4 fusion.3.pick_t
  214.5 1.4 fusion.1.pick
  215.9 1.6 fusion.6.bias
  217.6 29.5 %shard_map.298 = (f32[256,2048]{1,0:T(8,128)}, bf16[256,2048]{1,0:T(8,128)(2,1)}, bf16[256,2048]{1,0:T(8,128)(2,1)}, f32[256,640]{1,0:T(8,128)}, bf16[8,256,256]...) custom-call(bf16[256,2048]{1,0:T(8,128)(2,1)} %tok.3, ...), custom_call_target="tpu_custom_call" | custom-call | flops 10000000000 | bytes 40000000 | tf_op jit(solution)/shard_map/pallas_call | solution.py:1104
  247.3 0.8 fusion.7.sdn
  248.1 1.1 pad_slice_fusion.1
  249.2 0.8 constant_dynamic-slice_fusion
  250.0 85.4 %shard_map.299 = bf16[16,2,2,64,2048]{4,3,2,1,0:T(8,128)(2,1)} custom-call(bf16[2,64,2048]{2,1,0:T(8,128)(2,1)} %bitcast.117), custom_call_target="tpu_custom_call" | custom-call | tf_op jit(solution)/shard_map/pallas_call | solution.py:344
  335.4 210.7 %shard_map.300 = (bf16[2,2,64,4224]{3,2,1,0:T(8,128)(2,1)}, bf16[2048,2048]{1,0:T(8,128)(2,1)}, bf16[2048,2048]{1,0:T(8,128)(2,1)}, bf16[2048,704]{1,0:T(8,128)(...) custom-call(bf16[16,256,2048]{2,1,0:T(8,128)(2,1)} %bitcast.102, ...), custom_call_target="tpu_custom_call" | custom-call | flops 65000001536 | bytes 80000000 | tf_op jit(solution)/shard_map/pallas_call | solution.py:918
  546.1 2.3 slice.107.home
  548.4 2.1 convert_bitcast_fusion
  550.6 0.4 copy.162
  551.2 1.3 copy.168
  552.4 5.5 all-to-all-start.1
  557.9 11.3 %convolution_bitcast_fusion.2 = f32[1,2048,704]{1,2,0:T(8,128)} fusion(bf16[2048,2048]{1,0:T(8,128)(2,1)} %get-tuple-element.67, bf16[2048,704]{1,0:T(8,128)(2,1)} %get-tuple-element.68), kind=kOutput, calls=%fused_computation.2 | convolution fusion | flops 5905580032 | bytes 17039360 | tf_op jit(solution)/shard_map/dot_general | solution.py:67
  569.2 10.3 %convolution_bitcast_fusion = f32[1,704,2048]{2,1,0:T(8,128)} fusion(bf16[2048,704]{1,0:T(8,128)(2,1)S(1)} %copy-done.11, bf16[2048,2048]{1,0:T(8,128)(2,1)} %get-tuple-element.71), kind=kOutput, calls=%fused_computation | convolution fusion | flops 5905580032 | bytes 17039360 | tf_op jit(solution)/shard_map/dot_general | solution.py:67
  579.6 60.6 %shard_map.301 = (f32[256,2048]{1,0:T(8,128)}, bf16[2048,3200]{1,0:T(8,128)(2,1)}, bf16[16,4,32,512]{3,2,1,0:T(8,128)(2,1)}) custom-call(bf16[16,4,32,3712]{3,2,1,0:T(8,128)(2,1)} %bitcast.140, bf16[2048,3712]{1,0:T(8,128)(2,1)} %bitcast.139, bf16[256,2176]{1,0:T(8,128)(2,1)} %slice.107.home, bf16[256,2048]{1,0:T(8,128)(2,1)} %grad.1, ...), custom_call_target="tpu_custom_call" | custom-call | flops 24999999488 | bytes 70000000 | tf_op jit(solution)/shard_map/pallas_call | solution.py:1301
  640.2 2.6 add_convert_fusion
  642.9 10.4 %convolution_bitcast_fusion.1 = f32[1,2048,704]{1,2,0:T(8,128)} fusion(bf16[2048,2048]{1,0:T(8,128)(2,1)} %get-tuple-element.67, bf16[2048,704]{1,0:T(8,128)(2,1)S(1)} %copy-done.12), kind=kOutput, calls=%fused_computation.1 | convolution fusion | flops 5905580032 | bytes 17039360 | tf_op jit(solution)/shard_map/dot_general | solution.py:67
  653.4 115.0 %shard_map.302 = f32[2,64,3712]{2,1,0:T(8,128)} custom-call(bf16[16,2,64,3200]{3,2,1,0:T(8,128)(2,1)} %bitcast.103, bf16[16,2,64,512]{3,2,1,0:T(8,128)(2,1)} %bitcast.120), custom_call_target="tpu_custom_call" | custom-call | tf_op jit(solution)/shard_map/pallas_call | solution.py:535
  768.4 0.9 slice.113
  769.3 1.6 slice.117
  770.8 1.7 fusion.9
  772.5 1.0 slice.112
  773.5 1.9 fusion.11
  775.5 0.6 copy.156
  776.1 1.5 copy.159
  777.6 1.4 copy.158
  779.0 1.4 copy.153
  780.4 0.9 copy.155
  781.3 1.0 copy.157
  782.3 1.1 copy.144
  783.4 0.8 copy.163
  784.2 0.8 copy.154
  785.2 1.0 pad_maximum_fusion.1
  786.2 1.1 copy.148
  787.4 1.2 slice_bitcast_fusion
  788.6 2.4 copy.150
  791.0 1.1 copy.149
  792.1 1.3 copy.171
  (57 shorter events, 2.9 us)
Async XLA Ops:
  0.6 6.8 copy-start.9
  0.7 6.9 copy-start.7
  0.7 7.1 copy-start.4
  0.7 7.3 copy-start.5
  8.8 184.2 %copy-start.6 = (bf16[1408,128]{1,0:T(8,128)(2,1)S(1)}, bf16[1408,128]{1,0:T(8,128)(2,1)}, u32[]{:S(2)}) copy-start(bf16[1408,128]{1,0:T(8,128)(2,1)} %param.32) | copy-start | bytes 1081348
  194.2 52.9 %all-to-all-start = ((bf16[16,3,88,128]{3,2,1,0:T(8,128)(2,1)}), bf16[16,3,88,128]{3,2,1,0:T(8,128)(2,1)S(1)}, u32[]{:S(2)}, u32[]{:S(2)}) async-start(bf16[16,3,88,128]{3,2,1,0:T(8,128)(2,1)} %copy.133), calls=%async_computation | async-start | bytes 2162688 | tf_op jit(solution)/shard_map/all_to_all | solution.py:1335
  208.1 3.9 copy-start.10
  247.3 1.9 copy-start.8
  552.4 100.8 %all-to-all-start.1 = ((bf16[16,3,88,128]{3,2,1,0:T(8,128)(2,1)}), bf16[16,3,88,128]{3,2,1,0:T(8,128)(2,1)S(1)}, u32[]{:S(2)}, u32[]{:S(2)}) async-start(bf16[16,3,88,128]{3,2,1,0:T(8,128)(2,1)} %bitcast.100), calls=%async_computation.1 | async-start | bytes 2162688 | tf_op jit(solution)/shard_map/all_to_all | solution.py:1335
  557.9 11.3 %copy-start.11 = (bf16[2048,704]{1,0:T(8,128)(2,1)S(1)}, bf16[2048,704]{1,0:T(8,128)(2,1)}, u32[]{:S(2)}) copy-start(bf16[2048,704]{1,0:T(8,128)(2,1)} %get-tuple-element.70) | copy-start | bytes 8650756
  579.6 60.6 %copy-start.2 = (f32[256,2048]{1,0:T(8,128)S(1)}, f32[256,2048]{1,0:T(8,128)}, u32[]{:S(2)}) copy-start(f32[256,2048]{1,0:T(8,128)} %get-tuple-element.46.middle) | copy-start | bytes 6291460
  640.2 2.6 copy-start.12
  768.3 7.0 copy-start
  781.3 2.9 copy-start.3
  788.6 3.5 copy-start.1

commit v5 on v4

--- a/solution.py
+++ b/solution.py
@@ -566,10 +566,10 @@
 
 
 def moe_kernel(
-    moe, grd, pick, pick_t, wg, wu, wd, wr, sgu, sdn,
+    moe, grd, pick, pick_t, wg_in, wu_in, wd_in, wr, sgu, sdn,
     o_out, r_out, rg_out, act_out, da_out, db_out, sg_out, yr, xr, zr,
-    own, sib, sibr, stage, xb, gb, pk, pt, rr, rg, ly, ld, ry, rd, acts, das, dbs, dgs,
-    in_sem, out_sem, st_sem, free, cs, cr, xs, xrs, ys, yrs, zs, zrs, fs, fr,
+    wg, wu, wd, own, sib, sibr, stage, xb, gb, pk, pt, rr, rg, ly, ld, ry, rd, acts, das, dbs, dgs,
+    w_sem, in_sem, out_sem, st_sem, free, cs, cr, xs, xrs, ys, yrs, zs, zrs, fs, fr,
 ):
     me = lax.axis_index("dp")
     core = lax.axis_index("tensor")
@@ -603,6 +603,11 @@
 
     for c in loads(0):
         c.start()
+    weights = [
+        pltpu.make_async_copy(src, dst, w_sem.at[n]) for n, (src, dst) in enumerate(((wd_in, wd), (wg_in, wg), (wu_in, wu)))
+    ]
+    for c in weights:
+        c.start()
     bar = pltpu.get_barrier_semaphore()
 
     def sig(d, c):
@@ -686,6 +691,11 @@
                 c.start()
 
     def second_part(i):
+        @pl.when(i == 0)
+        def _():
+            for c in weights:
+                c.wait()
+
         logits = mm(rr[...], wr[...])
         lane = lax.broadcasted_iota(jnp.int32, logits.shape, 1)
         logits = jnp.where(lane < 16, logits, -jnp.inf)
@@ -867,16 +877,18 @@
         pl.when(zp < z)(lambda: zc(zp, dn, 1).start())
         pl.when(zp > z)(lambda: zc(zp, up, 0).start())
 
+    lag = jnp.where((z == 0) | (z == 3), 5, 7)
+
     def step(i, _):
         pl.when(i < 8)(lambda: first_part(i))
         pl.when((i >= 1) & (i <= 8))(lambda: pair_sum(i - 1))
         seconds = (i % 2 == 0) & (i >= 4) & (i <= 10)
-        lasts = (i % 2 == 1) & (i >= 7) & (i <= 13)
+        lasts = (i % 2 == 1) & (i >= lag) & (i <= lag + 6)
         pl.when(seconds)(lambda: second_fetch((i - 4) // 2))
-        pl.when(lasts)(lambda: last_fetch((i - 7) // 2))
+        pl.when(lasts)(lambda: last_fetch((i - lag) // 2))
         pl.when(i < 8)(lambda: second_part(i))
         pl.when(seconds)(lambda: second_hop((i - 4) // 2))
-        pl.when(lasts)(lambda: last_hop((i - 7) // 2))
+        pl.when(lasts)(lambda: last_hop((i - lag) // 2))
         pl.when(i < 8)(lambda: third_part(i))
         return 0
 
@@ -922,15 +934,16 @@
             shape(slots, ffe), jax.ShapeDtypeStruct((384, width), jnp.float32),
             shape(4, 3, 64, total), shape(4, 3, 64, total), shape(2, 4, *blk),
         ],
-        in_specs=[any_] * 4 + [vmem] * 6,
+        in_specs=[any_] * 7 + [vmem] * 3,
         out_specs=[vmem] + [any_] * 5 + [vmem] + [any_] * 3,
         scratch_shapes=[
+            V(wg.shape, low), V(wu.shape, low), V(wd.shape, low),
             V((16,) + blk, low), V((2,) + blk, low), V((2,) + blk, low), V((3,) + blk, low),
             V((2, 256, width), low), V((2, 256, width), low), V((2, 128, 256), low), V((2, 256, 128), low),
             V((256, width), low), V((256, width), low), V((2, 256, 256), low), V((2, 256, 384), low),
             V((2, 256, width), low), V((2, 384, width), low),
             V((256, ffe), low), V((256, ffe), low), V((256, ffe), low), V((256, 128), low),
-            S((4,)), S((5,)), S((4,)), pltpu.SemaphoreType.REGULAR, S, S, S((4, 3)), S((4, 3)), S((4, 3)), S((4, 3)), S((4,)), S((2, 4)), S, S,
+            S((3,)), S((4,)), S((5,)), S((4,)), pltpu.SemaphoreType.REGULAR, S, S, S((4, 3)), S((4, 3)), S((4, 3)), S((4, 3)), S((4,)), S((2, 4)), S, S,
         ],
         compiler_params=pltpu.CompilerParams(collective_id=cid, has_side_effects=True, vmem_limit_bytes=60 << 20),
         cost_estimate=pl.CostEstimate(flops=65 * 10**9, bytes_accessed=80 * 10**6, transcendentals=0),
@@ -1120,21 +1133,33 @@
 
 
 def att_bwd_kernel(
-    w4, w2, home, grad, middle, moe_low, tok, normed, lat_raw, qcat, keys, kv_in, lse, att, wr,
-    g_att, g_moe, g_lat, cos, sin, bias,
+    w4, w2, home, grad, middle, moe_low, wr, g_att, g_moe, g_lat, kv_in,
+    tok_in, normed_in, lat_raw_in, qcat_in, keys_in, lse_in, att_in, cos_in, sin_in, bias_in,
     tok_grad, packed, p4,
+    tok, normed, lat_raw, qcat, keys, lse, att, cos, sin, bias,
     kv, wq, wo, wkv, wlat, dmid, dnorm, dmid_low, d_att, dq, dqr, dkr, dk_out, dk_pair, dk_in, own_dk, part, arrived, d_keys,
-    w_sem, kv_sem, ks, kr, cs, cr, ps, pr, hs, hr, o_sem,
+    late_sem, w_sem, kv_sem, ks, kr, cs, cr, ps, pr, hs, hr, o_sem,
 ):
     me = lax.axis_index("dp")
     core = lax.axis_index("tensor")
-    width = tok.shape[1]
+    width = grad.shape[1]
     scale = (NOPE + ROPE) ** -0.5
     loads = [pltpu.make_async_copy(h, v, s) for h, v, s in slab_copies(w4, w2, wq, wo, wkv, wlat, w_sem)]
     stores = [pltpu.make_async_copy(v, h, s) for h, v, s in slab_copies(p4, packed, wq, wo, wkv, wlat, o_sem)]
     kv_load = pltpu.make_async_copy(kv_in, kv, kv_sem)
+    late = [
+        pltpu.make_async_copy(src, dst, late_sem.at[n])
+        for n, (src, dst) in enumerate(
+            (
+                (att_in, att), (qcat_in, qcat), (keys_in, keys), (bias_in, bias), (lse_in, lse), (cos_in, cos),
+                (sin_in, sin), (normed_in, normed), (lat_raw_in, lat_raw), (tok_in, tok),
+            )
+        )
+    ]
     loads[2].start()
     kv_load.start()
+    for c in late:
+        c.start()
     for n in (1, 3, 4, 5, 6, 0):
         loads[n].start()
     bar = pltpu.get_barrier_semaphore()
@@ -1166,6 +1191,8 @@
     small = tn(moe_low[...], moved) + tn(gains, one_lane(81))
 
     loads[2].wait()
+    for c in late:
+        c.wait()
     d_att[...] = mm(dmid_low[...], wo[...]).astype(jnp.bfloat16)
 
     def wo_rows(n, _):
@@ -1301,20 +1328,22 @@
     return pl.pallas_call(
         att_bwd_kernel,
         out_shape=[shape(f32, rows, width), shape(low, width, pack - 512), shape(low, 16, 4, 32, 512)],
-        in_specs=[any_, any_] + [vmem] * 9 + [any_] + [vmem] * 9,
+        in_specs=[any_, any_] + [vmem] * 8 + [any_] * 11,
         out_specs=[vmem, any_, any_],
         scratch_shapes=[
+            V((rows, width), low), V((rows, width), low), V((rows, 640), f32), V((8, rows, 256), low), V((SLOTS, rows, 640), low),
+            V((8, rows, 1), f32), V((rows, 1024), low), V((rows, 512), f32), V((rows, 512), f32), V((rows, KEYS), f32),
             V((KEYS, 2048), low), V((width, 1536), low), V((width, 1024), low), V((16, 32, 2048), low),
             V((width, 640), low), V((rows, width), f32), V((rows, width), f32), V((rows, width), low), V((rows, 1024), low),
             V((rows, 1536), low), V((rows, 512), f32), V((KEYS, 128), f32), V((SLOTS, rows, 640), low), V((SLOTS, rows // 2, 640), low),
             V((4, rows // 2, 640), low), V((rows // 2, 640), f32), V((rows, width), low), V((rows, width), low), V((rows, 640), low),
-            S((7,)), S, S((4,)), S((4,)), S, S, S, S, S, S, S((7,)),
+            S((10,)), S((7,)), S, S((4,)), S((4,)), S, S, S, S, S, S, S((7,)),
         ],
         compiler_params=pltpu.CompilerParams(collective_id=cid, has_side_effects=True, vmem_limit_bytes=60 << 20),
         cost_estimate=pl.CostEstimate(flops=25 * 10**9, bytes_accessed=70 * 10**6, transcendentals=0),
     )(
-        weights.reshape(16, 4, 32, pack), weights, home, grad, middle, moe_low, tok, normed, lat_raw, qcat, keys, kv, lse, att, wr,
-        g_att, g_moe, g_lat, cos, sin, bias,
+        weights.reshape(16, 4, 32, pack), weights, home, grad, middle, moe_low, wr, g_att, g_moe, g_lat, kv,
+        tok, normed, lat_raw, qcat, keys, lse, att, cos, sin, bias,
     )
 
 

time: 803 us -> 791 us (0.985)
  Pallas kernels: 682 us -> 665 us
    pallas_call x1, Pallas kernels: 211 us -> 195 us  [moe_call(): pl.pallas_call(moe_kernel, out_shape=[shape(2, *blk), shape(slots, width)...]
where the time goes in v5:
time: 791 us; the launch traced here: 782 us
  Pallas kernels  665 us (84%)
  local copies, waits for them, and re-layouts  49.4 us (6%)
  matrix products  32.2 us (4%)
  other arithmetic  17.1 us (2%)
  starting transfers between devices  16.6 us (2%)
    pallas_call x2, Pallas kernels, ag16(): pl.pallas_call(functools.partial(ag_kernel, kinds, cuts), out_shape=[jax....  267 us
    pallas_call x1, Pallas kernels, moe_call(): pl.pallas_call(moe_kernel, out_shape=[shape(2, *blk), shape(slots, width)...  195 us
    pallas_call x1, Pallas kernels, rs16(): pl.pallas_call(rs_kernel, out_shape=jax.ShapeDtypeStruct(blkshape, jnp.fl...  116 us
    pallas_call x1, Pallas kernels, att_bwd(): pl.pallas_call(att_bwd_kernel, out_shape=[shape(f32, rows, width), shape(...  57.6 us
    dot_general x3, matrix products, matmul_tn(): lax.dot_general(left_mat, right_mat, (((0,), (0,)), ((), ())), preferred_...  32 us
    pallas_call x1, Pallas kernels, att_fwd(): pl.pallas_call(att_fwd_kernel, out_shape=[shape(f32, rows, width), shape(...  29.5 us
    unnamed x45, local copies, waits for them, and re-layouts  18.8 us
    all_to_all x2, starting transfers between devices, exchange(): return lax.all_to_all(parts, 'dp', split_axis=0, concat_axis=0, tiled=True)  16.6 us
  transfers between devices with their start and end apart: 2, of which 0 were waited for; matrix products, arithmetic and copies ran while one was open for 7% of the time, Pallas kernels for 11%

profile of v5, /device:TPU:0, one launch (start us, length us, event | category | flops | bytes accessed | tf_op | source)
XLA Modules:
  0.0 781.5 jit_solution(13053931583222849394)
XLA Ops:
  0.7 1.3 copy.120
  2.1 0.7 convert_element_type.83
  2.8 0.7 pad.13
  3.4 0.2 concatenate.42
  3.6 0.9 concatenate.40
  4.5 0.9 concatenate.41
  5.4 0.8 copy.125
  6.5 0.9 copy.169
  7.8 0.2 copy.118
  8.8 1.9 constant_dynamic-slice_fusion.2
  10.8 1.1 concatenate.37.refs_0_
  11.9 181.1 %shard_map.297 = (bf16[16,1,2,64,3712]{4,3,2,1,0:T(8,128)(2,1)}, bf16[16,2,2,64,2048]{4,3,2,1,0:T(8,128)(2,1)}) custom-call(bf16[2,64,3712]{2,1,0:T(8,128)(2,1)} %concatenate.37.refs_0_, bf16[2,64,2048]{2,1,0:T(8,128)(2,1)} %bitcast.116), custom_call_target="tpu_custom_call" | custom-call | tf_op jit(solution)/shard_map/pallas_call | solution.py:344
  193.2 1.1 copy.133
  194.2 5.9 all-to-all-start
  200.2 1.4 slice_reduce_fusion
  201.6 2.6 convert_reduce_fusion
  204.2 1.4 convert_compare_fusion
  205.6 1.2 slice.87
  207.1 1.0 copy.132.sin.sin_in
  208.2 1.0 copy.131.cos.cos_in
  209.2 0.7 reshape.286.g_lat
  209.8 0.5 eq.50
  210.3 0.6 reduce_or.9
  211.1 0.9 pad.15.wr
  212.1 2.4 fusion.3.pick_t
  214.5 1.4 fusion.1.pick
  215.9 1.6 fusion.6.bias.bias_in
  217.6 29.5 %shard_map.298 = (f32[256,2048]{1,0:T(8,128)}, bf16[256,2048]{1,0:T(8,128)(2,1)}, bf16[256,2048]{1,0:T(8,128)(2,1)}, f32[256,640]{1,0:T(8,128)}, bf16[8,256,256]...) custom-call(bf16[256,2048]{1,0:T(8,128)(2,1)} %tok_in.1, ...), custom_call_target="tpu_custom_call" | custom-call | flops 10000000000 | bytes 40000000 | tf_op jit(solution)/shard_map/pallas_call | solution.py:1117
  247.3 0.8 fusion.7.sdn
  248.1 1.1 pad_slice_fusion.1
  249.2 0.8 constant_dynamic-slice_fusion
  250.0 85.4 %shard_map.299 = bf16[16,2,2,64,2048]{4,3,2,1,0:T(8,128)(2,1)} custom-call(bf16[2,64,2048]{2,1,0:T(8,128)(2,1)} %bitcast.117), custom_call_target="tpu_custom_call" | custom-call | tf_op jit(solution)/shard_map/pallas_call | solution.py:344
  335.4 195.2 %shard_map.300 = (bf16[2,2,64,4224]{3,2,1,0:T(8,128)(2,1)}, bf16[2048,2048]{1,0:T(8,128)(2,1)}, bf16[2048,2048]{1,0:T(8,128)(2,1)}, bf16[2048,704]{1,0:T(8,128)(...) custom-call(bf16[16,256,2048]{2,1,0:T(8,128)(2,1)} %bitcast.102, ...), custom_call_target="tpu_custom_call" | custom-call | flops 65000001536 | bytes 80000000 | tf_op jit(solution)/shard_map/pallas_call | solution.py:930
  530.7 2.3 slice.107.home
  533.0 2.1 convert_bitcast_fusion
  535.2 0.4 copy.162
  535.8 1.3 copy.168
  537.0 10.7 %all-to-all-start.1 = ((bf16[16,3,88,128]{3,2,1,0:T(8,128)(2,1)}), bf16[16,3,88,128]{3,2,1,0:T(8,128)(2,1)S(1)}, u32[]{:S(2)}, u32[]{:S(2)}) async-start(bf16[16,3,88,128]{3,2,1,0:T(8,128)(2,1)} %bitcast.100), calls=%async_computation.1 | async-start | bytes 2162688 | tf_op jit(solution)/shard_map/all_to_all | solution.py:1364
  547.7 11.3 %convolution_bitcast_fusion.2 = f32[1,2048,704]{1,2,0:T(8,128)} fusion(bf16[2048,2048]{1,0:T(8,128)(2,1)} %get-tuple-element.67, bf16[2048,704]{1,0:T(8,128)(2,1)} %get-tuple-element.68), kind=kOutput, calls=%fused_computation.2 | convolution fusion | flops 5905580032 | bytes 17039360 | tf_op jit(solution)/shard_map/dot_general | solution.py:67
  559.0 10.3 %convolution_bitcast_fusion = f32[1,704,2048]{2,1,0:T(8,128)} fusion(bf16[2048,704]{1,0:T(8,128)(2,1)S(1)} %copy-done.11, bf16[2048,2048]{1,0:T(8,128)(2,1)} %get-tuple-element.71), kind=kOutput, calls=%fused_computation | convolution fusion | flops 5905580032 | bytes 17039360 | tf_op jit(solution)/shard_map/dot_general | solution.py:67
  569.4 57.6 %shard_map.301 = (f32[256,2048]{1,0:T(8,128)}, bf16[2048,3200]{1,0:T(8,128)(2,1)}, bf16[16,4,32,512]{3,2,1,0:T(8,128)(2,1)}) custom-call(bf16[16,4,32,3712]{3,2,1,0:T(8,128)(2,1)} %bitcast.140, bf16[2048,3712]{1,0:T(8,128)(2,1)} %bitcast.139, bf16[256,2176]{1,0:T(8,128)(2,1)} %slice.107.home, bf16[256,2048]{1,0:T(8,128)(2,1)} %grad.1, ...), custom_call_target="tpu_custom_call" | custom-call | flops 24999999488 | bytes 70000000 | tf_op jit(solution)/shard_map/pallas_call | solution.py:1328
  627.0 2.6 add_convert_fusion
  629.6 10.4 %convolution_bitcast_fusion.1 = f32[1,2048,704]{1,2,0:T(8,128)} fusion(bf16[2048,2048]{1,0:T(8,128)(2,1)} %get-tuple-element.67, bf16[2048,704]{1,0:T(8,128)(2,1)S(1)} %copy-done.12), kind=kOutput, calls=%fused_computation.1 | convolution fusion | flops 5905580032 | bytes 17039360 | tf_op jit(solution)/shard_map/dot_general | solution.py:67
  640.1 115.8 %shard_map.302 = f32[2,64,3712]{2,1,0:T(8,128)} custom-call(bf16[16,2,64,3200]{3,2,1,0:T(8,128)(2,1)} %bitcast.103, bf16[16,2,64,512]{3,2,1,0:T(8,128)(2,1)} %bitcast.120), custom_call_target="tpu_custom_call" | custom-call | tf_op jit(solution)/shard_map/pallas_call | solution.py:535
  756.0 0.9 slice.113
  756.9 1.6 slice.117
  758.5 1.7 fusion.9
  760.1 1.0 slice.112
  761.1 1.9 fusion.11
  763.1 0.6 copy.156
  763.7 1.5 copy.159
  765.2 1.4 copy.158
  766.6 1.4 copy.153
  768.1 0.9 copy.155
  768.9 1.0 copy.157
  769.9 1.1 copy.144
  771.0 0.8 copy.163
  771.8 0.8 copy.154
  772.9 1.0 pad_maximum_fusion.1
  773.9 1.1 copy.148
  775.0 1.2 slice_bitcast_fusion
  776.3 2.4 copy.150
  778.7 1.1 copy.149
  779.8 1.3 copy.171
  (57 shorter events, 2.9 us)
Async XLA Ops:
  0.6 6.8 copy-start.9
  0.7 6.9 copy-start.7
  0.7 7.1 copy-start.4
  0.7 7.3 copy-start.5
  8.8 184.2 %copy-start.6 = (bf16[1408,128]{1,0:T(8,128)(2,1)S(1)}, bf16[1408,128]{1,0:T(8,128)(2,1)}, u32[]{:S(2)}) copy-start(bf16[1408,128]{1,0:T(8,128)(2,1)} %param.32) | copy-start | bytes 1081348
  194.2 52.9 %all-to-all-start = ((bf16[16,3,88,128]{3,2,1,0:T(8,128)(2,1)}), bf16[16,3,88,128]{3,2,1,0:T(8,128)(2,1)S(1)}, u32[]{:S(2)}, u32[]{:S(2)}) async-start(bf16[16,3,88,128]{3,2,1,0:T(8,128)(2,1)} %copy.133), calls=%async_computation | async-start | bytes 2162688 | tf_op jit(solution)/shard_map/all_to_all | solution.py:1364
  208.1 3.9 copy-start.10
  247.3 1.9 copy-start.8
  537.0 103.0 %all-to-all-start.1 = ((bf16[16,3,88,128]{3,2,1,0:T(8,128)(2,1)}), bf16[16,3,88,128]{3,2,1,0:T(8,128)(2,1)S(1)}, u32[]{:S(2)}, u32[]{:S(2)}) async-start(bf16[16,3,88,128]{3,2,1,0:T(8,128)(2,1)} %bitcast.100), calls=%async_computation.1 | async-start | bytes 2162688 | tf_op jit(solution)/shard_map/all_to_all | solution.py:1364
  547.7 11.3 %copy-start.11 = (bf16[2048,704]{1,0:T(8,128)(2,1)S(1)}, bf16[2048,704]{1,0:T(8,128)(2,1)}, u32[]{:S(2)}) copy-start(bf16[2048,704]{1,0:T(8,128)(2,1)} %get-tuple-element.70) | copy-start | bytes 8650756
  569.4 57.6 %copy-start.2 = (f32[256,2048]{1,0:T(8,128)S(1)}, f32[256,2048]{1,0:T(8,128)}, u32[]{:S(2)}) copy-start(f32[256,2048]{1,0:T(8,128)} %get-tuple-element.46.middle) | copy-start | bytes 6291460
  627.0 2.6 copy-start.12
  756.0 7.0 copy-start
  768.9 2.9 copy-start.3
  776.3 3.5 copy-start.1

commit v6 on v5

--- a/solution.py
+++ b/solution.py
@@ -568,7 +568,7 @@
 def moe_kernel(
     moe, grd, pick, pick_t, wg_in, wu_in, wd_in, wr, sgu, sdn,
     o_out, r_out, rg_out, act_out, da_out, db_out, sg_out, yr, xr, zr,
-    wg, wu, wd, own, sib, sibr, stage, xb, gb, pk, pt, rr, rg, ly, ld, ry, rd, acts, das, dbs, dgs,
+    sg_sum, wg, wu, wd, own, sib, sibr, stage, xb, gb, pk, pt, rr, rg, ly, ld, ry, rd, acts, das, dbs, dgs,
     w_sem, in_sem, out_sem, st_sem, free, cs, cr, xs, xrs, ys, yrs, zs, zrs, fs, fr,
 ):
     me = lax.axis_index("dp")
@@ -623,7 +623,7 @@
     for q in range(2):
         ry[q, hid:] = sdn[...]
         rd[q, hid:] = sgu[...]
-    sg_out[...] = jnp.zeros_like(sg_out)
+    sg_sum[...] = jnp.zeros_like(sg_sum)
 
     def y_(j, b, half, zp):
         return rc(own.at[b, half], yr.at[zp, j], ys.at[zp, j], yrs.at[zp, j], yn, core)
@@ -680,8 +680,8 @@
             ld[q, :, 2 * hid :] = d_b.astype(jnp.bfloat16)
 
         def shared_grads(n):
-            sg_out[: 2 * hid, n] += tn(ld[0, :, hid:], xb[0, :, n]) + tn(ld[1, :, hid:], xb[1, :, n])
-            sg_out[2 * hid :, n] += tn(ly[0, :, hid:], gb[0, :, n]) + tn(ly[1, :, hid:], gb[1, :, n])
+            sg_sum[: 2 * hid, n] += tn(ld[0, :, hid:], xb[0, :, n]) + tn(ld[1, :, hid:], xb[1, :, n])
+            sg_sum[2 * hid :, n] += tn(ly[0, :, hid:], gb[0, :, n]) + tn(ly[1, :, hid:], gb[1, :, n])
 
         columns(shared_grads)
 
@@ -893,6 +893,11 @@
         return 0
 
     lax.fori_loop(0, 14, step, 0)
+
+    def give(n):
+        sg_out[:, n] = sg_sum[:, n].astype(jnp.bfloat16)
+
+    columns(give)
     for a in range(2):
 
         def row(n, _):
@@ -931,13 +936,13 @@
         moe_kernel,
         out_shape=[
             shape(2, *blk), shape(slots, width), shape(slots, width), shape(slots, ffe), shape(slots, ffe),
-            shape(slots, ffe), jax.ShapeDtypeStruct((384, width), jnp.float32),
+            shape(slots, ffe), shape(384, width),
             shape(4, 3, 64, total), shape(4, 3, 64, total), shape(2, 4, *blk),
         ],
         in_specs=[any_] * 7 + [vmem] * 3,
         out_specs=[vmem] + [any_] * 5 + [vmem] + [any_] * 3,
         scratch_shapes=[
-            V(wg.shape, low), V(wu.shape, low), V(wd.shape, low),
+            V((384, width), jnp.float32), V(wg.shape, low), V(wu.shape, low), V(wd.shape, low),
             V((16,) + blk, low), V((2,) + blk, low), V((2,) + blk, low), V((3,) + blk, low),
             V((2, 256, width), low), V((2, 256, width), low), V((2, 128, 256), low), V((2, 256, 128), low),
             V((256, width), low), V((256, width), low), V((2, 256, 256), low), V((2, 256, 384), low),
@@ -965,21 +970,43 @@
     return lax.rsqrt(jnp.mean(v * v, axis=1, keepdims=True) + eps_norm)
 
 
-def neighbours(me, core, bar):
-    count = jnp.int32(1)
+def greet_all(me, core, bar):
     pl.semaphore_signal(bar, inc=1, device_id=(me, 1 - core), device_id_type=MESH)
-    for d in range(1, SLOTS):
-
-        @pl.when(me + d < 16)
-        def _():
-            pl.semaphore_signal(bar, inc=1, device_id=(jnp.minimum(me + d, 15), core), device_id_type=MESH)
-
-        @pl.when(me >= d)
-        def _():
-            pl.semaphore_signal(bar, inc=1, device_id=(jnp.maximum(me - d, 0), core), device_id_type=MESH)
-
-        count = count + (me + d < 16).astype(jnp.int32) + (me >= d).astype(jnp.int32)
-    return count
+    for j in range(1, 16):
+        pl.semaphore_signal(bar, inc=1, device_id=((me + j) % 16, core), device_id_type=MESH)
+    pl.semaphore_wait(bar, 16)
+
+
+class Trade:
+    def __init__(self, source, land, me, core, send_sem, recv_sem, own_sem):
+        def copy(j, to, to_slot):
+            return pltpu.make_async_remote_copy(
+                src_ref=source(to), dst_ref=land.at[to_slot], send_sem=send_sem.at[j - 1], recv_sem=recv_sem.at[j - 1],
+                device_id=(to, core), device_id_type=MESH,
+            )
+
+        self.out = [copy(j, (me + j) % 16, me) for j in range(1, 16)]
+        self.back = [copy(j, (me + 16 - j) % 16, (me + 16 - j) % 16) for j in range(1, 16)]
+        self.own = pltpu.make_async_copy(source(me), land.at[me], own_sem)
+
+    def start(self):
+        self.own.start()
+        for c in self.out:
+            c.start()
+
+    def wait(self):
+        self.own.wait()
+        for c in self.back:
+            c.wait_recv()
+        for c in self.out:
+            c.wait_send()
+
+
+def read_gains(wlat):
+    lane = lax.broadcasted_iota(jnp.int32, (16, 128), 1)
+    row = lax.broadcasted_iota(jnp.int32, (16, 128), 0)
+    rows = nt((lane == row + 80).astype(jnp.bfloat16), wlat[:, RANK:])
+    return rows[0:1], rows[1:2]
 
 
 def slab_copies(w4, w2, wq, wo, wkv, wlat, sem):
@@ -994,9 +1021,9 @@
 
 
 def att_fwd_kernel(
-    tok, w4, w2, g_att, g_moe, g_lat, cos, sin, bias,
-    middle, moe_low, normed, lat_raw, qcat, keys, kv_out, lse, att,
-    kv, wq, wo, wkv, wlat, part, arrived, w_sem, kv_sem, ks, kr, ts, tr, cs, cr,
+    tok, w4, w2, trade_in, g_lat, cos, sin, bias,
+    middle, moe_low, normed, lat_raw, qcat, keys, kv_out, lse, att, trade_out,
+    kv, wq, wo, wkv, wlat, part, arrived, w_sem, kv_sem, ks, kr, ts, tr, cs, cr, as_, ar, ao,
 ):
     me = lax.axis_index("dp")
     core = lax.axis_index("tensor")
@@ -1004,10 +1031,12 @@
     for c in loads:
         c.start()
     bar = pltpu.get_barrier_semaphore()
-    pl.semaphore_wait(bar, neighbours(me, core, bar))
+    greet_all(me, core, bar)
+    trade = Trade(lambda i: trade_in.at[i], trade_out, me, core, as_, ar, ao)
     t = tok[...].astype(jnp.float32)
-    normed[...] = (t * root(t) * g_att[...]).astype(jnp.bfloat16)
     loads[0].wait()
+    g_att, g_moe = read_gains(wlat)
+    normed[...] = (t * root(t) * g_att).astype(jnp.bfloat16)
     lat = mm(normed[...], wlat[...])
     lat_raw[...] = lat
     first = lat[:, :RANK]
@@ -1043,6 +1072,8 @@
         @pl.when(me < d)
         def _():
             keys[SLOTS - 1 - d] = jnp.zeros((256, 640), jnp.bfloat16)
+
+    trade.start()
 
     loads[1].wait()
     half = lax.broadcasted_iota(jnp.int32, (256, 128), 1) < 64
@@ -1101,14 +1132,15 @@
     swap.wait()
     m = tok[...].astype(jnp.float32) + (part[...].astype(jnp.float32) + arrived[...].astype(jnp.float32))
     middle[...] = m
-    moe_low[...] = (m * root(m) * g_moe[...]).astype(jnp.bfloat16)
+    moe_low[...] = (m * root(m) * g_moe).astype(jnp.bfloat16)
     save.wait()
+    trade.wait()
     for d in range(1, SLOTS):
         pl.when(me + d < 16)(lambda d=d: send(d).wait_send())
         pl.when(me >= d)(lambda d=d: hand(d).wait_send())
 
 
-def att_fwd(tok, weights, g_att, g_moe, g_lat, cos, sin, bias, cid):
+def att_fwd(tok, weights, trade, g_lat, cos, sin, bias, cid):
     low, f32, S, V = jnp.bfloat16, jnp.float32, pltpu.SemaphoreType.DMA, pltpu.VMEM
     any_, vmem = pl.BlockSpec(memory_space=pl.ANY), pl.BlockSpec(memory_space=pltpu.VMEM)
     shape = lambda kind, *s: jax.ShapeDtypeStruct(s, kind)
@@ -1119,26 +1151,28 @@
         out_shape=[
             shape(f32, rows, width), shape(low, rows, width), shape(low, rows, width), shape(f32, rows, 640),
             shape(low, 8, rows, 256), shape(low, SLOTS, rows, 640), shape(low, KEYS, 2048), shape(f32, 8, rows, 1),
-            shape(low, rows, 1024),
+            shape(low, rows, 1024), shape(low, *trade.shape),
         ],
-        in_specs=[vmem, any_, any_] + [vmem] * 6,
-        out_specs=[vmem] * 6 + [any_] + [vmem] * 2,
+        in_specs=[vmem, any_, any_, any_] + [vmem] * 4,
+        out_specs=[vmem] * 6 + [any_] + [vmem] * 2 + [any_],
         scratch_shapes=[
             V((KEYS, 2048), low), V((width, 1536), low), V((width, 1024), low), V((16, 32, 2048), low), V((width, 640), low),
             V((rows, width), low), V((rows, width), low), S((7,)), S, S((4,)), S((4,)), S((4,)), S((4,)), S, S,
+            S((15,)), S((15,)), S,
         ],
         compiler_params=pltpu.CompilerParams(collective_id=cid, has_side_effects=True, vmem_limit_bytes=60 << 20),
         cost_estimate=pl.CostEstimate(flops=10**10, bytes_accessed=40 * 10**6, transcendentals=0),
-    )(tok, weights.reshape(16, 4, 32, pack), weights, g_att, g_moe, g_lat, cos, sin, bias)
+    )(tok, weights.reshape(16, 4, 32, pack), weights, trade, g_lat, cos, sin, bias)
 
 
 def att_bwd_kernel(
-    w4, w2, home, grad, middle, moe_low, wr, g_att, g_moe, g_lat, kv_in,
+    w4, w2, home_in, trade_in, grad, middle, moe_low, wr, g_lat, kv_in,
     tok_in, normed_in, lat_raw_in, qcat_in, keys_in, lse_in, att_in, cos_in, sin_in, bias_in,
-    tok_grad, packed, p4,
+    tok_grad, packed, p4, trade_out,
+    home,
     tok, normed, lat_raw, qcat, keys, lse, att, cos, sin, bias,
     kv, wq, wo, wkv, wlat, dmid, dnorm, dmid_low, d_att, dq, dqr, dkr, dk_out, dk_pair, dk_in, own_dk, part, arrived, d_keys,
-    late_sem, w_sem, kv_sem, ks, kr, cs, cr, ps, pr, hs, hr, o_sem,
+    home_sem, as_, ar, ao, late_sem, w_sem, kv_sem, ks, kr, cs, cr, ps, pr, hs, hr, o_sem,
 ):
     me = lax.axis_index("dp")
     core = lax.axis_index("tensor")
@@ -1156,14 +1190,24 @@
             )
         )
     ]
+    home_load = pltpu.make_async_copy(home_in.at[:, width:], home, home_sem)
+    home_load.start()
+    loads[0].start()
     loads[2].start()
     kv_load.start()
     for c in late:
         c.start()
-    for n in (1, 3, 4, 5, 6, 0):
+    for n in (1, 3, 4, 5, 6):
         loads[n].start()
     bar = pltpu.get_barrier_semaphore()
-    pl.semaphore_wait(bar, neighbours(me, core, bar))
+    greet_all(me, core, bar)
+    trade = Trade(
+        lambda i: trade_in.at[:, pl.ds(pl.multiple_of(i * 128, 128), 128)], trade_out, me, core, as_, ar, ao
+    )
+    trade.start()
+    loads[0].wait()
+    g_att, g_moe = read_gains(wlat)
+    home_load.wait()
     lane = lax.broadcasted_iota(jnp.int32, (256, 128), 1)
 
     logits = jnp.where(lane < 16, mm(moe_low[...], wr[...]), -jnp.inf)
@@ -1182,7 +1226,7 @@
         return (lane == n).astype(jnp.bfloat16)
 
     d_moe = home[:, :width].astype(jnp.float32) + nt(d_logits, wr[...])
-    d_norm2, gain_rows = norm_back(middle[...], g_moe[...], d_moe)
+    d_norm2, gain_rows = norm_back(middle[...], g_moe, d_moe)
     d_middle = grad[...].astype(jnp.float32) + d_norm2
     dmid[...] = d_middle
     dmid_low[...] = d_middle.astype(jnp.bfloat16)
@@ -1298,9 +1342,8 @@
     d_second = turned(d_keys[:, RANK:].astype(jnp.float32), cos[:, :128], -sin[:, :128])
     d_second = jnp.where(lane < 64, d_second, 0.0)
     d_lat_low = jnp.concatenate([d_first, d_second], 1).astype(jnp.bfloat16)
-    loads[0].wait()
     d_normed = dnorm[...] + nt(d_lat_low, wlat[...])
-    d_norm1, att_gain_rows = norm_back(tok[...].astype(jnp.float32), g_att[...], d_normed)
+    d_norm1, att_gain_rows = norm_back(tok[...].astype(jnp.float32), g_att, d_normed)
     tok_grad[...] = dmid[...] + d_norm1
     small = small + tn(normed[...], d_lat_low[:, RANK:]) + tn(att_gain_rows.astype(jnp.bfloat16), one_lane(80))
     wlat[:, :RANK] = tn(normed[...], d_lat_low[:, :RANK]).astype(jnp.bfloat16)
@@ -1312,6 +1355,7 @@
     stores[0].start()
     for c in stores:
         c.wait()
+    trade.wait()
     for d in range(1, SLOTS):
         pl.when(me >= d)(lambda d=d: send(d, me - d).wait_send())
     pair.wait_send()
@@ -1319,7 +1363,9 @@
     half(mine).wait_send()
 
 
-def att_bwd(weights, home, grad, middle, moe_low, tok, normed, lat_raw, qcat, keys, kv, lse, att, wr, g_att, g_moe, g_lat, cos, sin, bias, cid):
+def att_bwd(
+    weights, home, trade, grad, middle, moe_low, tok, normed, lat_raw, qcat, keys, kv, lse, att, wr, g_lat, cos, sin, bias, cid
+):
     low, f32, S, V = jnp.bfloat16, jnp.float32, pltpu.SemaphoreType.DMA, pltpu.VMEM
     any_, vmem = pl.BlockSpec(memory_space=pl.ANY), pl.BlockSpec(memory_space=pltpu.VMEM)
     shape = lambda kind, *s: jax.ShapeDtypeStruct(s, kind)
@@ -1327,28 +1373,25 @@
     pack = weights.shape[1]
     return pl.pallas_call(
         att_bwd_kernel,
-        out_shape=[shape(f32, rows, width), shape(low, width, pack - 512), shape(low, 16, 4, 32, 512)],
-        in_specs=[any_, any_] + [vmem] * 8 + [any_] * 11,
-        out_specs=[vmem, any_, any_],
+        out_shape=[shape(f32, rows, width), shape(low, width, pack - 512), shape(low, 16, 4, 32, 512), shape(low, 16, 384, 128)],
+        in_specs=[any_] * 4 + [vmem] * 5 + [any_] * 11,
+        out_specs=[vmem, any_, any_, any_],
         scratch_shapes=[
+            V((rows, width + 128), low),
             V((rows, width), low), V((rows, width), low), V((rows, 640), f32), V((8, rows, 256), low), V((SLOTS, rows, 640), low),
             V((8, rows, 1), f32), V((rows, 1024), low), V((rows, 512), f32), V((rows, 512), f32), V((rows, KEYS), f32),
             V((KEYS, 2048), low), V((width, 1536), low), V((width, 1024), low), V((16, 32, 2048), low),
             V((width, 640), low), V((rows, width), f32), V((rows, width), f32), V((rows, width), low), V((rows, 1024), low),
             V((rows, 1536), low), V((rows, 512), f32), V((KEYS, 128), f32), V((SLOTS, rows, 640), low), V((SLOTS, rows // 2, 640), low),
             V((4, rows // 2, 640), low), V((rows // 2, 640), f32), V((rows, width), low), V((rows, width), low), V((rows, 640), low),
-            S((10,)), S((7,)), S, S((4,)), S((4,)), S, S, S, S, S, S, S((7,)),
+            S, S((15,)), S((15,)), S, S((10,)), S((7,)), S, S((4,)), S((4,)), S, S, S, S, S, S, S((7,)),
         ],
         compiler_params=pltpu.CompilerParams(collective_id=cid, has_side_effects=True, vmem_limit_bytes=60 << 20),
         cost_estimate=pl.CostEstimate(flops=25 * 10**9, bytes_accessed=70 * 10**6, transcendentals=0),
     )(
-        weights.reshape(16, 4, 32, pack), weights, home, grad, middle, moe_low, wr, g_att, g_moe, g_lat, kv,
+        weights.reshape(16, 4, 32, pack), weights, home, trade, grad, middle, moe_low, wr, g_lat, kv,
         tok, normed, lat_raw, qcat, keys, lse, att, cos, sin, bias,
     )
-
-
-def swapped(v):
-    return lax.ppermute(v, "tensor", [(0, 1), (1, 0)])
 
 
 def my_half(v, rows):
@@ -1358,10 +1401,6 @@
 def row_halves(v):
     rows = v.shape[0] // 2
     return my_half(v, rows).reshape(2, rows // 2, v.shape[1])
-
-
-def exchange(parts):
-    return lax.all_to_all(parts, "dp", split_axis=0, concat_axis=0, tiled=True)
 
 
 def nope_first(w):
@@ -1448,16 +1487,10 @@
         ],
         1,
     )
-    shared_send, weights = lax.optimization_barrier((shared_send, weights))
-    shared_all = exchange(shared_send).transpose(1, 2, 0, 3).reshape(3, shared_part, width)
-    lead = jnp.pad(shared_all, ((0, 0), (0, 128 - shared_part), (0, 0)))
-    shared_in, shared_out = lead[:2].reshape(256, width), lead[2]
-
+    shared_send = jnp.pad(shared_send, ((0, 0), (0, 0), (0, 96 - shared_part), (0, 0)))
     at = q_width + o_width + lat_width
     wr_full = weights[:, at : at + experts]
     at += experts
-    gain_attn = weights[:, at].astype(jnp.float32)
-    gain_moe = weights[:, at + 1].astype(jnp.float32)
     gain_latent = (
         weights[:, at + 2].reshape(dp_count, depth)[:, :kv_rows].reshape(-1).astype(jnp.float32)
     )
@@ -1483,10 +1516,12 @@
     )
 
     bias = jnp.where(allowed, 0.0, -jnp.inf)
-    middle, moe_low, normed_low, lat_raw, qcat, keys, kv, lse, attended_low = att_fwd(
-        tokens, weights, gain_attn[None], gain_moe[None], gain_latent[None], cos_lanes, sin_lanes, bias, 7
-    )
-    moe_low, shared_in, shared_out = lax.optimization_barrier((moe_low, shared_in, shared_out))
+    middle, moe_low, normed_low, lat_raw, qcat, keys, kv, lse, attended_low, shared_all = att_fwd(
+        tokens, weights, shared_send.reshape(dp_count, 3 * 96, depth), gain_latent[None], cos_lanes, sin_lanes, bias, 7
+    )
+    shared_all = shared_all.reshape(dp_count, 3, 96, depth)[:, :, :shared_part].transpose(1, 2, 0, 3)
+    lead = jnp.pad(shared_all.reshape(3, shared_part, width), ((0, 0), (0, 128 - shared_part), (0, 0)))
+    shared_in, shared_out = lead[:2].reshape(256, width), lead[2]
     (moe_all,) = ag16([row_halves(moe_low)], (True,), 3)
     chosen = jnp.any(all_routes == dp_index, axis=1).reshape(dp_count, n_rows)
     earlier = jnp.arange(n_rows)[:, None] < jnp.arange(n_rows)[None, :]
@@ -1516,24 +1551,19 @@
     grad_down = matmul_tn(scaled_act, rows_grad)[None]
     grad_gate = matmul_tn(rows_in, d_ea_low)[None]
     grad_up = matmul_tn(rows_in, d_eb_low)[None]
-    shared_home = exchange(
-        shared_grads.astype(jnp.bfloat16)
-        .reshape(3, 128, dp_count, depth)[:, :shared_part]
-        .transpose(2, 0, 1, 3)
-    ).astype(jnp.float32)
-    shared_home = shared_home.transpose(1, 0, 2, 3).reshape(3, dp_count * shared_part, depth)
-
-    token_input_gradient, packed_grads, kv_grads = att_bwd(
-        weights, home[:, width:], out_grad, middle, moe_low, tokens, normed_low, lat_raw, qcat, keys, kv, lse,
-        attended_low, moe_wr, gain_attn[None], gain_moe[None], gain_latent[None], cos_lanes, sin_lanes, bias, 8
-    )
-    packed_grads, shared_home = lax.optimization_barrier((packed_grads, shared_home))
+    token_input_gradient, packed_grads, kv_grads, shared_home = att_bwd(
+        weights, home, shared_grads, out_grad, middle, moe_low, tokens, normed_low, lat_raw, qcat, keys, kv, lse,
+        attended_low, moe_wr, gain_latent[None], cos_lanes, sin_lanes, bias, 8
+    )
     mine = rs16(
         packed_grads.reshape(dp_count, 2, depth // 2, pack_width - kv_part),
         kv_grads.reshape(dp_count, 2, depth // 2, kv_part),
         6,
     ).reshape(depth, pack_width)
-    grad_sgate, grad_sup, grad_sdown = shared_home[0].T, shared_home[1].T, shared_home[2]
+    shared_home = shared_home.reshape(dp_count, 3, 128, depth)[:, :, :shared_part].astype(jnp.float32)
+    grad_sgate = shared_home[:, 0].transpose(2, 0, 1).reshape(depth, -1)
+    grad_sup = shared_home[:, 1].transpose(2, 0, 1).reshape(depth, -1)
+    grad_sdown = shared_home[:, 2].reshape(-1, depth)
     out_wq = heads_first(mine[:, :q_width])
     at = q_width
     out_wo = mine[:, at : at + o_width].T

time: 791 us -> 780 us (0.986)
  Pallas kernels: 665 us -> 687 us
  starting transfers between devices: 16.6 us -> 0 us
  local copies, waits for them, and re-layouts: 49.4 us -> 40.9 us
    all_to_all x2 -> x0, starting transfers between devices: 16.6 us -> none  [exchange(): return lax.all_to_all(parts, 'dp', split_axis=0, concat_axis=0, tiled=True)]
    pallas_call x1, Pallas kernels: 57.6 us -> 65.7 us  [att_bwd(): pl.pallas_call(att_bwd_kernel, out_shape=[shape(f32, rows, width), shape(...]
  transfers between devices with their start and end apart: 2 -> 0, of which waited for: 0 -> 0; matrix products, arithmetic and copies ran while one was open for 7% -> 0% of each run, Pallas kernels for 11% -> 0%
where the time goes in v6:
time: 780 us; the launch traced here: 771 us
  Pallas kernels  687 us (88%)
  local copies, waits for them, and re-layouts  40.9 us (5%)
  matrix products  30.1 us (4%)
  other arithmetic  12 us (2%)
    pallas_call x2, Pallas kernels, ag16(): pl.pallas_call(functools.partial(ag_kernel, kinds, cuts), out_shape=[jax....  268 us
    pallas_call x1, Pallas kernels, moe_call(): pl.pallas_call(moe_kernel, out_shape=[shape(2, *blk), shape(slots, width)...  197 us
    pallas_call x1, Pallas kernels, rs16(): pl.pallas_call(rs_kernel, out_shape=jax.ShapeDtypeStruct(blkshape, jnp.fl...  123 us
    pallas_call x1, Pallas kernels, att_bwd(): pl.pallas_call(att_bwd_kernel, out_shape=[shape(f32, rows, width), shape(...  65.7 us
    pallas_call x1, Pallas kernels, att_fwd(): pl.pallas_call(att_fwd_kernel, out_shape=[shape(f32, rows, width), shape(...  33 us
    dot_general x3, matrix products, matmul_tn(): lax.dot_general(left_mat, right_mat, (((0,), (0,)), ((), ())), preferred_...  30 us

profile of v6, /device:TPU:0, one launch (start us, length us, event | category | flops | bytes accessed | tf_op | source)
XLA Modules:
  0.0 771.2 jit_solution(16904548708607782627)
XLA Ops:
  0.7 0.7 pad.17
  1.4 0.7 constant_dynamic-slice_fusion.1
  2.1 0.7 convert_element_type.58
  2.8 0.8 pad_dynamic-slice_fusion
  3.6 0.2 concatenate.42
  3.8 0.9 concatenate.40
  4.7 0.9 concatenate.41
  5.6 0.8 copy.60
  6.7 0.2 multiply_sine_fusion
  6.9 0.9 copy.104
  7.8 1.1 copy.59
  8.8 1.1 copy.58
  9.9 1.2 copy.66
  11.2 0.2 copy.67
  11.6 1.1 pad.18.clone
  12.7 0.2 copy.55
  13.6 1.1 concatenate.37.refs_0_
  14.8 1.0 copy.70.sin.sin_in
  15.9 1.0 copy.69.cos.cos_in
  16.9 0.8 constant_dynamic-slice_fusion.2
  17.7 1.6 fusion.6.bias.bias_in
  19.3 181.1 %shard_map.297 = (bf16[16,1,2,64,3712]{4,3,2,1,0:T(8,128)(2,1)}, bf16[16,2,2,64,2048]{4,3,2,1,0:T(8,128)(2,1)}) custom-call(bf16[2,64,3712]{2,1,0:T(8,128)(2,1)} %concatenate.37.refs_0_, bf16[2,64,2048]{2,1,0:T(8,128)(2,1)} %bitcast.106), custom_call_target="tpu_custom_call" | custom-call | tf_op jit(solution)/shard_map/pallas_call | solution.py:344
  200.5 1.4 slice_reduce_fusion
  201.9 0.7 reshape.263.g_lat
  202.6 1.4 convert_compare_fusion
  204.0 0.5 eq.50
  204.5 0.6 reduce_or.9
  205.3 1.3 slice.100
  206.6 0.9 pad.19.wr
  207.5 2.4 fusion.3.pick_t
  209.9 1.4 fusion.1.pick
  211.3 33.0 %shard_map.298 = (f32[256,2048]{1,0:T(8,128)}, bf16[256,2048]{1,0:T(8,128)(2,1)}, bf16[256,2048]{1,0:T(8,128)(2,1)}, f32[256,640]{1,0:T(8,128)}, bf16[8,256,256]...) custom-call(bf16[256,2048]{1,0:T(8,128)(2,1)} %tok_in.1, ...), custom_call_target="tpu_custom_call" | custom-call | flops 10000000000 | bytes 40000000 | tf_op jit(solution)/shard_map/pallas_call | solution.py:1149
  244.3 1.3 slice.101
  245.8 0.5 reshape.249
  246.2 0.6 copy-done.8
  246.8 0.8 constant_dynamic-slice_fusion
  247.7 0.8 fusion.7.sdn
  248.5 1.1 pad_slice_fusion.1
  249.6 87.0 %shard_map.299 = bf16[16,2,2,64,2048]{4,3,2,1,0:T(8,128)(2,1)} custom-call(bf16[2,64,2048]{2,1,0:T(8,128)(2,1)} %bitcast.107), custom_call_target="tpu_custom_call" | custom-call | tf_op jit(solution)/shard_map/pallas_call | solution.py:344
  336.6 196.8 %shard_map.300 = (bf16[2,2,64,4224]{3,2,1,0:T(8,128)(2,1)}, bf16[2048,2048]{1,0:T(8,128)(2,1)}, bf16[2048,2048]{1,0:T(8,128)(2,1)}, bf16[2048,704]{1,0:T(8,128)(...) custom-call(bf16[16,256,2048]{2,1,0:T(8,128)(2,1)} %bitcast.93, ...), custom_call_target="tpu_custom_call" | custom-call | flops 65000001536 | bytes 80000000 | tf_op jit(solution)/shard_map/pallas_call | solution.py:935
  533.4 65.7 %shard_map.301 = (f32[256,2048]{1,0:T(8,128)}, bf16[2048,3200]{1,0:T(8,128)(2,1)}, bf16[16,4,32,512]{3,2,1,0:T(8,128)(2,1)}, bf16[16,384,128]{2,1,0:T(8,128)(2,1)}) custom-call(bf16[16,4,32,3712]{3,2,1,0:T(8,128)(2,1)} %bitcast.137, bf16[2048,3712]{1,0:T(8,128)(2,1)} %bitcast.138, bf16[256,4224]{1,0:T(8,128)(2,1)} %bitcast.127, ...), custom_call_target="tpu_custom_call" | custom-call | flops 24999999488 | bytes 70000000 | tf_op jit(solution)/shard_map/pallas_call | solution.py:1374
  599.1 2.5 add_convert_fusion
  601.6 123.1 %shard_map.302 = f32[2,64,3712]{2,1,0:T(8,128)} custom-call(bf16[16,2,64,3200]{3,2,1,0:T(8,128)(2,1)} %bitcast.94, bf16[16,2,64,512]{3,2,1,0:T(8,128)(2,1)} %bitcast.110), custom_call_target="tpu_custom_call" | custom-call | tf_op jit(solution)/shard_map/pallas_call | solution.py:535
  724.7 0.9 slice.107
  725.6 0.6 copy.92
  726.2 0.9 slice.111
  727.1 0.7 copy.95
  727.8 1.0 fusion.10
  728.8 0.6 copy.94
  729.4 0.6 copy.89
  730.0 1.0 slice.106
  731.0 0.9 copy.91
  732.1 1.0 copy.93
  733.2 0.8 copy.99
  734.1 0.2 copy.75
  734.4 1.1 copy.84
  735.6 0.5 copy-done.3
  736.2 1.0 fusion.9
  737.2 1.1 copy.86
  738.3 1.1 copy.85
  739.5 11.3 %convolution_bitcast_fusion.2 = f32[1,2048,704]{1,2,0:T(8,128)} fusion(bf16[2048,2048]{1,0:T(8,128)(2,1)} %get-tuple-element.57, bf16[2048,704]{1,0:T(8,128)(2,1)} %get-tuple-element.58), kind=kOutput, calls=%fused_computation.2 | convolution fusion | flops 5905580032 | bytes 17039360 | tf_op jit(solution)/shard_map/dot_general | solution.py:67
  750.8 10.5 %convolution_bitcast_fusion.1 = f32[1,2048,704]{1,2,0:T(8,128)} fusion(bf16[2048,2048]{1,0:T(8,128)(2,1)} %get-tuple-element.57, bf16[2048,704]{1,0:T(8,128)(2,1)S(1)} %copy-done.10), kind=kOutput, calls=%fused_computation.1 | convolution fusion | flops 5905580032 | bytes 17039360 | tf_op jit(solution)/shard_map/dot_general | solution.py:67
  761.3 8.2 %convolution_bitcast_fusion = f32[1,704,2048]{2,1,0:T(8,128)} fusion(bf16[2048,704]{1,0:T(8,128)(2,1)S(1)} %copy-done.9, bf16[2048,2048]{1,0:T(8,128)(2,1)S(1)} %bitcast.152), kind=kOutput, calls=%fused_computation | convolution fusion | flops 5905580032 | bytes 17039360 | tf_op jit(solution)/shard_map/dot_general | solution.py:67
  769.5 1.3 copy.106
  (51 shorter events, 2.2 us)
Async XLA Ops:
  0.6 10.7 %copy-start.6 = (bf16[1408,128]{1,0:T(8,128)(2,1)S(1)}, bf16[1408,128]{1,0:T(8,128)(2,1)}, u32[]{:S(2)}) copy-start(bf16[1408,128]{1,0:T(8,128)(2,1)} %param.32) | copy-start | bytes 1081348
  0.7 10.5 %copy-start.5 = (bf16[128,1408]{1,0:T(8,128)(2,1)S(1)}, bf16[128,1408]{1,0:T(8,128)(2,1)}, u32[]{:S(2)}) copy-start(bf16[128,1408]{1,0:T(8,128)(2,1)} %param.31) | copy-start | bytes 1081348
  11.5 1.2 copy-start.4
  14.8 2.1 copy-start.7
  245.6 1.2 copy-start.8
  533.4 65.7 %copy-start.2 = (f32[256,2048]{1,0:T(8,128)S(1)}, f32[256,2048]{1,0:T(8,128)}, u32[]{:S(2)}) copy-start(f32[256,2048]{1,0:T(8,128)} %get-tuple-element.40.middle) | copy-start | bytes 6291460
  724.7 7.2 copy-start
  734.3 1.7 copy-start.3
  739.5 11.3 %copy-start.10 = (bf16[2048,704]{1,0:T(8,128)(2,1)S(1)}, bf16[2048,704]{1,0:T(8,128)(2,1)}, u32[]{:S(2)}) copy-start(bf16[2048,704]{1,0:T(8,128)(2,1)} %get-tuple-element.59) | copy-start | bytes 8650756
  739.5 21.8 %slice-start = ((s8[8388608]{0:T(1024)(128)(4,1)}), s8[4194304]{0:T(1024)(128)(4,1)S(1)}, s32[]{:S(2)}) async-start(s8[8388608]{0:T(1024)(128)(4,1)} %bitcast.151), calls=%async_computation | async-start | bytes 8388608
  750.8 10.5 %slice-start.1 = ((s8[8388608]{0:T(1024)(128)(4,1)}), s8[4194304]{0:T(1024)(128)(4,1)S(1)}, s32[]{:S(2)}) async-start(s8[8388608]{0:T(1024)(128)(4,1)} %bitcast.151), calls=%async_computation.1 | async-start | bytes 8388608
  750.8 10.5 %copy-start.9 = (bf16[2048,704]{1,0:T(8,128)(2,1)S(1)}, bf16[2048,704]{1,0:T(8,128)(2,1)}, u32[]{:S(2)}) copy-start(bf16[2048,704]{1,0:T(8,128)(2,1)} %get-tuple-element.60) | copy-start | bytes 8650756
  761.3 8.2 %copy-start.1 = (f32[256,2048]{1,0:T(8,128)S(1)}, f32[256,2048]{1,0:T(8,128)}, u32[]{:S(2)}) copy-start(f32[256,2048]{1,0:T(8,128)} %get-tuple-element.110) | copy-start | bytes 6291460

commit v7 on v6

--- a/solution.py
+++ b/solution.py
@@ -895,7 +895,9 @@
     lax.fori_loop(0, 14, step, 0)
 
     def give(n):
-        sg_out[:, n] = sg_sum[:, n].astype(jnp.bfloat16)
+        for part in range(3):
+            kept = sg_sum[part * hid : part * hid + 96, n]
+            sg_out[part * 96 : (part + 1) * 96, n] = kept.astype(jnp.bfloat16)
 
     columns(give)
     for a in range(2):
@@ -936,7 +938,7 @@
         moe_kernel,
         out_shape=[
             shape(2, *blk), shape(slots, width), shape(slots, width), shape(slots, ffe), shape(slots, ffe),
-            shape(slots, ffe), shape(384, width),
+            shape(slots, ffe), shape(288, width),
             shape(4, 3, 64, total), shape(4, 3, 64, total), shape(2, 4, *blk),
         ],
         in_specs=[any_] * 7 + [vmem] * 3,
@@ -1373,7 +1375,7 @@
     pack = weights.shape[1]
     return pl.pallas_call(
         att_bwd_kernel,
-        out_shape=[shape(f32, rows, width), shape(low, width, pack - 512), shape(low, 16, 4, 32, 512), shape(low, 16, 384, 128)],
+        out_shape=[shape(f32, rows, width), shape(low, width, pack - 512), shape(low, 16, 4, 32, 512), shape(low, 16, 288, 128)],
         in_specs=[any_] * 4 + [vmem] * 5 + [any_] * 11,
         out_specs=[vmem, any_, any_, any_],
         scratch_shapes=[
@@ -1560,7 +1562,7 @@
         kv_grads.reshape(dp_count, 2, depth // 2, kv_part),
         6,
     ).reshape(depth, pack_width)
-    shared_home = shared_home.reshape(dp_count, 3, 128, depth)[:, :, :shared_part].astype(jnp.float32)
+    shared_home = shared_home.reshape(dp_count, 3, 96, depth)[:, :, :shared_part].astype(jnp.float32)
     grad_sgate = shared_home[:, 0].transpose(2, 0, 1).reshape(depth, -1)
     grad_sup = shared_home[:, 1].transpose(2, 0, 1).reshape(depth, -1)
     grad_sdown = shared_home[:, 2].reshape(-1, depth)

time: 780 us -> 773 us (level)
  no operation moved by 1% of the time
where the time goes in v7:
time: 773 us; the launch traced here: 765 us
  Pallas kernels  681 us (88%)
  local copies, waits for them, and re-layouts  40.5 us (5%)
  matrix products  30.1 us (4%)
  other arithmetic  12 us (2%)
    pallas_call x2, Pallas kernels, ag16(): pl.pallas_call(functools.partial(ag_kernel, kinds, cuts), out_shape=[jax....  268 us
    pallas_call x1, Pallas kernels, moe_call(): pl.pallas_call(moe_kernel, out_shape=[shape(2, *blk), shape(slots, width)...  197 us
    pallas_call x1, Pallas kernels, rs16(): pl.pallas_call(rs_kernel, out_shape=jax.ShapeDtypeStruct(blkshape, jnp.fl...  118 us
    pallas_call x1, Pallas kernels, att_bwd(): pl.pallas_call(att_bwd_kernel, out_shape=[shape(f32, rows, width), shape(...  65.2 us
    pallas_call x1, Pallas kernels, att_fwd(): pl.pallas_call(att_fwd_kernel, out_shape=[shape(f32, rows, width), shape(...  33 us
    dot_general x3, matrix products, matmul_tn(): lax.dot_general(left_mat, right_mat, (((0,), (0,)), ((), ())), preferred_...  30 us

profile of v7, /device:TPU:0, one launch (start us, length us, event | category | flops | bytes accessed | tf_op | source)
XLA Modules:
  0.0 764.8 jit_solution(268375192624134093)
XLA Ops:
  0.7 0.7 pad.17
  1.4 0.7 constant_dynamic-slice_fusion.1
  2.1 0.7 convert_element_type.58
  2.8 0.8 pad_dynamic-slice_fusion
  3.6 0.2 concatenate.42
  3.8 0.9 concatenate.40
  4.7 0.9 concatenate.41
  5.6 0.8 copy.60
  6.7 0.2 multiply_sine_fusion
  6.9 0.9 copy.104
  7.8 1.1 copy.59
  8.8 1.1 copy.58
  9.9 1.2 copy.66
  11.2 0.2 copy.67
  11.6 1.1 pad.18.clone
  12.7 0.2 copy.55
  13.0 0.2 copy.56
  13.6 1.1 concatenate.37.refs_0_
  14.8 1.0 copy.70.sin.sin_in
  15.9 1.0 copy.69.cos.cos_in
  16.9 0.8 constant_dynamic-slice_fusion.2
  17.7 1.6 fusion.6.bias.bias_in
  19.3 181.1 %shard_map.297 = (bf16[16,1,2,64,3712]{4,3,2,1,0:T(8,128)(2,1)}, bf16[16,2,2,64,2048]{4,3,2,1,0:T(8,128)(2,1)}) custom-call(bf16[2,64,3712]{2,1,0:T(8,128)(2,1)} %concatenate.37.refs_0_, bf16[2,64,2048]{2,1,0:T(8,128)(2,1)} %bitcast.106), custom_call_target="tpu_custom_call" | custom-call | tf_op jit(solution)/shard_map/pallas_call | solution.py:344
  200.5 1.4 slice_reduce_fusion
  201.9 0.7 reshape.263.g_lat
  202.6 1.4 convert_compare_fusion
  204.0 0.5 eq.50
  204.5 0.6 reduce_or.9
  205.3 1.3 slice.100
  206.6 0.9 pad.19.wr
  207.5 2.4 fusion.3.pick_t
  209.9 1.4 fusion.1.pick
  211.3 33.0 %shard_map.298 = (f32[256,2048]{1,0:T(8,128)}, bf16[256,2048]{1,0:T(8,128)(2,1)}, bf16[256,2048]{1,0:T(8,128)(2,1)}, f32[256,640]{1,0:T(8,128)}, bf16[8,256,256]...) custom-call(bf16[256,2048]{1,0:T(8,128)(2,1)} %tok_in.1, ...), custom_call_target="tpu_custom_call" | custom-call | flops 10000000000 | bytes 40000000 | tf_op jit(solution)/shard_map/pallas_call | solution.py:1151
  244.3 1.3 slice.101
  245.8 0.5 reshape.249
  246.2 0.6 copy-done.8
  246.9 0.8 constant_dynamic-slice_fusion
  247.7 0.8 fusion.7.sdn
  248.5 1.1 pad_slice_fusion.1
  249.6 87.0 %shard_map.299 = bf16[16,2,2,64,2048]{4,3,2,1,0:T(8,128)(2,1)} custom-call(bf16[2,64,2048]{2,1,0:T(8,128)(2,1)} %bitcast.107), custom_call_target="tpu_custom_call" | custom-call | tf_op jit(solution)/shard_map/pallas_call | solution.py:344
  336.6 196.6 %shard_map.300 = (bf16[2,2,64,4224]{3,2,1,0:T(8,128)(2,1)}, bf16[2048,2048]{1,0:T(8,128)(2,1)}, bf16[2048,2048]{1,0:T(8,128)(2,1)}, bf16[2048,704]{1,0:T(8,128)(...) custom-call(bf16[16,256,2048]{2,1,0:T(8,128)(2,1)} %bitcast.93, ...), custom_call_target="tpu_custom_call" | custom-call | flops 65000001536 | bytes 80000000 | tf_op jit(solution)/shard_map/pallas_call | solution.py:937
  533.3 65.2 %shard_map.301 = (f32[256,2048]{1,0:T(8,128)}, bf16[2048,3200]{1,0:T(8,128)(2,1)}, bf16[16,4,32,512]{3,2,1,0:T(8,128)(2,1)}, bf16[16,288,128]{2,1,0:T(8,128)(2,1)}) custom-call(bf16[16,4,32,3712]{3,2,1,0:T(8,128)(2,1)} %bitcast.137, bf16[2048,3712]{1,0:T(8,128)(2,1)} %bitcast.138, bf16[256,4224]{1,0:T(8,128)(2,1)} %bitcast.127, ...), custom_call_target="tpu_custom_call" | custom-call | flops 24999999488 | bytes 70000000 | tf_op jit(solution)/shard_map/pallas_call | solution.py:1376
  598.5 2.5 add_convert_fusion
  601.0 117.8 %shard_map.302 = f32[2,64,3712]{2,1,0:T(8,128)} custom-call(bf16[16,2,64,3200]{3,2,1,0:T(8,128)(2,1)} %bitcast.94, bf16[16,2,64,512]{3,2,1,0:T(8,128)(2,1)} %bitcast.110), custom_call_target="tpu_custom_call" | custom-call | tf_op jit(solution)/shard_map/pallas_call | solution.py:535
  718.8 0.9 slice.107
  719.7 0.6 copy.92
  720.3 0.9 slice.111
  721.2 0.7 copy.95
  721.9 1.0 fusion.10
  722.9 0.6 copy.94
  723.5 0.6 copy.89
  724.1 1.0 slice.106
  725.1 0.9 copy.91
  726.1 1.0 copy.93
  727.3 0.8 copy.99
  728.2 0.2 copy.75
  728.5 1.1 copy.84
  729.9 1.0 fusion.9
  730.9 1.1 copy.86
  732.0 1.1 copy.85
  733.1 11.3 %convolution_bitcast_fusion.2 = f32[1,2048,704]{1,2,0:T(8,128)} fusion(bf16[2048,2048]{1,0:T(8,128)(2,1)} %get-tuple-element.57, bf16[2048,704]{1,0:T(8,128)(2,1)} %get-tuple-element.58), kind=kOutput, calls=%fused_computation.2 | convolution fusion | flops 5905580032 | bytes 17039360 | tf_op jit(solution)/shard_map/dot_general | solution.py:67
  744.4 10.5 %convolution_bitcast_fusion.1 = f32[1,2048,704]{1,2,0:T(8,128)} fusion(bf16[2048,2048]{1,0:T(8,128)(2,1)} %get-tuple-element.57, bf16[2048,704]{1,0:T(8,128)(2,1)S(1)} %copy-done.10), kind=kOutput, calls=%fused_computation.1 | convolution fusion | flops 5905580032 | bytes 17039360 | tf_op jit(solution)/shard_map/dot_general | solution.py:67
  755.0 8.2 %convolution_bitcast_fusion = f32[1,704,2048]{2,1,0:T(8,128)} fusion(bf16[2048,704]{1,0:T(8,128)(2,1)S(1)} %copy-done.9, bf16[2048,2048]{1,0:T(8,128)(2,1)S(1)} %bitcast.152), kind=kOutput, calls=%fused_computation | convolution fusion | flops 5905580032 | bytes 17039360 | tf_op jit(solution)/shard_map/dot_general | solution.py:67
  763.1 1.3 copy.106
  (51 shorter events, 2.1 us)
Async XLA Ops:
  0.6 10.7 %copy-start.6 = (bf16[1408,128]{1,0:T(8,128)(2,1)S(1)}, bf16[1408,128]{1,0:T(8,128)(2,1)}, u32[]{:S(2)}) copy-start(bf16[1408,128]{1,0:T(8,128)(2,1)} %param.32) | copy-start | bytes 1081348
  0.7 10.5 %copy-start.5 = (bf16[128,1408]{1,0:T(8,128)(2,1)S(1)}, bf16[128,1408]{1,0:T(8,128)(2,1)}, u32[]{:S(2)}) copy-start(bf16[128,1408]{1,0:T(8,128)(2,1)} %param.31) | copy-start | bytes 1081348
  11.5 1.2 copy-start.4
  14.8 2.1 copy-start.7
  245.6 1.2 copy-start.8
  533.3 65.2 %copy-start.2 = (f32[256,2048]{1,0:T(8,128)S(1)}, f32[256,2048]{1,0:T(8,128)}, u32[]{:S(2)}) copy-start(f32[256,2048]{1,0:T(8,128)} %get-tuple-element.40.middle) | copy-start | bytes 6291460
  718.8 7.2 copy-start
  728.4 1.3 copy-start.3
  733.1 11.3 %copy-start.10 = (bf16[2048,704]{1,0:T(8,128)(2,1)S(1)}, bf16[2048,704]{1,0:T(8,128)(2,1)}, u32[]{:S(2)}) copy-start(bf16[2048,704]{1,0:T(8,128)(2,1)} %get-tuple-element.59) | copy-start | bytes 8650756
  733.1 21.8 %slice-start = ((s8[8388608]{0:T(1024)(128)(4,1)}), s8[4194304]{0:T(1024)(128)(4,1)S(1)}, s32[]{:S(2)}) async-start(s8[8388608]{0:T(1024)(128)(4,1)} %bitcast.151), calls=%async_computation | async-start | bytes 8388608
  744.4 10.5 %slice-start.1 = ((s8[8388608]{0:T(1024)(128)(4,1)}), s8[4194304]{0:T(1024)(128)(4,1)S(1)}, s32[]{:S(2)}) async-start(s8[8388608]{0:T(1024)(128)(4,1)} %bitcast.151), calls=%async_computation.1 | async-start | bytes 8388608
  744.4 10.5 %copy-start.9 = (bf16[2048,704]{1,0:T(8,128)(2,1)S(1)}, bf16[2048,704]{1,0:T(8,128)(2,1)}, u32[]{:S(2)}) copy-start(bf16[2048,704]{1,0:T(8,128)(2,1)} %get-tuple-element.60) | copy-start | bytes 8650756
  755.0 8.2 %copy-start.1 = (f32[256,2048]{1,0:T(8,128)S(1)}, f32[256,2048]{1,0:T(8,128)}, u32[]{:S(2)}) copy-start(f32[256,2048]{1,0:T(8,128)} %get-tuple-element.110) | copy-start | bytes 6291460

commit v8 on v7

--- a/solution.py
+++ b/solution.py
@@ -698,9 +698,9 @@
 
         logits = mm(rr[...], wr[...])
         lane = lax.broadcasted_iota(jnp.int32, logits.shape, 1)
-        logits = jnp.where(lane < 16, logits, -jnp.inf)
+        logits = jnp.where((lane >= ROPE) & (lane < ROPE + 16), logits, -jnp.inf)
         e = jnp.exp(logits - jnp.max(logits, axis=1, keepdims=True))
-        gate = jnp.sum(jnp.where(lane == me, e, 0.0), axis=1, keepdims=True) / jnp.sum(
+        gate = jnp.sum(jnp.where(lane == ROPE + me, e, 0.0), axis=1, keepdims=True) / jnp.sum(
             e, axis=1, keepdims=True
         )
         pre = nt(rg[...], wd[...])
@@ -722,7 +722,7 @@
         columns(spread)
         for c in outs(i):
             c.start()
-        dgs[...] = jnp.where(lane == me, d_gate, 0.0).astype(jnp.bfloat16)
+        dgs[...] = jnp.where(lane == ROPE + me, d_gate, 0.0).astype(jnp.bfloat16)
 
     def third_part(i):
         k, half = i // 2, i % 2
@@ -1212,10 +1212,11 @@
     home_load.wait()
     lane = lax.broadcasted_iota(jnp.int32, (256, 128), 1)
 
-    logits = jnp.where(lane < 16, mm(moe_low[...], wr[...]), -jnp.inf)
+    routed = (lane >= ROPE) & (lane < ROPE + 16)
+    logits = jnp.where(routed, mm(moe_low[...], wr[...]), -jnp.inf)
     e = jnp.exp(logits - jnp.max(logits, axis=1, keepdims=True))
     router = e / jnp.sum(e, axis=1, keepdims=True)
-    d_router = jnp.where(lane < 16, home[:, width:].astype(jnp.float32), 0.0)
+    d_router = jnp.where(routed, home[:, width:].astype(jnp.float32), 0.0)
     d_logits = (router * (d_router - jnp.sum(router * d_router, axis=1, keepdims=True))).astype(jnp.bfloat16)
 
     def norm_back(v, gain, dy):
@@ -1233,8 +1234,7 @@
     dmid[...] = d_middle
     dmid_low[...] = d_middle.astype(jnp.bfloat16)
     gains = gain_rows.astype(jnp.bfloat16)
-    moved = pltpu.roll(d_logits.astype(jnp.float32), 64, 1).astype(jnp.bfloat16)
-    small = tn(moe_low[...], moved) + tn(gains, one_lane(81))
+    small = tn(moe_low[...], d_logits) + tn(gains, one_lane(81))
 
     loads[2].wait()
     for c in late:
@@ -1490,16 +1490,12 @@
         1,
     )
     shared_send = jnp.pad(shared_send, ((0, 0), (0, 0), (0, 96 - shared_part), (0, 0)))
-    at = q_width + o_width + lat_width
-    wr_full = weights[:, at : at + experts]
-    at += experts
+    moe_wr = weights[:, q_width + o_width + RANK : q_width + o_width + RANK + 128]
+    at = ROPE + experts
     gain_latent = (
-        weights[:, at + 2].reshape(dp_count, depth)[:, :kv_rows].reshape(-1).astype(jnp.float32)
-    )
-
-    all_routes = (
-        weights[:, at + 3 : at + 3 + route_width].reshape(total, TOPK).astype(jnp.int32)
-    )
+        moe_wr[:, at + 2].reshape(dp_count, depth)[:, :kv_rows].reshape(-1).astype(jnp.float32)
+    )
+    all_routes = moe_wr[:, at + 3 : at + 3 + route_width].reshape(total, TOPK).astype(jnp.int32)
 
     local_heads = q_width // (NOPE + ROPE)
     positions = (row_start + jnp.arange(n_rows, dtype=jnp.int32)).astype(jnp.float32)
@@ -1534,7 +1530,6 @@
     ).astype(jnp.bfloat16)
 
     slot_rows = dp_count * capacity
-    moe_wr = jnp.pad(wr_full, ((0, 0), (0, 128 - experts)))
     home, rows_in, rows_grad, scaled_act, d_ea_low, d_eb_low, shared_grads = moe_call(
         moe_all.reshape(dp_count, n_rows, width),
         grad_all.reshape(dp_count, n_rows, width),

time: 773 us -> 773 us (level)
  no operation moved by 1% of the time
where the time goes in v8:
time: 773 us; the launch traced here: 765 us
  Pallas kernels  681 us (88%)
  local copies, waits for them, and re-layouts  40.2 us (5%)
  matrix products  30.1 us (4%)
  other arithmetic  12 us (2%)
    pallas_call x2, Pallas kernels, ag16(): pl.pallas_call(functools.partial(ag_kernel, kinds, cuts), out_shape=[jax....  268 us
    pallas_call x1, Pallas kernels, moe_call(): pl.pallas_call(moe_kernel, out_shape=[shape(2, *blk), shape(slots, width)...  197 us
    pallas_call x1, Pallas kernels, rs16(): pl.pallas_call(rs_kernel, out_shape=jax.ShapeDtypeStruct(blkshape, jnp.fl...  118 us
    pallas_call x1, Pallas kernels, att_bwd(): pl.pallas_call(att_bwd_kernel, out_shape=[shape(f32, rows, width), shape(...  65.3 us
    pallas_call x1, Pallas kernels, att_fwd(): pl.pallas_call(att_fwd_kernel, out_shape=[shape(f32, rows, width), shape(...  33 us
    dot_general x3, matrix products, matmul_tn(): lax.dot_general(left_mat, right_mat, (((0,), (0,)), ((), ())), preferred_...  30 us

profile of v8, /device:TPU:0, one launch (start us, length us, event | category | flops | bytes accessed | tf_op | source)
XLA Modules:
  0.0 764.5 jit_solution(8719205215119986976)
XLA Ops:
  0.7 0.7 pad.13
  1.4 0.7 constant_dynamic-slice_fusion.1
  2.1 0.7 convert_element_type.56
  2.8 0.8 pad_dynamic-slice_fusion
  3.6 0.2 concatenate.42
  3.8 0.9 concatenate.40
  4.7 0.9 concatenate.41
  5.6 0.8 copy.60
  6.7 0.2 multiply_sine_fusion
  6.9 0.9 copy.104
  7.8 1.1 copy.59
  8.8 1.1 copy.58
  9.9 1.2 copy.66
  11.2 0.2 copy.67
  11.6 1.1 pad.14.clone
  12.7 0.2 copy.55
  13.0 0.2 copy.56
  13.6 1.1 concatenate.37.refs_0_
  14.8 1.0 copy.70.sin.sin_in
  15.9 1.0 copy.69.cos.cos_in
  16.9 0.8 constant_dynamic-slice_fusion.2
  17.7 1.6 fusion.6.bias.bias_in
  19.3 181.1 %shard_map.297 = (bf16[16,1,2,64,3712]{4,3,2,1,0:T(8,128)(2,1)}, bf16[16,2,2,64,2048]{4,3,2,1,0:T(8,128)(2,1)}) custom-call(bf16[2,64,3712]{2,1,0:T(8,128)(2,1)} %concatenate.37.refs_0_, bf16[2,64,2048]{2,1,0:T(8,128)(2,1)} %bitcast.106), custom_call_target="tpu_custom_call" | custom-call | tf_op jit(solution)/shard_map/pallas_call | solution.py:344
  200.5 1.4 slice_reduce_fusion
  201.9 0.7 reshape.263.g_lat
  202.6 1.4 convert_compare_fusion
  204.0 0.5 eq.50
  204.5 0.6 reduce_or.9
  205.3 1.9 slice.102.wr
  207.2 2.4 fusion.3.pick_t
  209.6 1.4 fusion.1.pick
  211.0 33.0 %shard_map.298 = (f32[256,2048]{1,0:T(8,128)}, bf16[256,2048]{1,0:T(8,128)(2,1)}, bf16[256,2048]{1,0:T(8,128)(2,1)}, f32[256,640]{1,0:T(8,128)}, bf16[8,256,256]...) custom-call(bf16[256,2048]{1,0:T(8,128)(2,1)} %tok_in.1, ...), custom_call_target="tpu_custom_call" | custom-call | flops 10000000000 | bytes 40000000 | tf_op jit(solution)/shard_map/pallas_call | solution.py:1151
  244.0 1.3 slice.103
  245.5 0.5 reshape.249
  246.0 0.6 copy-done.8
  246.6 0.8 constant_dynamic-slice_fusion
  247.4 0.8 fusion.7.sdn
  248.2 1.1 pad_slice_fusion.1
  249.3 86.9 %shard_map.299 = bf16[16,2,2,64,2048]{4,3,2,1,0:T(8,128)(2,1)} custom-call(bf16[2,64,2048]{2,1,0:T(8,128)(2,1)} %bitcast.107), custom_call_target="tpu_custom_call" | custom-call | tf_op jit(solution)/shard_map/pallas_call | solution.py:344
  336.2 196.8 %shard_map.300 = (bf16[2,2,64,4224]{3,2,1,0:T(8,128)(2,1)}, bf16[2048,2048]{1,0:T(8,128)(2,1)}, bf16[2048,2048]{1,0:T(8,128)(2,1)}, bf16[2048,704]{1,0:T(8,128)(...) custom-call(bf16[16,256,2048]{2,1,0:T(8,128)(2,1)} %bitcast.93, ...), custom_call_target="tpu_custom_call" | custom-call | flops 65000001536 | bytes 80000000 | tf_op jit(solution)/shard_map/pallas_call | solution.py:937
  533.0 65.3 %shard_map.301 = (f32[256,2048]{1,0:T(8,128)}, bf16[2048,3200]{1,0:T(8,128)(2,1)}, bf16[16,4,32,512]{3,2,1,0:T(8,128)(2,1)}, bf16[16,288,128]{2,1,0:T(8,128)(2,1)}) custom-call(bf16[16,4,32,3712]{3,2,1,0:T(8,128)(2,1)} %bitcast.137, bf16[2048,3712]{1,0:T(8,128)(2,1)} %bitcast.138, bf16[256,4224]{1,0:T(8,128)(2,1)} %bitcast.127, ...), custom_call_target="tpu_custom_call" | custom-call | flops 24999999488 | bytes 70000000 | tf_op jit(solution)/shard_map/pallas_call | solution.py:1376
  598.4 2.5 add_convert_fusion
  600.9 117.8 %shard_map.302 = f32[2,64,3712]{2,1,0:T(8,128)} custom-call(bf16[16,2,64,3200]{3,2,1,0:T(8,128)(2,1)} %bitcast.94, bf16[16,2,64,512]{3,2,1,0:T(8,128)(2,1)} %bitcast.110), custom_call_target="tpu_custom_call" | custom-call | tf_op jit(solution)/shard_map/pallas_call | solution.py:535
  718.7 0.9 slice.109
  719.6 0.6 copy.92
  720.2 0.9 slice.113
  721.1 0.7 copy.95
  721.8 1.0 fusion.10
  722.8 0.6 copy.94
  723.4 0.6 copy.89
  724.0 1.0 slice.108
  725.0 0.9 copy.91
  726.0 1.0 copy.93
  727.0 0.2 copy.79
  727.2 0.8 copy.99
  728.1 0.2 copy.75
  728.4 1.1 copy.84
  729.7 1.0 fusion.9
  730.7 1.1 copy.86
  731.9 1.1 copy.85
  733.0 11.3 %convolution_bitcast_fusion.2 = f32[1,2048,704]{1,2,0:T(8,128)} fusion(bf16[2048,2048]{1,0:T(8,128)(2,1)} %get-tuple-element.57, bf16[2048,704]{1,0:T(8,128)(2,1)} %get-tuple-element.58), kind=kOutput, calls=%fused_computation.2 | convolution fusion | flops 5905580032 | bytes 17039360 | tf_op jit(solution)/shard_map/dot_general | solution.py:67
  744.3 10.5 %convolution_bitcast_fusion.1 = f32[1,2048,704]{1,2,0:T(8,128)} fusion(bf16[2048,2048]{1,0:T(8,128)(2,1)} %get-tuple-element.57, bf16[2048,704]{1,0:T(8,128)(2,1)S(1)} %copy-done.10), kind=kOutput, calls=%fused_computation.1 | convolution fusion | flops 5905580032 | bytes 17039360 | tf_op jit(solution)/shard_map/dot_general | solution.py:67
  754.8 8.2 %convolution_bitcast_fusion = f32[1,704,2048]{2,1,0:T(8,128)} fusion(bf16[2048,704]{1,0:T(8,128)(2,1)S(1)} %copy-done.9, bf16[2048,2048]{1,0:T(8,128)(2,1)S(1)} %bitcast.152), kind=kOutput, calls=%fused_computation | convolution fusion | flops 5905580032 | bytes 17039360 | tf_op jit(solution)/shard_map/dot_general | solution.py:67
  763.0 1.3 copy.106
  (50 shorter events, 1.9 us)
Async XLA Ops:
  0.6 10.7 %copy-start.6 = (bf16[1408,128]{1,0:T(8,128)(2,1)S(1)}, bf16[1408,128]{1,0:T(8,128)(2,1)}, u32[]{:S(2)}) copy-start(bf16[1408,128]{1,0:T(8,128)(2,1)} %param.32) | copy-start | bytes 1081348
  0.7 10.5 %copy-start.5 = (bf16[128,1408]{1,0:T(8,128)(2,1)S(1)}, bf16[128,1408]{1,0:T(8,128)(2,1)}, u32[]{:S(2)}) copy-start(bf16[128,1408]{1,0:T(8,128)(2,1)} %param.31) | copy-start | bytes 1081348
  11.5 1.2 copy-start.4
  14.8 2.1 copy-start.7
  245.3 1.2 copy-start.8
  533.0 65.3 %copy-start.2 = (f32[256,2048]{1,0:T(8,128)S(1)}, f32[256,2048]{1,0:T(8,128)}, u32[]{:S(2)}) copy-start(f32[256,2048]{1,0:T(8,128)} %get-tuple-element.40.middle) | copy-start | bytes 6291460
  718.7 7.2 copy-start
  728.3 1.3 copy-start.3
  733.0 11.3 %copy-start.10 = (bf16[2048,704]{1,0:T(8,128)(2,1)S(1)}, bf16[2048,704]{1,0:T(8,128)(2,1)}, u32[]{:S(2)}) copy-start(bf16[2048,704]{1,0:T(8,128)(2,1)} %get-tuple-element.59) | copy-start | bytes 8650756
  733.0 21.8 %slice-start = ((s8[8388608]{0:T(1024)(128)(4,1)}), s8[4194304]{0:T(1024)(128)(4,1)S(1)}, s32[]{:S(2)}) async-start(s8[8388608]{0:T(1024)(128)(4,1)} %bitcast.151), calls=%async_computation | async-start | bytes 8388608
  744.3 10.5 %slice-start.1 = ((s8[8388608]{0:T(1024)(128)(4,1)}), s8[4194304]{0:T(1024)(128)(4,1)S(1)}, s32[]{:S(2)}) async-start(s8[8388608]{0:T(1024)(128)(4,1)} %bitcast.151), calls=%async_computation.1 | async-start | bytes 8388608
  744.3 10.5 %copy-start.9 = (bf16[2048,704]{1,0:T(8,128)(2,1)S(1)}, bf16[2048,704]{1,0:T(8,128)(2,1)}, u32[]{:S(2)}) copy-start(bf16[2048,704]{1,0:T(8,128)(2,1)} %get-tuple-element.60) | copy-start | bytes 8650756
  754.8 8.2 %copy-start.1 = (f32[256,2048]{1,0:T(8,128)S(1)}, f32[256,2048]{1,0:T(8,128)}, u32[]{:S(2)}) copy-start(f32[256,2048]{1,0:T(8,128)} %get-tuple-element.110) | copy-start | bytes 6291460
